TPU v7x, 128 devices: a whole 4x4x4 slice. The times are simulated.
128 devices in a mesh: slab: 2 (over z_lo), trow: 4 (over y), tcol: 16 (over x, z_hi, core).
Axes of the slice: x: 4, y: 4, z: 4 (z_hi: 2, z_lo: 2; z = z_hi * 2 + z_lo), core: 2. Of those that a mesh axis runs over, the one named last changes fastest.
Arguments:
- design: bfloat16 [4096, 16384], P('slab', ('tcol', 'trow')), may hold values from -6 to 6
- targets: float32 [4096], P('slab'), may hold values from -8 to 8
- coeffs: bfloat16 [16384], P(('tcol', 'trow')), may hold values from -0.046875 to 0.046875
- threshold: float32 [1], replicated, may hold values from 0.5 to 2
- damping: float32 [1], replicated, may hold values from 0.1 to 1
Outputs:
- hessian: float32 [16, 4, 256, 16384], P('slab', 'trow', None, 'tcol')
- gradient: float32 [16384], P(('tcol', 'trow'))
All inputs are finite; a program needn't handle non-finite values.
Results may differ from a plain program's by a relative error of at most 0.0012.
Values may be sent and summed in bfloat16 or wider, within the bound.
No kernel may reach another device: no remote copies, remote signals or barrier semaphores. Data moves between devices by JAX's collectives and lax.ppermute only.
A program may use at most 192 MiB of HBM per device.

v0:
```python
import jax
import jax.numpy as jnp
from jax import lax
from jax.sharding import PartitionSpec as P


def local(design, targets, coeffs, threshold, damping):
    rows_here = design.shape[0]
    shard_width = design.shape[1]
    slab_size = lax.axis_size("slab")
    samples = rows_here * slab_size
    partial_value = jnp.dot(design, coeffs, preferred_element_type=jnp.float32)
    predicted = lax.psum(partial_value, ("trow", "tcol"))
    residual = targets - predicted
    cutoff = threshold[0]
    weight = cutoff / jnp.maximum(jnp.abs(residual), cutoff)
    influence = weight * residual
    local_grad = jnp.dot(influence, design.astype(jnp.float32), precision=lax.Precision.HIGHEST)
    gradient = -lax.psum(local_grad, "slab") / samples
    columns = lax.all_gather(design, "trow", axis=1, tiled=True)
    col_width = columns.shape[1]
    weighted = (columns.astype(jnp.float32) * weight[:, None]).astype(jnp.bfloat16)
    tcol_size = lax.axis_size("tcol")
    blocks_mine = tcol_size // slab_size
    own_rows = blocks_mine * shard_width
    products = jnp.einsum(
        "sa,sb->ab",
        lax.all_gather(design, "tcol", axis=1, tiled=True),
        weighted,
        preferred_element_type=jnp.float32,
    )
    summed = lax.psum(products, "slab")
    own_part = lax.dynamic_slice_in_dim(summed, lax.axis_index("slab") * own_rows, own_rows, 0)
    own_part = (own_part / samples).reshape(blocks_mine, 1, shard_width, col_width)
    block_ids = lax.axis_index("slab") * blocks_mine + jnp.arange(blocks_mine, dtype=jnp.int32)
    diag_block = block_ids == lax.axis_index("tcol")
    feature_cols = lax.axis_index("trow") * shard_width + jnp.arange(shard_width, dtype=jnp.int32)
    on_diag = diag_block[:, None, None, None] & (
        jnp.arange(col_width, dtype=jnp.int32)[None, None, None, :]
        == feature_cols[None, None, :, None]
    )
    hessian = own_part + jnp.where(on_diag, damping[0], jnp.float32(0.0))
    return (hessian, gradient)


def solution(mesh):
    in_specs = (P("slab", ("tcol", "trow")), P("slab"), P(("tcol", "trow")), P(), P())
    out_specs = (P("slab", "trow", None, "tcol"), P(("tcol", "trow")))
    return jax.shard_map(local, mesh=mesh, in_specs=in_specs, out_specs=out_specs, check_vma=False)
```

profile of v0, /device:TPU:0, one launch (start us, length us, event | category | flops | bytes accessed | tf_op | source)
XLA Modules:
  0.0 632.7 jit_solution(7034792957879562105)
XLA Ops:
  7.2 0.0 all-gather.3.cloned.1.call-start
  7.2 0.7 all-gather.3.cloned.1.call-update
  7.9 0.0 all-gather.5.cloned.1.call-start
  7.9 0.7 all-gather.5.cloned.1.call-update
  8.6 0.0 all-reduce.2.cloned.1.call-start
  8.7 0.7 reshape.65
  10.0 1.6 fusion.1
  11.6 174.9 %psum.21 = f32[2048]{0:T(1024)S(1)} all-reduce(f32[2048]{0:T(1024)S(1)} %bitcast.16), channel_id=1, replica_groups=mesh['slab'=2,'trow'=4,'tcol'=16] {'trow','tcol'}, use_global_device_ids=true, to_apply=%region_0.0 | all-reduce | flops 2048 | bytes 16384 | tf_op jit(solution)/shard_map/psum | solution.py:13
  186.5 0.7 subtract_multiply_fusion
  187.2 0.0 all-gather.3.cloned.1.call-done
  187.2 4.9 all-gather.5.cloned.1.call-done
  192.1 24.3 %convolution_bitcast_fusion = f32[4096,1024]{0,1:T(8,128)} fusion(bf16[2048,4096]{1,0:T(8,128)(2,1)} %all-gather.5.cloned.1.call-done, bf16[2048,1024]{1,0:T(8,128)(2,1)} %all-gather.3.cloned.1.call-done, f32[2048]{0:T(1024)S(1)} %get-tuple-element.3), kind=kOutput, calls=%fused_computation | convolution fusion | flops 17186160640 | bytes 37756928 | tf_op jit(solution)/shard_map/sa,sb->ab/dot_general | solution.py:26
  216.4 0.0 copy-start
  216.4 0.0 all-reduce.2.cloned.1.call-update
  217.2 0.5 copy-done
  217.7 0.5 fusion.2
  218.2 4.9 psum.23
  223.1 0.6 negate_multiply_fusion
  223.7 0.2 iota_compare_fusion
  223.9 375.6 %all-reduce.2.cloned.1.call-done = f32[4096,1024]{0,1:T(8,128)} async-done(((f32[4096,1024]{0,1:T(8,128)}), f32[4096,1024]{0,1:T(8,128)}) %all-reduce.2.cloned.1.call-update) | async-done | bytes 16777232 | tf_op jit(solution)/shard_map/psum | solution.py:32
  599.5 8.4 %dynamic-slice_multiply_fusion = f32[2048,1024]{0,1:T(8,128)} fusion(f32[4096,1024]{0,1:T(8,128)} %all-reduce.2.cloned.1.call-done, s32[]{:T(128)S(6)} %select_n.15), kind=kLoop, calls=%fused_computation.2 | loop fusion | flops 2097152 | bytes 16777220 | tf_op jit(solution)/shard_map/div | solution.py:34
  607.9 9.3 %copy.8 = f32[2048,1024]{1,0:T(8,128)} copy(f32[2048,1024]{0,1:T(8,128)} %dynamic-slice_multiply_fusion) | data formatting | bytes 16777216 | tf_op jit(solution)/shard_map/reshape | solution.py:34
  617.2 9.0 %select_add_fusion = f32[8,1,256,1024]{3,2,1,0:T(8,128)} fusion(f32[8,1,256,1024]{3,2,1,0:T(8,128)} %bitcast.15, f32[]{:T(128)} %bitcast.14, pred[256,1024]{1,0:T(8,128)(4,1)S(1)} %iota_compare_fusion, pred[8]{0:T(512)(128)(4,1)S(1)} %add_compare_fusion), kind=kLoop, calls=%fused_computation.1 | loop fusion | flops 6291456 | bytes 17039372 | tf_op jit(solution)/shard_map/add | solution.py:42
  (2 shorter events, 0.0 us)
Async XLA Ops:
  7.2 180.0 %all-gather.3.cloned.1.call-start = ((), (), s32[]{:S(2)}) async-start(), calls=%async_computation | async-start | bytes 5242880 | tf_op jit(solution)/shard_map/all_gather | solution.py:20
  7.9 184.2 %all-gather.5.cloned.1.call-start = ((), (), s32[]{:S(2)}) async-start(), calls=%async_computation.1 | async-start | bytes 17825792 | tf_op jit(solution)/shard_map/all_gather | solution.py:28
  8.6 590.9 %all-reduce.2.cloned.1.call-start = ((), (), s32[]{:S(2)}) async-start(), calls=%async_computation.2 | async-start | bytes 33554432 | tf_op jit(solution)/shard_map/psum | solution.py:32
  216.4 1.2 copy-start
Sparse Core Ops, SparseCore 0:
  9.7 54.4 all-gather.2
  66.4 125.6 all-gather.4
  216.6 382.8 all-reduce.1
where the time goes:
time: 634 us; the launch traced here: 633 us
  waiting for transfers between devices  382 us (60%)
  blocking collectives  180 us (28%)
  matrix products  26.4 us (4%)
  other arithmetic  18.9 us (3%)
  between operations  15.2 us (2%)
  local copies, waits for them, and re-layouts  10.4 us (2%)
    psum x1, waiting for transfers between devices, local(): summed = lax.psum(products, 'slab')  376 us
    psum x1, blocking collectives, local(): predicted = lax.psum(partial_value, ('trow', 'tcol'))  175 us
    dot_general x1, matrix products, local(): jnp.einsum('sa,sb->ab', lax.all_gather(design, 'tcol', axis=1, tiled=True...  24.3 us
  transfers between devices with their start and end apart: 3, of which 2 were waited for; matrix products, arithmetic and copies ran while one was open for 1% of the time, Pallas kernels for 0%

commit v1 on v0

v1 whole, which is shorter than its diff:
```python
import functools

import jax
import jax.numpy as jnp
from jax import lax
from jax.experimental import pallas as pl
from jax.experimental.pallas import tpu as pltpu
from jax.sharding import PartitionSpec as P

AXES = ("slab", "trow", "tcol")
N_X, N_Y, N_Z, N_CORE = 4, 4, 4, 2


def index_of(x, y, z, core):
    return ((z % 2) * N_Y + y) * 16 + x * 4 + (z // 2) * 2 + core


def is_native(x, z):
    return (x // 2) == (z % 2)


def pairs(x=0, y=0, z=0, core=0, senders=None):
    found = []
    for cx in range(N_X):
        for cy in range(N_Y):
            for cz in range(N_Z):
                if senders is not None and not senders(cx, cz):
                    continue
                for ck in range(N_CORE):
                    found.append((index_of(cx, cy, cz, ck), index_of(cx ^ x, cy ^ y, cz ^ z, ck ^ core)))
    return found


def move(value, **where):
    return lax.ppermute(value, AXES, pairs(**where))


def weigh_kernel(blocks_ref, weight_ref, *refs):
    *shard_refs, out_ref = refs
    width = shard_refs[0].shape[1]
    lanes = weight_ref.shape[1]
    weight = weight_ref[...]
    for m, shard_ref in enumerate(shard_refs):
        base = blocks_ref[m] * width
        for part in range(width // lanes):
            scaled = shard_ref[:, part * lanes:(part + 1) * lanes].astype(jnp.float32) * weight
            at = pl.multiple_of(base + part * lanes, lanes)
            out_ref[:, pl.ds(at, lanes)] = scaled.astype(jnp.bfloat16)


def weigh(blocks, weight, shards):
    rows, width = shards[0].shape
    spread = jnp.broadcast_to(weight[:, None], (rows, 128))
    vmem = pl.BlockSpec(memory_space=pltpu.VMEM)
    return pl.pallas_call(
        weigh_kernel,
        out_shape=jax.ShapeDtypeStruct((rows, width * len(shards)), jnp.bfloat16),
        in_specs=[pl.BlockSpec(memory_space=pltpu.SMEM)] + [vmem] * (1 + len(shards)),
        out_specs=vmem,
        compiler_params=pltpu.CompilerParams(vmem_limit_bytes=40 * 2**20),
        cost_estimate=pl.CostEstimate(flops=rows * width * 4, bytes_accessed=rows * width * 18, transcendentals=0),
        name="weigh",
    )(blocks, spread, *shards)


def gram_kernel(meta_ref, damping_ref, lhs_ref, own_ref, other_ref, *refs, samples):
    out_ref = refs[-1]
    step = pl.program_id(0)
    steps = pl.num_programs(0)
    contract = (((0,), (0,)), ((), ()))
    total = lax.dot_general(lhs_ref[0, 0], own_ref[...], contract, preferred_element_type=jnp.float32)
    total += lax.dot_general(lhs_ref[0, 1], other_ref[...], contract, preferred_element_type=jnp.float32)
    out_ref[0] = total * (1.0 / samples)

    @pl.when(meta_ref[steps + step] == 1)
    def _():
        height = out_ref.shape[1]
        at = pl.multiple_of(meta_ref[2 * steps] * height, height)
        eye = (lax.broadcasted_iota(jnp.int32, (height, height), 0)
               == lax.broadcasted_iota(jnp.int32, (height, height), 1))
        out_ref[0, :, pl.ds(at, height)] += jnp.where(eye, damping_ref[0], 0.0)


def gram_blocks(lhs, own, other, damping, tiles, diagonal, row, samples, into=None):
    count, _, rows, height = lhs.shape
    width = own.shape[1]
    meta = jnp.concatenate([tiles, diagonal, row[None]]).astype(jnp.int32)
    whole = pl.BlockSpec((rows, width), lambda i, meta: (0, 0), pipeline_mode=pl.Buffered(1))
    in_specs = [
        pl.BlockSpec(memory_space=pltpu.SMEM),
        pl.BlockSpec((1, 2, rows, height), lambda i, meta: (i, 0, 0, 0)),
        whole,
        whole,
    ]
    operands = [meta, damping, lhs, own, other]
    aliases = {}
    if into is not None:
        in_specs.append(pl.BlockSpec(memory_space=pl.ANY))
        operands.append(into)
        aliases = {5: 0}
    flops = 2 * count * 2 * rows * height * width
    moved = count * (2 * rows * height * 2 + height * width * 4) + 4 * rows * width
    return pl.pallas_call(
        functools.partial(gram_kernel, samples=samples),
        out_shape=jax.ShapeDtypeStruct((8, height, width), jnp.float32),
        grid_spec=pltpu.PrefetchScalarGridSpec(
            num_scalar_prefetch=1,
            grid=(count,),
            in_specs=in_specs,
            out_specs=pl.BlockSpec((1, height, width), lambda i, meta: (meta[i], 0, 0)),
        ),
        input_output_aliases=aliases,
        compiler_params=pltpu.CompilerParams(vmem_limit_bytes=48 * 2**20),
        cost_estimate=pl.CostEstimate(flops=flops, bytes_accessed=moved, transcendentals=0),
        name="gram",
    )(*operands)


def local(design, targets, coeffs, threshold, damping):
    rows, width = design.shape
    samples = rows * lax.axis_size("slab")
    slab, row, col = lax.axis_index("slab"), lax.axis_index("trow"), lax.axis_index("tcol")
    x, zh, core = col // 4, (col // 2) % 2, col % 2
    native = (x // 2) == slab

    def pick(if_native, if_far):
        return jnp.where(native, if_native, if_far)

    columns = lax.all_gather(design, "trow", axis=1, tiled=True)

    from_zp = move(design, z=1)
    from_zo = move(design, z=3)
    from_xp = move(design, x=1, senders=is_native)
    from_xo = move(design, x=3)

    partial_value = jnp.dot(design, coeffs, preferred_element_type=jnp.float32).reshape(rows // 128, 128)
    for where in ({"core": 1}, {"x": 1}, {"y": 1}, {"x": 2}, {"y": 2}, {"z": 2}):
        partial_value = partial_value + move(partial_value, **where)
    residual = targets - partial_value.reshape(rows)
    residual_other = move(residual.reshape(rows // 128, 128), z=1).reshape(rows)
    cutoff = threshold[0]
    weight = cutoff / jnp.maximum(jnp.abs(residual), cutoff)
    weight_other = cutoff / jnp.maximum(jnp.abs(residual_other), cutoff)
    influence = weight * residual
    local_grad = jnp.dot(influence, design.astype(jnp.float32), precision=lax.Precision.HIGHEST)
    gradient = -(local_grad + move(local_grad, z=1)) / samples

    other_y1 = move(from_zp, y=1)
    other_y3 = move(from_zp, y=3)
    other_y2 = move(from_zp, y=2)

    second_xp = move(pick(from_zp, from_xo), x=1)
    second_zo = move(pick(from_xo, from_zp), z=3)
    second_zp = move(from_xo, z=1, senders=is_native)
    third_xp = move(pick(second_zo, second_zp), x=1)
    third_xo = move(second_zo, x=3, senders=is_native)
    fourth_xp = move(pick(from_zo, second_zo), x=1)
    fourth_xo = move(third_xp, x=3, senders=is_native)

    first_part = jnp.stack([
        jnp.stack([pick(design, from_xo), pick(from_zp, second_zp)]),
        jnp.stack([pick(second_zo, third_xo), pick(from_zo, second_zo)]),
        jnp.stack([pick(from_xp, second_xp), pick(second_xp, third_xp)]),
    ])
    last_part = jnp.stack([pick(third_xp, fourth_xo), fourth_xp])[None]
    first_sibling = move(first_part, core=1)
    last_sibling = move(last_part, core=1)

    order = jnp.arange(4, dtype=jnp.int32)
    own_weighted = (columns.astype(jnp.float32) * weight[:, None]).astype(jnp.bfloat16)
    other_weighted = weigh(row ^ order, weight_other, [from_zp, other_y1, other_y2, other_y3])

    column_a = pick(x, x ^ 3)
    column_b = column_a ^ 1

    def tile(column, half, core_at):
        return (column * 4 + half * 2 + core_at) - 8 * slab

    def fill(lhs, columns_halves, core_at, into):
        tiles = jnp.stack([tile(c, h, core_at) for c, h in columns_halves])
        diagonal = (tiles + 8 * slab == col).astype(jnp.int32)
        return gram_blocks(lhs, own_weighted, other_weighted, damping, tiles, diagonal, row, samples, into)

    first_at = [(column_a, zh), (column_a, 1 - zh), (column_b, zh)]
    last_at = [(column_b, 1 - zh)]
    result = fill(first_part, first_at, core, None)
    result = fill(first_sibling, first_at, 1 - core, result)
    result = fill(last_part, last_at, core, result)
    result = fill(last_sibling, last_at, 1 - core, result)
    hessian = result.reshape(8, 1, width, own_weighted.shape[1])
    return (hessian, gradient)


def solution(mesh):
    in_specs = (P("slab", ("tcol", "trow")), P("slab"), P(("tcol", "trow")), P(), P())
    out_specs = (P("slab", "trow", None, "tcol"), P(("tcol", "trow")))
    return jax.shard_map(local, mesh=mesh, in_specs=in_specs, out_specs=out_specs, check_vma=False)
```

time: 634 us -> 322 us (0.51)
  waiting for transfers between devices: 382 us -> 200 us
  blocking collectives: 180 us -> 0 us
  starting transfers between devices: 0.11 us -> 42.7 us
  Pallas kernels: 0 us -> 41.4 us
  matrix products: 26.4 us -> 0.89 us
  local copies, waits for them, and re-layouts: 10.4 us -> 2.76 us
    psum x1 -> x0, waiting for transfers between devices: 376 us -> none  [local(): summed = lax.psum(products, 'slab')]
    ppermute x0 -> x24, waiting for transfers between devices: none -> 200 us  [move(): return lax.ppermute(value, AXES, pairs(**where))]
    psum x2 -> x0, blocking collectives: 180 us -> none  [the longest x1 175 us: local(): predicted = lax.psum(partial_value, ('trow', 'tcol'))]
    ppermute x0 -> x24, starting transfers between devices: none -> 42.7 us  [move(): return lax.ppermute(value, AXES, pairs(**where))]
    pallas_call x0 -> x5, Pallas kernels: none -> 41.4 us  [the longest x4 39.3 us: gram_blocks(): pl.pallas_call(functools.partial(gram_kernel, samples=samples), out_shape...]
    dot_general x2 -> x1, matrix products: 25.9 us -> 0.37 us  [local(): jnp.dot(design, coeffs, preferred_element_type=jnp.float32)]
    another operation x0 -> x6, other arithmetic: none -> 9.74 us  [the longest x4 5.09 us: local(): jnp.stack([jnp.stack([pick(design, from_xo), pick(from_zp, second_zp)]),...]
    reshape x1 -> x0, local copies, waits for them, and re-layouts: 9.28 us -> none  [local(): (own_part / samples).reshape(blocks_mine, 1, shard_width, col_width)]
  transfers between devices with their start and end apart: 3 -> 25, of which waited for: 2 -> 19; matrix products, arithmetic and copies ran while one was open for 1% -> 5% of each run, Pallas kernels for 0% -> 10%
where the time goes in v1:
time: 322 us
  waiting for transfers between devices  200 us (62%)
  starting transfers between devices  42.7 us (13%)
  Pallas kernels  41.4 us (13%)
  other arithmetic  18.5 us (6%)
  between operations  15.6 us (5%)
    ppermute x24, waiting for transfers between devices, move(): return lax.ppermute(value, AXES, pairs(**where))  200 us
    ppermute x24, starting transfers between devices, move(): return lax.ppermute(value, AXES, pairs(**where))  42.7 us
    pallas_call x4, Pallas kernels, gram_blocks(): pl.pallas_call(functools.partial(gram_kernel, samples=samples), out_shape...  39.3 us
  transfers between devices with their start and end apart: 25, of which 19 were waited for; matrix products, arithmetic and copies ran while one was open for 5% of the time, Pallas kernels for 10%

profile of v1, /device:TPU:0, one launch (start us, length us, event | category | flops | bytes accessed | tf_op | source)
XLA Modules:
  0.0 321.7 jit_solution(12918681053878746413)
XLA Ops:
  7.2 2.9 collective-permute-start
  12.0 21.6 %collective-permute-done = bf16[2048,256]{1,0:T(8,128)(2,1)} collective-permute-done((bf16[2048,256]{1,0:T(8,128)(2,1)}, bf16[2048,256]{1,0:T(8,128)(2,1)}, u32[]{:S(2)}, u32[]{:S(2)}) %collective-permute-start) | collective-permute-done | bytes 1048608 | tf_op jit(solution)/shard_map/ppermute | solution.py:35
  33.6 5.0 %collective-permute-start.3 = (bf16[2048,256]{1,0:T(8,128)(2,1)}, bf16[2048,256]{1,0:T(8,128)(2,1)}, u32[]{:S(2)}, u32[]{:S(2)}) collective-permute-start(bf16[2048,256]{1,0:T(8,128)(2,1)} %collective-permute-done), channel_id=1, source_target_pairs={{0,64},{1,65},{2,66},{3,67},{16,80},{17,81},{18,82},{19,83},{32,96... | collective-permute-start | bytes 3145736 | tf_op jit(solution)/shard_map/ppermute | solution.py:35
  38.6 20.9 %collective-permute-done.3 = bf16[2048,256]{1,0:T(8,128)(2,1)} collective-permute-done((bf16[2048,256]{1,0:T(8,128)(2,1)}, bf16[2048,256]{1,0:T(8,128)(2,1)}, u32[]{:S(2)}, u32[]{:S(2)}) %collective-permute-start.3) | collective-permute-done | bytes 1048608 | tf_op jit(solution)/shard_map/ppermute | solution.py:35
  59.5 3.1 broadcast_select_fusion
  62.6 4.6 %collective-permute-start.2 = (bf16[2048,256]{1,0:T(8,128)(2,1)S(1)}, bf16[2048,256]{1,0:T(8,128)(2,1)S(1)}, u32[]{:S(2)}, u32[]{:S(2)}) collective-permute-start(bf16[2048,256]{1,0:T(8,128)(2,1)S(1)} %get-tuple-element.7), channel_id=1, source_target_pairs={{0,66},{1,67},{64,2},{65,3},{2,64},{3,65},{66,0},{67,1},{16,82},{1... | collective-permute-start | bytes 3145736 | tf_op jit(solution)/shard_map/ppermute | solution.py:35
  67.2 24.0 %collective-permute-done.2 = bf16[2048,256]{1,0:T(8,128)(2,1)S(1)} collective-permute-done((bf16[2048,256]{1,0:T(8,128)(2,1)S(1)}, bf16[2048,256]{1,0:T(8,128)(2,1)S(1)}, u32[]{:S(2)}, u32[]{:S(2)}) %collective-permute-start.2) | collective-permute-done | bytes 1048608 | tf_op jit(solution)/shard_map/ppermute | solution.py:35
  91.3 3.9 %collective-permute-start.19 = (bf16[2048,256]{1,0:T(8,128)(2,1)S(1)}, bf16[2048,256]{1,0:T(8,128)(2,1)S(1)}, u32[]{:S(2)}, u32[]{:S(2)}) collective-permute-start(bf16[2048,256]{1,0:T(8,128)(2,1)S(1)} %collective-permute-done.2), channel_id=1, source_target_pairs={{0,12},{1,13},{2,14},{3,15},{16,28},{17,29},{18,30},{19,31},{32,44... | collective-permute-start | bytes 3145736 | tf_op jit(solution)/shard_map/ppermute | solution.py:35
  95.2 15.8 %collective-permute-done.6 = bf16[2048,256]{1,0:T(8,128)(2,1)S(1)} collective-permute-done((bf16[2048,256]{1,0:T(8,128)(2,1)S(1)}, bf16[2048,256]{1,0:T(8,128)(2,1)S(1)}, u32[]{:S(2)}, u32[]{:S(2)}) %collective-permute-start.6) | collective-permute-done | bytes 1048608 | tf_op jit(solution)/shard_map/ppermute | solution.py:35
  113.4 3.9 %collective-permute-start.20 = (bf16[2048,256]{1,0:T(8,128)(2,1)S(1)}, bf16[2048,256]{1,0:T(8,128)(2,1)}, u32[]{:S(2)}, u32[]{:S(2)}) collective-permute-start(bf16[2048,256]{1,0:T(8,128)(2,1)S(1)} %copy-done.2), channel_id=1, source_target_pairs={{0,4},{1,5},{2,6},{3,7},{16,20},{17,21},{18,22},{19,23},{32,36},{3... | collective-permute-start | bytes 3145736 | tf_op jit(solution)/shard_map/ppermute | solution.py:35
  117.4 22.2 %collective-permute-done.4 = bf16[2048,256]{1,0:T(8,128)(2,1)} collective-permute-done((bf16[2048,256]{1,0:T(8,128)(2,1)S(1)}, bf16[2048,256]{1,0:T(8,128)(2,1)}, u32[]{:S(2)}, u32[]{:S(2)}) %collective-permute-start.4) | collective-permute-done | bytes 1048608 | tf_op jit(solution)/shard_map/ppermute | solution.py:35
  139.6 7.8 %collective-permute-start.5 = (bf16[2048,256]{1,0:T(8,128)(2,1)}, bf16[2048,256]{1,0:T(8,128)(2,1)}, u32[]{:S(2)}, u32[]{:S(2)}) collective-permute-start(bf16[2048,256]{1,0:T(8,128)(2,1)} %collective-permute-done.4), channel_id=1, source_target_pairs={{0,12},{1,13},{2,14},{3,15},{16,28},{17,29},{18,30},{19,31},{32,44... | collective-permute-start | bytes 3145736 | tf_op jit(solution)/shard_map/ppermute | solution.py:35
  149.5 12.6 %collective-permute-done.20 = bf16[2048,256]{1,0:T(8,128)(2,1)} collective-permute-done((bf16[2048,256]{1,0:T(8,128)(2,1)S(1)}, bf16[2048,256]{1,0:T(8,128)(2,1)}, u32[]{:S(2)}, u32[]{:S(2)}) %collective-permute-start.20) | collective-permute-done | bytes 1048608 | tf_op jit(solution)/shard_map/ppermute | solution.py:35
  162.1 18.1 %collective-permute-done.21 = bf16[2048,256]{1,0:T(8,128)(2,1)} collective-permute-done((bf16[2048,256]{1,0:T(8,128)(2,1)}, bf16[2048,256]{1,0:T(8,128)(2,1)}, u32[]{:S(2)}, u32[]{:S(2)}) %collective-permute-start.21) | collective-permute-done | bytes 1048608 | tf_op jit(solution)/shard_map/ppermute | solution.py:35
  180.1 3.1 select_bitcast_fusion.1
  183.4 3.1 pad_maximum_fusion.lhs_ref
  187.5 8.8 %collective-permute-done.9 = f32[16,128]{1,0:T(8,128)S(1)} collective-permute-done((f32[16,128]{1,0:T(8,128)S(1)}, f32[16,128]{1,0:T(8,128)S(1)}, u32[]{:S(2)}, u32[]{:S(2)}) %collective-permute-start.9) | collective-permute-done | bytes 8224 | tf_op jit(solution)/shard_map/ppermute | solution.py:35
  196.6 3.4 %collective-permute-done.10 = f32[16,128]{1,0:T(8,128)S(1)} collective-permute-done((f32[16,128]{1,0:T(8,128)S(1)}, f32[16,128]{1,0:T(8,128)S(1)}, u32[]{:S(2)}, u32[]{:S(2)}) %collective-permute-start.10) | collective-permute-done | bytes 8224 | tf_op jit(solution)/shard_map/ppermute | solution.py:35
  203.7 5.1 %collective-permute-done.12 = f32[16,128]{1,0:T(8,128)S(1)} collective-permute-done((f32[16,128]{1,0:T(8,128)S(1)}, f32[16,128]{1,0:T(8,128)S(1)}, u32[]{:S(2)}, u32[]{:S(2)}) %collective-permute-start.12) | collective-permute-done | bytes 8224 | tf_op jit(solution)/shard_map/ppermute | solution.py:35
  208.8 3.2 collective-permute-start.13
  215.5 3.5 %collective-permute-done.14 = f32[16,128]{1,0:T(8,128)S(1)} collective-permute-done((f32[16,128]{1,0:T(8,128)S(1)}, f32[16,128]{1,0:T(8,128)S(1)}, u32[]{:S(2)}, u32[]{:S(2)}) %collective-permute-start.14) | collective-permute-done | bytes 8224 | tf_op jit(solution)/shard_map/ppermute | solution.py:35
  222.1 2.9 collective-permute-start.17
  226.9 9.6 %collective-permute-done.7 = bf16[2048,256]{1,0:T(8,128)(2,1)} collective-permute-done((bf16[2048,256]{1,0:T(8,128)(2,1)S(1)}, bf16[2048,256]{1,0:T(8,128)(2,1)}, u32[]{:S(2)}, u32[]{:S(2)}) %collective-permute-start.7) | collective-permute-done | bytes 1048608 | tf_op jit(solution)/shard_map/ppermute | solution.py:35
  240.1 6.6 %collective-permute-done.16.refs_1_ = bf16[2048,256]{1,0:T(8,128)(2,1)S(1)} collective-permute-done((bf16[2048,256]{1,0:T(8,128)(2,1)S(1)}, bf16[2048,256]{1,0:T(8,128)(2,1)S(1)}, u32[]{:S(2)}, u32[]{:S(2)}) %collective-permute-start.16) | collective-permute-done | bytes 1048608 | tf_op jit(solution)/shard_map/ppermute | solution.py:35
  246.7 18.9 %collective-permute-done.17.refs_2_ = bf16[2048,256]{1,0:T(8,128)(2,1)S(1)} collective-permute-done((bf16[2048,256]{1,0:T(8,128)(2,1)S(1)}, bf16[2048,256]{1,0:T(8,128)(2,1)S(1)}, u32[]{:S(2)}, u32[]{:S(2)}) %collective-permute-start.17) | collective-permute-done | bytes 1048608 | tf_op jit(solution)/shard_map/ppermute | solution.py:35
  265.6 2.6 collective-permute-done.18.refs_3_
  268.5 2.1 weigh.1.other_ref
  272.6 2.9 multiply_convert_fusion.own_ref
  275.5 12.5 %gram.4.refs_0_ = f32[8,256,1024]{2,1,0:T(8,128)} custom-call(s32[7]{0:T(128)S(1)} %concatenate.17.meta_ref, f32[1]{0:T(128)S(6)} %copy.15.damping_ref, bf16[3,2,2048,256]{3,2,1,0:T(8,128)(2,1)} %pad_maximum_fusion.lhs_ref, bf16[2048,1024]{1,0:T(8,128)(2,1)S(1)} %multiply_convert_fusion.own_ref, bf16[2048,1024]{1,0:T(8,128)(2,1)} %copy-done), custom_call_target="tpu_custom_call" | custom-call | flops 6442450944 | bytes 17825792 | tf_op jit(solution)/shard_map/gram/pallas_call | solution.py:103
  288.0 11.6 %gram.5.refs_0_ = f32[8,256,1024]{2,1,0:T(8,128)} custom-call(s32[7]{0:T(128)S(1)} %concatenate.16.meta_ref, f32[1]{0:T(128)S(6)} %copy.15.damping_ref, bf16[3,2,2048,256]{3,2,1,0:T(8,128)(2,1)} %collective-permute-done.22.lhs_ref, bf16[2048,1024]{1,0:T(8,128)(2,1)S(1)} %multiply_convert_fusion.own_ref, ...), custom_call_target="tpu_custom_call", output_to_operand_aliasing={{}: (5, {})} | custom-call | flops 6442450944 | bytes 17825792 | tf_op jit(solution)/shard_map/gram/pallas_call | solution.py:103
  299.6 7.3 %gram.6.refs_0_ = f32[8,256,1024]{2,1,0:T(8,128)} custom-call(s32[3]{0:T(128)S(1)} %add_add_fusion.1.meta_ref, f32[1]{0:T(128)S(6)} %copy.15.damping_ref, bf16[1,2,2048,256]{3,2,1,0:T(8,128)(2,1)S(1)} %maximum_bitcast_fusion.lhs_ref, bf16[2048,1024]{1,0:T(8,128)(2,1)} %copy-done.1, bf16[2048,1024]{1,0:T(8,128)(2,1)} %copy-done, ...), custom_call_target="tpu_custom_call", output_to_operand_aliasing={{}: (5, {})} | custom-call | flops 2147483648 | bytes 11534336 | tf_op jit(solution)/shard_map/gram/pallas_call | solution.py:103
  306.9 7.9 %gram.7 = f32[8,256,1024]{2,1,0:T(8,128)} custom-call(s32[3]{0:T(128)S(1)} %add_add_fusion.meta_ref, f32[1]{0:T(128)S(6)} %copy.15.damping_ref, bf16[1,2,2048,256]{3,2,1,0:T(8,128)(2,1)} %collective-permute-done.8.lhs_ref, bf16[2048,1024]{1,0:T(8,128)(2,1)} %copy-done.1, bf16[2048,1024]{1,0:T(8,128)(2,1)} %copy-done, ...), custom_call_target="tpu_custom_call", output_to_operand_aliasing={{}: (5, {})} | custom-call | flops 2147483648 | bytes 11534336 | tf_op jit(solution)/shard_map/gram/pallas_call | solution.py:103
  (71 shorter events, 24.6 us)
Async XLA Ops:
  7.2 265.4 %all-gather.2.cloned.1.call-start = ((), (), s32[]{:S(2)}) async-start(), calls=%async_computation | async-start | bytes 5242880 | tf_op jit(solution)/shard_map/all_gather | solution.py:129
  7.2 26.4 %collective-permute-start = (bf16[2048,256]{1,0:T(8,128)(2,1)}, bf16[2048,256]{1,0:T(8,128)(2,1)}, u32[]{:S(2)}, u32[]{:S(2)}) collective-permute-start(bf16[2048,256]{1,0:T(8,128)(2,1)} %param.5), channel_id=1, source_target_pairs={{0,12},{1,13},{64,76},{65,77},{2,14},{3,15},{66,78},{67,79},{16,28... | collective-permute-start | bytes 3145736 | tf_op jit(solution)/shard_map/ppermute | solution.py:35
  10.1 28.5 %collective-permute-start.1 = (bf16[2048,256]{1,0:T(8,128)(2,1)}, bf16[2048,256]{1,0:T(8,128)(2,1)S(1)}, u32[]{:S(2)}, u32[]{:S(2)}) collective-permute-start(bf16[2048,256]{1,0:T(8,128)(2,1)} %param.5), channel_id=1, source_target_pairs={{0,64},{1,65},{64,0},{65,1},{2,66},{3,67},{66,2},{67,3},{16,80},{1... | collective-permute-start | bytes 3145736 | tf_op jit(solution)/shard_map/ppermute | solution.py:35
  33.6 25.9 %collective-permute-start.3 = (bf16[2048,256]{1,0:T(8,128)(2,1)}, bf16[2048,256]{1,0:T(8,128)(2,1)}, u32[]{:S(2)}, u32[]{:S(2)}) collective-permute-start(bf16[2048,256]{1,0:T(8,128)(2,1)} %collective-permute-done), channel_id=1, source_target_pairs={{0,64},{1,65},{2,66},{3,67},{16,80},{17,81},{18,82},{19,83},{32,96... | collective-permute-start | bytes 3145736 | tf_op jit(solution)/shard_map/ppermute | solution.py:35
  38.6 28.6 %copy-start.2 = (bf16[2048,256]{1,0:T(8,128)(2,1)S(1)}, bf16[2048,256]{1,0:T(8,128)(2,1)}, u32[]{:S(2)}) copy-start(bf16[2048,256]{1,0:T(8,128)(2,1)} %param.5) | copy-start | bytes 3145732
  62.6 28.7 %collective-permute-start.2 = (bf16[2048,256]{1,0:T(8,128)(2,1)S(1)}, bf16[2048,256]{1,0:T(8,128)(2,1)S(1)}, u32[]{:S(2)}, u32[]{:S(2)}) collective-permute-start(bf16[2048,256]{1,0:T(8,128)(2,1)S(1)} %get-tuple-element.7), channel_id=1, source_target_pairs={{0,66},{1,67},{64,2},{65,3},{2,64},{3,65},{66,0},{67,1},{16,82},{1... | collective-permute-start | bytes 3145736 | tf_op jit(solution)/shard_map/ppermute | solution.py:35
  67.2 43.8 %collective-permute-start.6 = (bf16[2048,256]{1,0:T(8,128)(2,1)S(1)}, bf16[2048,256]{1,0:T(8,128)(2,1)S(1)}, u32[]{:S(2)}, u32[]{:S(2)}) collective-permute-start(bf16[2048,256]{1,0:T(8,128)(2,1)S(1)} %copy-done.2), channel_id=1, source_target_pairs={{0,66},{1,67},{64,2},{65,3},{2,64},{3,65},{66,0},{67,1},{16,82},{1... | collective-permute-start | bytes 3145736 | tf_op jit(solution)/shard_map/ppermute | solution.py:35
  91.3 20.6 %collective-permute-start.19 = (bf16[2048,256]{1,0:T(8,128)(2,1)S(1)}, bf16[2048,256]{1,0:T(8,128)(2,1)S(1)}, u32[]{:S(2)}, u32[]{:S(2)}) collective-permute-start(bf16[2048,256]{1,0:T(8,128)(2,1)S(1)} %collective-permute-done.2), channel_id=1, source_target_pairs={{0,12},{1,13},{2,14},{3,15},{16,28},{17,29},{18,30},{19,31},{32,44... | collective-permute-start | bytes 3145736 | tf_op jit(solution)/shard_map/ppermute | solution.py:35
  113.4 26.2 %collective-permute-start.4 = (bf16[2048,256]{1,0:T(8,128)(2,1)S(1)}, bf16[2048,256]{1,0:T(8,128)(2,1)}, u32[]{:S(2)}, u32[]{:S(2)}) collective-permute-start(bf16[2048,256]{1,0:T(8,128)(2,1)S(1)} %get-tuple-element.12), channel_id=1, source_target_pairs={{0,4},{1,5},{64,68},{65,69},{2,6},{3,7},{66,70},{67,71},{16,20},{1... | collective-permute-start | bytes 3145736 | tf_op jit(solution)/shard_map/ppermute | solution.py:35
  113.4 48.7 %collective-permute-start.20 = (bf16[2048,256]{1,0:T(8,128)(2,1)S(1)}, bf16[2048,256]{1,0:T(8,128)(2,1)}, u32[]{:S(2)}, u32[]{:S(2)}) collective-permute-start(bf16[2048,256]{1,0:T(8,128)(2,1)S(1)} %copy-done.2), channel_id=1, source_target_pairs={{0,4},{1,5},{2,6},{3,7},{16,20},{17,21},{18,22},{19,23},{32,36},{3... | collective-permute-start | bytes 3145736 | tf_op jit(solution)/shard_map/ppermute | solution.py:35
  117.3 62.8 %collective-permute-start.21 = (bf16[2048,256]{1,0:T(8,128)(2,1)}, bf16[2048,256]{1,0:T(8,128)(2,1)}, u32[]{:S(2)}, u32[]{:S(2)}) collective-permute-start(bf16[2048,256]{1,0:T(8,128)(2,1)} %get-tuple-element.6), channel_id=1, source_target_pairs={{0,4},{1,5},{64,68},{65,69},{2,6},{3,7},{66,70},{67,71},{16,20},{1... | collective-permute-start | bytes 3145736 | tf_op jit(solution)/shard_map/ppermute | solution.py:35
  139.6 40.5 %collective-permute-start.5 = (bf16[2048,256]{1,0:T(8,128)(2,1)}, bf16[2048,256]{1,0:T(8,128)(2,1)}, u32[]{:S(2)}, u32[]{:S(2)}) collective-permute-start(bf16[2048,256]{1,0:T(8,128)(2,1)} %collective-permute-done.4), channel_id=1, source_target_pairs={{0,12},{1,13},{2,14},{3,15},{16,28},{17,29},{18,30},{19,31},{32,44... | collective-permute-start | bytes 3145736 | tf_op jit(solution)/shard_map/ppermute | solution.py:35
  183.4 3.2 copy-start.8
  183.4 3.2 copy-start.3
  183.4 31.9 %copy-start.5 = (bf16[2048,256]{1,0:T(8,128)(2,1)S(1)}, bf16[2048,256]{1,0:T(8,128)(2,1)}, u32[]{:S(2)}) copy-start(bf16[2048,256]{1,0:T(8,128)(2,1)} %get-tuple-element.11) | copy-start | bytes 3145732
  183.4 35.6 %copy-start.7 = (f32[2048]{0:T(1024)S(1)}, f32[2048]{0:T(1024)}, u32[]{:S(2)}) copy-start(f32[2048]{0:T(1024)} %param.6) | copy-start | bytes 24580
  186.6 101.4 %collective-permute-start.22 = (bf16[3,2,2048,256]{3,2,1,0:T(8,128)(2,1)}, bf16[3,2,2048,256]{3,2,1,0:T(8,128)(2,1)}, u32[]{:S(2)}, u32[]{:S(2)}) collective-permute-start(bf16[3,2,2048,256]{3,2,1,0:T(8,128)(2,1)} %pad_maximum_fusion.lhs_ref), channel_id=1, source_target_pairs={{0,1},{1,0},{64,65},{65,64},{2,3},{3,2},{66,67},{67,66},{16,17},{1... | collective-permute-start | bytes 18874376 | tf_op jit(solution)/shard_map/ppermute | solution.py:35
  187.0 9.3 %collective-permute-start.9 = (f32[16,128]{1,0:T(8,128)S(1)}, f32[16,128]{1,0:T(8,128)S(1)}, u32[]{:S(2)}, u32[]{:S(2)}) collective-permute-start(f32[16,128]{1,0:T(8,128)S(1)} %bitcast.57), channel_id=1, source_target_pairs={{0,1},{1,0},{64,65},{65,64},{2,3},{3,2},{66,67},{67,66},{16,17},{1... | collective-permute-start | bytes 24584 | tf_op jit(solution)/shard_map/ppermute | solution.py:35
  196.3 3.7 %collective-permute-start.10 = (f32[16,128]{1,0:T(8,128)S(1)}, f32[16,128]{1,0:T(8,128)S(1)}, u32[]{:S(2)}, u32[]{:S(2)}) collective-permute-start(f32[16,128]{1,0:T(8,128)S(1)} %add.97), channel_id=1, source_target_pairs={{0,4},{1,5},{64,68},{65,69},{2,6},{3,7},{66,70},{67,71},{16,20},{1... | collective-permute-start | bytes 24584 | tf_op jit(solution)/shard_map/ppermute | solution.py:35
  199.9 3.7 %collective-permute-start.11 = (f32[16,128]{1,0:T(8,128)S(1)}, f32[16,128]{1,0:T(8,128)S(1)}, u32[]{:S(2)}, u32[]{:S(2)}) collective-permute-start(f32[16,128]{1,0:T(8,128)S(1)} %add.98), channel_id=1, source_target_pairs={{0,16},{1,17},{64,80},{65,81},{2,18},{3,19},{66,82},{67,83},{16,0}... | collective-permute-start | bytes 24584 | tf_op jit(solution)/shard_map/ppermute | solution.py:35
  203.6 5.2 %collective-permute-start.12 = (f32[16,128]{1,0:T(8,128)S(1)}, f32[16,128]{1,0:T(8,128)S(1)}, u32[]{:S(2)}, u32[]{:S(2)}) collective-permute-start(f32[16,128]{1,0:T(8,128)S(1)} %add.99), channel_id=1, source_target_pairs={{0,8},{1,9},{64,72},{65,73},{2,10},{3,11},{66,74},{67,75},{16,24},... | collective-permute-start | bytes 24584 | tf_op jit(solution)/shard_map/ppermute | solution.py:35
  208.8 5.2 %collective-permute-start.13 = (f32[16,128]{1,0:T(8,128)S(1)}, f32[16,128]{1,0:T(8,128)S(1)}, u32[]{:S(2)}, u32[]{:S(2)}) collective-permute-start(f32[16,128]{1,0:T(8,128)S(1)} %add.100), channel_id=1, source_target_pairs={{0,32},{1,33},{64,96},{65,97},{2,34},{3,35},{66,98},{67,99},{16,48... | collective-permute-start | bytes 24584 | tf_op jit(solution)/shard_map/ppermute | solution.py:35
  213.9 5.2 %collective-permute-start.14 = (f32[16,128]{1,0:T(8,128)S(1)}, f32[16,128]{1,0:T(8,128)S(1)}, u32[]{:S(2)}, u32[]{:S(2)}) collective-permute-start(f32[16,128]{1,0:T(8,128)S(1)} %add.101), channel_id=1, source_target_pairs={{0,2},{1,3},{64,66},{65,67},{2,0},{3,1},{66,64},{67,65},{16,18},{1... | collective-permute-start | bytes 24584 | tf_op jit(solution)/shard_map/ppermute | solution.py:35
  215.3 21.1 %collective-permute-start.7 = (bf16[2048,256]{1,0:T(8,128)(2,1)S(1)}, bf16[2048,256]{1,0:T(8,128)(2,1)}, u32[]{:S(2)}, u32[]{:S(2)}) collective-permute-start(bf16[2048,256]{1,0:T(8,128)(2,1)S(1)} %copy-done.5), channel_id=1, source_target_pairs={{0,4},{1,5},{64,68},{65,69},{2,6},{3,7},{66,70},{67,71},{16,20},{1... | collective-permute-start | bytes 3145736 | tf_op jit(solution)/shard_map/ppermute | solution.py:35
  219.6 5.4 %collective-permute-start.23 = (f32[256]{0:T(256)S(1)}, f32[256]{0:T(256)S(1)}, u32[]{:S(2)}, u32[]{:S(2)}) collective-permute-start(f32[256]{0:T(256)S(1)} %bitcast.61), channel_id=1, source_target_pairs={{0,64},{1,65},{64,0},{65,1},{2,66},{3,67},{66,2},{67,3},{16,80},{1... | collective-permute-start | bytes 3080 | tf_op jit(solution)/shard_map/ppermute | solution.py:35
  220.5 26.1 %collective-permute-start.16 = (bf16[2048,256]{1,0:T(8,128)(2,1)S(1)}, bf16[2048,256]{1,0:T(8,128)(2,1)S(1)}, u32[]{:S(2)}, u32[]{:S(2)}) collective-permute-start(bf16[2048,256]{1,0:T(8,128)(2,1)S(1)} %collective-permute-done.1.refs_0_), channel_id=1, source_target_pairs={{0,16},{1,17},{64,80},{65,81},{2,18},{3,19},{66,82},{67,83},{16,0}... | collective-permute-start | bytes 3145736 | tf_op jit(solution)/shard_map/ppermute | solution.py:35
  222.1 43.4 %collective-permute-start.17 = (bf16[2048,256]{1,0:T(8,128)(2,1)S(1)}, bf16[2048,256]{1,0:T(8,128)(2,1)S(1)}, u32[]{:S(2)}, u32[]{:S(2)}) collective-permute-start(bf16[2048,256]{1,0:T(8,128)(2,1)S(1)} %collective-permute-done.1.refs_0_), channel_id=1, source_target_pairs={{0,32},{1,33},{64,96},{65,97},{2,34},{3,35},{66,98},{67,99},{16,48... | collective-permute-start | bytes 3145736 | tf_op jit(solution)/shard_map/ppermute | solution.py:35
  225.0 43.1 %collective-permute-start.18 = (bf16[2048,256]{1,0:T(8,128)(2,1)S(1)}, bf16[2048,256]{1,0:T(8,128)(2,1)S(1)}, u32[]{:S(2)}, u32[]{:S(2)}) collective-permute-start(bf16[2048,256]{1,0:T(8,128)(2,1)S(1)} %collective-permute-done.1.refs_0_), channel_id=1, source_target_pairs={{0,48},{1,49},{64,112},{65,113},{2,50},{3,51},{66,114},{67,115},{1... | collective-permute-start | bytes 3145736 | tf_op jit(solution)/shard_map/ppermute | solution.py:35
  236.4 3.7 %collective-permute-start.15 = (f32[16,128]{1,0:T(8,128)S(1)}, f32[16,128]{1,0:T(8,128)S(1)}, u32[]{:S(2)}, u32[]{:S(2)}) collective-permute-start(f32[16,128]{1,0:T(8,128)S(1)} %bitcast.60), channel_id=1, source_target_pairs={{0,64},{1,65},{64,0},{65,1},{2,66},{3,67},{66,2},{67,3},{16,80},{1... | collective-permute-start | bytes 24584 | tf_op jit(solution)/shard_map/ppermute | solution.py:35
  240.1 66.8 %collective-permute-start.8 = (bf16[1,2,2048,256]{3,2,1,0:T(8,128)(2,1)S(1)}, bf16[1,2,2048,256]{3,2,1,0:T(8,128)(2,1)}, u32[]{:S(2)}, u32[]{:S(2)}) collective-permute-start(bf16[1,2,2048,256]{3,2,1,0:T(8,128)(2,1)S(1)} %maximum_bitcast_fusion.lhs_ref), channel_id=1, source_target_pairs={{0,1},{1,0},{64,65},{65,64},{2,3},{3,2},{66,67},{67,66},{16,17},{1... | collective-permute-start | bytes 6291464 | tf_op jit(solution)/shard_map/ppermute | solution.py:35
  270.6 2.0 copy-start
  275.5 12.5 %copy-start.1 = (bf16[2048,1024]{1,0:T(8,128)(2,1)}, bf16[2048,1024]{1,0:T(8,128)(2,1)S(1)}, u32[]{:S(2)}) copy-start(bf16[2048,1024]{1,0:T(8,128)(2,1)S(1)} %multiply_convert_fusion.own_ref) | copy-start | bytes 12582916
  (2 other events, 3.4 us)
Sparse Core Ops, SparseCore 0:
  147.6 51.8 all-gather.1

commit v2 on v0

v2 whole, which is shorter than its diff:
```python
import functools

import jax
import jax.numpy as jnp
from jax import lax
from jax.experimental import pallas as pl
from jax.experimental.pallas import tpu as pltpu
from jax.sharding import PartitionSpec as P

AXES = ("slab", "trow", "tcol")
N_X, N_Y, N_Z, N_CORE = 4, 4, 4, 2


def index_of(x, y, z, core):
    return ((z % 2) * N_Y + y) * 16 + x * 4 + (z // 2) * 2 + core


def is_native(x, z):
    return (x // 2) == (z % 2)


def pairs(route):
    found = []
    for x in range(N_X):
        for y in range(N_Y):
            for z in range(N_Z):
                step = route(x, z)
                if step is None:
                    continue
                dx, dy, dz, dcore = step
                for core in range(N_CORE):
                    target = index_of(x ^ dx, y ^ dy, z ^ dz, core ^ dcore)
                    found.append((index_of(x, y, z, core), target))
    return found


def move(value, x=0, y=0, z=0, core=0):
    return lax.ppermute(value, AXES, pairs(lambda cx, cz: (x, y, z, core)))


def move_by_role(value, native=None, far=None):
    return lax.ppermute(value, AXES, pairs(lambda cx, cz: native if is_native(cx, cz) else far))


def weigh_kernel(blocks_ref, spread_ref, *refs, places):
    *shard_refs, out_ref = refs
    lanes = spread_ref.shape[1]
    for m, shard_ref in zip(places, shard_refs):
        width = shard_ref.shape[1]
        for part in range(0, width, lanes):
            scaled = shard_ref[:, part:part + lanes].astype(jnp.float32) * spread_ref[...]
            at = pl.multiple_of(blocks_ref[m] * width + part, lanes)
            out_ref[:, pl.ds(at, lanes)] = scaled.astype(jnp.bfloat16)


def weigh(blocks, spread, shards, places):
    rows, width = shards[0].shape
    step = rows // 4

    def block(columns):
        return pl.BlockSpec((step, columns), lambda i, blocks: (i, 0))

    return pl.pallas_call(
        functools.partial(weigh_kernel, places=places),
        out_shape=jax.ShapeDtypeStruct((rows, width * N_Y), jnp.bfloat16),
        grid_spec=pltpu.PrefetchScalarGridSpec(
            num_scalar_prefetch=1,
            grid=(rows // step,),
            in_specs=[block(spread.shape[1])] + [block(width)] * len(shards),
            out_specs=block(width * N_Y),
        ),
        compiler_params=pltpu.CompilerParams(vmem_limit_bytes=60 * 2**20),
        cost_estimate=pl.CostEstimate(flops=0, bytes_accessed=0, transcendentals=0),
        name="weigh",
    )(blocks, spread, *shards)


N_TILES = 4
TILE_AT, DIAGONAL_AT, OWN_AT, OTHER_AT, ROW_AT, BLOCK_AT = 0, 4, 8, 12, 16, 17
FIRST_NEEDS, LATER_NEEDS = (1, 3), ((2, 6), (7, 5), (4,))


def gram_kernel(meta_ref, damping_ref, own_hbm, shards_hbm, *refs, samples, fresh):
    if fresh:
        before_hbm, spread_hbm, column_hbm = refs[:3]
        out_ref, other_hbm, weighted, slots, weighted_sems, slot_sems, column, spread, column_sems = refs[3:]
    else:
        before_hbm = refs[0]
        out_ref, weighted, slots, weighted_sems, slot_sems = refs[2:]
    step = pl.program_id(0)
    contract = (((0,), (0,)), ((), ()))
    scale = 1.0 / samples

    def slot_copy(n):
        return pltpu.make_async_copy(shards_hbm.at[n], slots.at[n], slot_sems.at[n])

    def product(n, at):
        return lax.dot_general(
            slots[meta_ref[at + step]], weighted[n], contract, preferred_element_type=jnp.float32)

    own_copy = pltpu.make_async_copy(own_hbm, weighted.at[0], weighted_sems.at[0])
    other_copy = pltpu.make_async_copy(before_hbm, weighted.at[1], weighted_sems.at[1])
    if fresh:
        column_copies = (
            pltpu.make_async_copy(column_hbm, column, column_sems.at[0]),
            pltpu.make_async_copy(spread_hbm, spread, column_sems.at[1]))
        hand_on = pltpu.make_async_copy(weighted.at[1], other_hbm, weighted_sems.at[1])

    def scale_column():
        rows, width = column.shape
        lanes = spread.shape[1]
        chunk = 512

        @pl.loop(0, rows // chunk)
        def _(i):
            at_rows = pl.ds(pl.multiple_of(i * chunk, chunk), chunk)
            weight = spread[at_rows, :]
            for part in range(0, width, lanes):
                scaled = column[at_rows, part:part + lanes].astype(jnp.float32) * weight
                at = pl.multiple_of(meta_ref[BLOCK_AT] * width + part, lanes)
                weighted[1, at_rows, pl.ds(at, lanes)] = scaled.astype(jnp.bfloat16)

    @pl.when(step == 0)
    def _():
        own_copy.start()
        slot_copy(0).start()
        if fresh:
            for copy in column_copies:
                copy.start()
        other_copy.start()
        for n in FIRST_NEEDS:
            slot_copy(n).start()
        own_copy.wait()
        slot_copy(0).wait()
        out_ref[0] = product(0, OWN_AT)
        other_copy.wait()
        if fresh:
            for copy in column_copies:
                copy.wait()
            scale_column()
            hand_on.start()
        for n in FIRST_NEEDS:
            slot_copy(n).wait()
        for needed in LATER_NEEDS:
            for n in needed:
                slot_copy(n).start()
        out_ref[0] = (out_ref[0] + product(1, OTHER_AT)) * scale

    for at, needed in enumerate(LATER_NEEDS):
        @pl.when(step == at + 1)
        def _(needed=needed):
            for n in needed:
                slot_copy(n).wait()

    @pl.when(step > 0)
    def _():
        out_ref[0] = (product(0, OWN_AT) + product(1, OTHER_AT)) * scale

    @pl.when(meta_ref[DIAGONAL_AT + step] == 1)
    def _():
        height = out_ref.shape[1]
        at = pl.multiple_of(meta_ref[ROW_AT] * height, height)
        eye = (lax.broadcasted_iota(jnp.int32, (height, height), 0)
               == lax.broadcasted_iota(jnp.int32, (height, height), 1))
        out_ref[0, :, pl.ds(at, height)] += jnp.where(eye, damping_ref[0], 0.0)

    if fresh:
        @pl.when(step == N_TILES - 1)
        def _():
            hand_on.wait()


def gram_blocks(meta, damping, own, other, shards, samples, spread=None, column=None, into=None):
    _, rows, height = shards.shape
    width = own.shape[1]
    fresh = into is None
    hbm = pl.BlockSpec(memory_space=pl.ANY)
    arrays = [meta, damping, own, shards] + ([other, spread, column] if fresh else [other, into])
    result = jax.ShapeDtypeStruct((2 * N_TILES, height, width), jnp.float32)
    block = pl.BlockSpec((1, height, width), lambda i, meta: (meta[i], 0, 0))
    scratch = [
        pltpu.VMEM((2, rows, width), jnp.bfloat16),
        pltpu.VMEM((8, rows, height), jnp.bfloat16),
        pltpu.SemaphoreType.DMA((2,)),
        pltpu.SemaphoreType.DMA((8,)),
    ]
    if fresh:
        scratch += [
            pltpu.VMEM((rows, height), jnp.bfloat16),
            pltpu.VMEM(spread.shape, jnp.float32),
            pltpu.SemaphoreType.DMA((2,)),
        ]
    flops = N_TILES * 2 * 2 * rows * height * width
    moved = 8 * rows * height * 2 + N_TILES * height * width * 4 + 4 * rows * width
    return pl.pallas_call(
        functools.partial(gram_kernel, samples=samples, fresh=fresh),
        out_shape=(result, jax.ShapeDtypeStruct(own.shape, own.dtype)) if fresh else result,
        grid_spec=pltpu.PrefetchScalarGridSpec(
            num_scalar_prefetch=1,
            grid=(N_TILES,),
            in_specs=[pl.BlockSpec(memory_space=pltpu.SMEM)] + [hbm] * (len(arrays) - 2),
            out_specs=(block, hbm) if fresh else block,
            scratch_shapes=scratch,
        ),
        input_output_aliases={} if fresh else {len(arrays) - 1: 0},
        compiler_params=pltpu.CompilerParams(vmem_limit_bytes=60 * 2**20),
        cost_estimate=pl.CostEstimate(flops=flops, bytes_accessed=moved, transcendentals=0),
        name="gram_first" if fresh else "gram",
    )(*arrays)


def local(design, targets, coeffs, threshold, damping):
    rows, width = design.shape
    samples = rows * lax.axis_size("slab")
    slab, row, col = lax.axis_index("slab"), lax.axis_index("trow"), lax.axis_index("tcol")
    x, zh, core = col // 4, (col // 2) % 2, col % 2
    native = (x // 2) == slab
    tie = lax.optimization_barrier

    def pick(if_native, if_far):
        return jnp.where(native, if_native, if_far)

    columns = lax.all_gather(design, "trow", axis=1, tiled=True)

    from_xo = move(design, x=3)
    first = (row == 0) & (col == 0)
    share = jnp.where(first, targets, 0.0) - jnp.dot(design, coeffs, preferred_element_type=jnp.float32)
    share = share.reshape(rows // 128, 128)
    share = share + move(share, z=2)
    design_z, share = tie((design, share))
    from_zp = move(design_z, z=1)
    from_zo = move(design_z, z=3)
    share = share + move(share, x=1)
    design_x, share = tie((design, share))
    from_xp = move(design_x, x=1)
    for where in ({"core": 1}, {"y": 1}, {"y": 2}, {"x": 3}):
        share = share + move(share, **where)
    from_zp, from_zo, from_xp, from_xo, share = tie((from_zp, from_zo, from_xp, from_xo, share))

    second_xp = move(from_xo, x=1)
    by_zo, by_zp, share_other = tie((pick(from_xo, from_zp), pick(from_xo, from_xp), move(share, z=1)))
    second_zo = move(by_zo, z=3)
    second_zp = move(by_zp, z=1)
    other_y1 = move(from_zp, y=1)
    other_y3 = move(from_zp, y=3)
    second_xp, from_xp = tie((second_xp, from_xp))
    by_z = pick(second_xp, from_xp)
    second_xp, second_zo, second_zp, by_z, share, from_zp_y = tie((second_xp, second_zo, second_zp, by_z, share, from_zp))

    third_xp = move(second_zo, x=1)
    third_xo = move_by_role(second_zo, native=(3, 0, 0, 0))
    third_z = move_by_role(by_z, native=(0, 0, 1, 0), far=(0, 0, 3, 0))
    by_z2, from_zp_y, other_y1, other_y3 = tie((second_xp, from_zp_y, other_y1, other_y3))
    third_z2 = move_by_role(by_z2, far=(0, 0, 2, 0))
    other_y2 = move(from_zp_y, y=2)

    cutoff = threshold[0]
    residual, residual_other = share.reshape(rows), share_other.reshape(rows)
    weight = cutoff / jnp.maximum(jnp.abs(residual), cutoff)
    weight_other = cutoff / jnp.maximum(jnp.abs(residual_other), cutoff)
    influence = weight * residual
    local_grad = jnp.dot(influence, design.astype(jnp.float32), precision=lax.Precision.HIGHEST)
    spread = jnp.broadcast_to(weight_other[:, None], (rows, 128))
    blocks = row ^ jnp.arange(N_Y, dtype=jnp.int32)
    columns, other_y1, other_y3 = tie((columns, other_y1, other_y3))
    own_weighted = (columns.astype(jnp.float32) * weight[:, None]).astype(jnp.bfloat16)
    other_weighted = weigh(blocks, spread, [from_zp, other_y1, other_y3], (0, 1, 3))
    third_z, own_weighted, other_weighted, spread, local_grad = tie(
        (third_z, own_weighted, other_weighted, spread, local_grad))
    here = jnp.stack([
        pick(design, from_xo), pick(from_zp, second_xp), second_zo, second_zp,
        third_xp, third_z, pick(from_zo, third_xo), pick(from_xp, third_z2)])
    here, other_y2 = tie((here, other_y2))

    sibling = move(here, core=1)

    column_a = pick(x, x ^ 3)
    column_b = column_a ^ 1
    own_slots = pick(jnp.array([0, 2, 7, 4]), jnp.array([0, 6, 1, 7]))
    other_slots = pick(jnp.array([1, 6, 3, 5]), jnp.array([3, 2, 5, 4]))

    def describe(core_at):
        places = ((column_a, zh), (column_a, 1 - zh), (column_b, zh), (column_b, 1 - zh))
        tiles = jnp.stack([column * 4 + at * 2 + core_at - 8 * slab for column, at in places])
        diagonal = tiles + 8 * slab == col
        return jnp.concatenate([tiles, diagonal, own_slots, other_slots, row[None], blocks[2:3]]).astype(jnp.int32)

    result, other_weighted = gram_blocks(
        describe(core), damping, own_weighted, other_weighted, here, samples, spread=spread, column=other_y2)
    result, local_grad = tie((result, local_grad))
    gradient = -(local_grad + move(local_grad, z=1)) / samples
    result = gram_blocks(
        describe(1 - core), damping, own_weighted, other_weighted, sibling, samples, into=result)
    hessian = result.reshape(2 * N_TILES, 1, width, columns.shape[1])
    return (hessian, gradient)


def solution(mesh):
    in_specs = (P("slab", ("tcol", "trow")), P("slab"), P(("tcol", "trow")), P(), P())
    out_specs = (P("slab", "trow", None, "tcol"), P(("tcol", "trow")))
    return jax.shard_map(local, mesh=mesh, in_specs=in_specs, out_specs=out_specs, check_vma=False)
```

time: 634 us -> 161 us (0.25)
  waiting for transfers between devices: 382 us -> 42.8 us
  blocking collectives: 180 us -> 0 us
  Pallas kernels: 0 us -> 37.7 us
  starting transfers between devices: 0.11 us -> 31.8 us
  matrix products: 26.4 us -> 2.1 us
    psum x1 -> x0, waiting for transfers between devices: 376 us -> none  [local(): summed = lax.psum(products, 'slab')]
    psum x2 -> x0, blocking collectives: 180 us -> none  [the longest x1 175 us: local(): predicted = lax.psum(partial_value, ('trow', 'tcol'))]
    ppermute x0 -> x23, waiting for transfers between devices: none -> 42.1 us  [the longest x20 42.1 us: move(): return lax.ppermute(value, AXES, pairs(lambda cx, cz: (x, y, z, core)))]
    pallas_call x0 -> x3, Pallas kernels: none -> 37.7 us  [the longest x2 31.8 us: gram_blocks(): pl.pallas_call(functools.partial(gram_kernel, samples=samples, fresh=fres...]
    ppermute x0 -> x23, starting transfers between devices: none -> 31.7 us  [the longest x20 26.9 us: move(): return lax.ppermute(value, AXES, pairs(lambda cx, cz: (x, y, z, core)))]
    dot_general x2 -> x1, matrix products: 25.9 us -> 1.59 us  [local(): jnp.dot(design, coeffs, preferred_element_type=jnp.float32)]
    reshape x1 -> x0, local copies, waits for them, and re-layouts: 9.28 us -> none  [local(): (own_part / samples).reshape(blocks_mine, 1, shard_width, col_width)]
    div x2, other arithmetic: 9 us -> 0.57 us  [the longest x1 0.57 us: local(): gradient = -(local_grad + move(local_grad, z=1)) / samples]
  transfers between devices with their start and end apart: 3 -> 24, of which waited for: 2 -> 16; matrix products, arithmetic and copies ran while one was open for 1% -> 20% of each run, Pallas kernels for 0% -> 14%
where the time goes in v2:
time: 161 us; the launch traced here: 160 us
  waiting for transfers between devices  42.8 us (27%)
  Pallas kernels  37.7 us (23%)
  starting transfers between devices  31.8 us (20%)
  other arithmetic  18.7 us (12%)
  between operations  15.5 us (10%)
  local copies, waits for them, and re-layouts  11.9 us (7%)
  matrix products  2.1 us (1%)
    ppermute x20, waiting for transfers between devices, move(): return lax.ppermute(value, AXES, pairs(lambda cx, cz: (x, y, z, core)))  42.1 us
    pallas_call x2, Pallas kernels, gram_blocks(): pl.pallas_call(functools.partial(gram_kernel, samples=samples, fresh=fres...  31.8 us
    ppermute x20, starting transfers between devices, move(): return lax.ppermute(value, AXES, pairs(lambda cx, cz: (x, y, z, core)))  26.9 us
    unnamed x23, local copies, waits for them, and re-layouts  7.37 us
    unnamed x3, other arithmetic  6.18 us
    pallas_call x1, Pallas kernels, weigh(): pl.pallas_call(functools.partial(weigh_kernel, places=places), out_shape=...  5.88 us
    convert_element_type x1, other arithmetic, local(): (columns.astype(jnp.float32) * weight[:, None]).astype(jnp.bfloat16)  4.9 us
    ppermute x3, starting transfers between devices, move_by_role(): lax.ppermute(value, AXES, pairs(lambda cx, cz: native if is_native(cx, cz...  4.83 us
  transfers between devices with their start and end apart: 24, of which 16 were waited for; matrix products, arithmetic and copies ran while one was open for 20% of the time, Pallas kernels for 14%

profile of v2, /device:TPU:0, one launch (start us, length us, event | category | flops | bytes accessed | tf_op | source)
XLA Modules:
  0.0 160.4 jit_solution(5669524140169988828)
XLA Ops:
  8.6 1.6 fusion.2
  10.9 3.3 %collective-permute-start = (f32[16,128]{1,0:T(8,128)S(1)}, f32[16,128]{1,0:T(8,128)S(1)}, u32[]{:S(2)}, u32[]{:S(2)}) collective-permute-start(f32[16,128]{1,0:T(8,128)S(1)} %subtract_bitcast_fusion), channel_id=1, source_target_pairs={{0,2},{1,3},{64,66},{65,67},{2,0},{3,1},{66,64},{67,65},{16,18},{1... | collective-permute-start | bytes 24584 | tf_op jit(solution)/shard_map/ppermute | solution.py:38
  14.2 1.8 %collective-permute-done = f32[16,128]{1,0:T(8,128)S(1)} collective-permute-done((f32[16,128]{1,0:T(8,128)S(1)}, f32[16,128]{1,0:T(8,128)S(1)}, u32[]{:S(2)}, u32[]{:S(2)}) %collective-permute-start) | collective-permute-done | bytes 8224 | tf_op jit(solution)/shard_map/ppermute | solution.py:38
  17.3 2.1 %collective-permute-start.5 = (bf16[2048,256]{1,0:T(8,128)(2,1)}, bf16[2048,256]{1,0:T(8,128)(2,1)}, u32[]{:S(2)}, u32[]{:S(2)}) collective-permute-start(bf16[2048,256]{1,0:T(8,128)(2,1)} %param.9), channel_id=1, source_target_pairs={{0,12},{1,13},{64,76},{65,77},{2,14},{3,15},{66,78},{67,79},{16,28... | collective-permute-start | bytes 3145736 | tf_op jit(solution)/shard_map/ppermute | solution.py:38
  19.4 1.6 collective-permute-start.1
  21.0 2.5 %collective-permute-start.2 = (bf16[2048,256]{1,0:T(8,128)(2,1)}, bf16[2048,256]{1,0:T(8,128)(2,1)}, u32[]{:S(2)}, u32[]{:S(2)}) collective-permute-start(bf16[2048,256]{1,0:T(8,128)(2,1)} %param.9), channel_id=1, source_target_pairs={{0,66},{1,67},{64,2},{65,3},{2,64},{3,65},{66,0},{67,1},{16,82},{1... | collective-permute-start | bytes 3145736 | tf_op jit(solution)/shard_map/ppermute | solution.py:38
  25.3 1.6 collective-permute-start.7
  26.9 2.2 %collective-permute-done.7 = f32[16,128]{1,0:T(8,128)S(1)} collective-permute-done((f32[16,128]{1,0:T(8,128)S(1)}, f32[16,128]{1,0:T(8,128)S(1)}, u32[]{:S(2)}, u32[]{:S(2)}) %collective-permute-start.7) | collective-permute-done | bytes 8224 | tf_op jit(solution)/shard_map/ppermute | solution.py:38
  29.1 3.2 %collective-permute-start.8 = (f32[16,128]{1,0:T(8,128)S(1)}, f32[16,128]{1,0:T(8,128)S(1)}, u32[]{:S(2)}, u32[]{:S(2)}) collective-permute-start(f32[16,128]{1,0:T(8,128)S(1)} %add.96), channel_id=1, source_target_pairs={{0,32},{1,33},{64,96},{65,97},{2,34},{3,35},{66,98},{67,99},{16,48... | collective-permute-start | bytes 24584 | tf_op jit(solution)/shard_map/ppermute | solution.py:38
  32.3 2.1 %collective-permute-done.8 = f32[16,128]{1,0:T(8,128)S(1)} collective-permute-done((f32[16,128]{1,0:T(8,128)S(1)}, f32[16,128]{1,0:T(8,128)S(1)}, u32[]{:S(2)}, u32[]{:S(2)}) %collective-permute-start.8) | collective-permute-done | bytes 8224 | tf_op jit(solution)/shard_map/ppermute | solution.py:38
  36.1 6.6 %collective-permute-done.9 = f32[16,128]{1,0:T(8,128)S(1)} collective-permute-done((f32[16,128]{1,0:T(8,128)S(1)}, f32[16,128]{1,0:T(8,128)S(1)}, u32[]{:S(2)}, u32[]{:S(2)}) %collective-permute-start.9) | collective-permute-done | bytes 8224 | tf_op jit(solution)/shard_map/ppermute | solution.py:38
  43.1 2.3 %collective-permute-done.2 = bf16[2048,256]{1,0:T(8,128)(2,1)} collective-permute-done((bf16[2048,256]{1,0:T(8,128)(2,1)}, bf16[2048,256]{1,0:T(8,128)(2,1)}, u32[]{:S(2)}, u32[]{:S(2)}) %collective-permute-start.2) | collective-permute-done | bytes 1048608 | tf_op jit(solution)/shard_map/ppermute | solution.py:38
  46.4 1.6 collective-permute-start.15
  48.0 2.2 %collective-permute-start.16 = (bf16[2048,256]{1,0:T(8,128)(2,1)S(1)}, bf16[2048,256]{1,0:T(8,128)(2,1)S(1)}, u32[]{:S(2)}, u32[]{:S(2)}) collective-permute-start(bf16[2048,256]{1,0:T(8,128)(2,1)S(1)} %collective-permute-done.1.refs_0_), channel_id=1, source_target_pairs={{0,48},{1,49},{64,112},{65,113},{2,50},{3,51},{66,114},{67,115},{1... | collective-permute-start | bytes 3145736 | tf_op jit(solution)/shard_map/ppermute | solution.py:38
  51.7 1.4 broadcast_select_fusion.1
  54.4 1.6 %collective-permute-start.12 = (bf16[2048,256]{1,0:T(8,128)(2,1)S(1)}, bf16[2048,256]{1,0:T(8,128)(2,1)}, u32[]{:S(2)}, u32[]{:S(2)}) collective-permute-start(bf16[2048,256]{1,0:T(8,128)(2,1)S(1)} %get-tuple-element.49), channel_id=1, source_target_pairs={{0,66},{1,67},{64,2},{65,3},{2,64},{3,65},{66,0},{67,1},{16,82},{1... | collective-permute-start | bytes 3145736 | tf_op jit(solution)/shard_map/ppermute | solution.py:38
  56.0 2.5 %bitcast_dynamic-update-slice_fusion.7 = bf16[8,2048,256]{2,1,0:T(8,128)(2,1)} fusion(bf16[2048,256]{1,0:T(8,128)(2,1)} %param.9, bf16[2048,256]{1,0:T(8,128)(2,1)} %collective-permute-done.5, pred[]{:T(512)S(6)} %eq.22), kind=kLoop, calls=%fused_computation.8 | loop fusion | flops 524287 | bytes 3145729
  58.5 13.2 %collective-permute-done.10 = bf16[2048,256]{1,0:T(8,128)(2,1)} collective-permute-done((bf16[2048,256]{1,0:T(8,128)(2,1)}, bf16[2048,256]{1,0:T(8,128)(2,1)}, u32[]{:S(2)}, u32[]{:S(2)}) %collective-permute-start.10) | collective-permute-done | bytes 1048608 | tf_op jit(solution)/shard_map/ppermute | solution.py:38
  71.7 2.3 %broadcast_select_fusion = bf16[2048,256]{1,0:T(8,128)(2,1)} fusion(bf16[2048,256]{1,0:T(8,128)(2,1)} %collective-permute-done.10, bf16[2048,256]{1,0:T(8,128)(2,1)S(1)} %collective-permute-done.4, pred[]{:T(512)S(6)} %eq.22), kind=kLoop, calls=%fused_computation.9 | loop fusion | flops 524288 | bytes 3145729 | tf_op jit(solution)/shard_map/jit(_where)/select_n | solution.py:221
  74.0 1.9 %collective-permute-done.12 = bf16[2048,256]{1,0:T(8,128)(2,1)} collective-permute-done((bf16[2048,256]{1,0:T(8,128)(2,1)S(1)}, bf16[2048,256]{1,0:T(8,128)(2,1)}, u32[]{:S(2)}, u32[]{:S(2)}) %collective-permute-start.12) | collective-permute-done | bytes 1048608 | tf_op jit(solution)/shard_map/ppermute | solution.py:38
  76.2 1.4 collective-permute-start.17
  77.6 4.1 %collective-permute-start.18 = (bf16[2048,256]{1,0:T(8,128)(2,1)}, bf16[2048,256]{1,0:T(8,128)(2,1)}, u32[]{:S(2)}, u32[]{:S(2)}) collective-permute-start(bf16[2048,256]{1,0:T(8,128)(2,1)} %collective-permute-done.12), channel_id=1, source_target_pairs={{0,12},{1,13},{2,14},{3,15},{16,28},{17,29},{18,30},{19,31},{32,44... | collective-permute-start | bytes 3145736 | tf_op jit(solution)/shard_map/ppermute | solution.py:42
  85.5 1.6 collective-permute-start.20
  87.1 2.3 %bitcast_dynamic-update-slice_fusion.5 = bf16[8,2048,256]{2,1,0:T(8,128)(2,1)} fusion(bf16[8,2048,256]{2,1,0:T(8,128)(2,1)} %bitcast_dynamic-update-slice_fusion.6, bf16[2048,256]{1,0:T(8,128)(2,1)} %collective-permute-done.12), kind=kLoop, calls=%fused_computation.6 | loop fusion | bytes 2097152
  90.4 5.3 %collective-permute-done.17 = bf16[2048,256]{1,0:T(8,128)(2,1)S(1)} collective-permute-done((bf16[2048,256]{1,0:T(8,128)(2,1)}, bf16[2048,256]{1,0:T(8,128)(2,1)S(1)}, u32[]{:S(2)}, u32[]{:S(2)}) %collective-permute-start.17) | collective-permute-done | bytes 1048608 | tf_op jit(solution)/shard_map/ppermute | solution.py:38
  96.8 4.9 %multiply_convert_fusion.own_hbm = bf16[2048,1024]{1,0:T(8,128)(2,1)} fusion(bf16[2048,1024]{1,0:T(8,128)(2,1)} %all-gather.2.cloned.1.call-done, f32[2048]{0:T(1024)S(1)} %get-tuple-element.83), kind=kLoop, calls=%fused_computation | loop fusion | flops 6291456 | bytes 8396800 | tf_op jit(solution)/shard_map/convert_element_type | solution.py:266
  103.0 5.9 %weigh.1.refs_0_ = bf16[2048,1024]{1,0:T(8,128)(2,1)} custom-call(s32[4]{0:T(128)} %iota_xor_fusion.blocks_ref, f32[2048,128]{1,0:T(8,128)} %broadcast_in_dim.17.spread_ref.refs_1_, bf16[2048,256]{1,0:T(8,128)(2,1)} %copy-done.1, bf16[2048,256]{1,0:T(8,128)(2,1)} %copy-done.2, bf16[2048,256]{1,0:T(8,128)(2,1)} %copy-done.3), custom_call_target="tpu_custom_call" | custom-call | tf_op jit(solution)/shard_map/weigh/pallas_call | solution.py:63
  108.9 2.3 %bitcast_dynamic-update-slice_fusion.2 = bf16[8,2048,256]{2,1,0:T(8,128)(2,1)} fusion(bf16[8,2048,256]{2,1,0:T(8,128)(2,1)} %bitcast_dynamic-update-slice_fusion.3, bf16[2048,256]{1,0:T(8,128)(2,1)} %collective-permute-done.14), kind=kLoop, calls=%fused_computation.3 | loop fusion | bytes 2097152
  111.2 2.4 %bitcast_dynamic-update-slice_fusion.1 = bf16[8,2048,256]{2,1,0:T(8,128)(2,1)} fusion(bf16[8,2048,256]{2,1,0:T(8,128)(2,1)} %bitcast_dynamic-update-slice_fusion.2, bf16[2048,256]{1,0:T(8,128)(2,1)} %collective-permute-done.2, bf16[2048,256]{1,0:T(8,128)(2,1)} %collective-permute-done.18, pred[]{:T(512)S(6)} %eq.22), kind=kLoop, calls=%fused_computation.2 | loop fusion | flops 524288 | bytes 3145729
  117.5 17.0 %gram_first.1 = (f32[8,256,1024]{2,1,0:T(8,128)}, bf16[2048,1024]{1,0:T(8,128)(2,1)}) custom-call(s32[18]{0:T(128)} %concatenate.9.meta_ref, f32[1]{0:T(128)S(6)} %copy.22.damping_ref, bf16[2048,1024]{1,0:T(8,128)(2,1)} %multiply_convert_fusion.own_hbm, bf16[8,2048,256]{2,1,0:T(8,128)(2,1)} %bitcast_dynamic-update-slice_fusion.shards_hbm, ...), custom_call_target="tpu_custom_call" | custom-call | flops 8589934592 | bytes 20971520 | tf_op jit(solution)/shard_map/gram_first/pallas_call | solution.py:195
  136.8 1.3 collective-permute-done.22
  138.8 14.8 %gram.1 = f32[8,256,1024]{2,1,0:T(8,128)} custom-call(s32[18]{0:T(128)} %concatenate.8.meta_ref, f32[1]{0:T(128)S(6)} %copy.22.damping_ref, bf16[2048,1024]{1,0:T(8,128)(2,1)} %multiply_convert_fusion.own_hbm, bf16[8,2048,256]{2,1,0:T(8,128)(2,1)} %collective-permute-done.21.shards_hbm, ...), custom_call_target="tpu_custom_call", output_to_operand_aliasing={{}: (5, {})} | custom-call | flops 8589934592 | bytes 20971520 | tf_op jit(solution)/shard_map/gram/pallas_call | solution.py:195
  (70 shorter events, 24.0 us)
Async XLA Ops:
  7.2 75.8 %copy-start = (bf16[2048,256]{1,0:T(8,128)(2,1)S(1)}, bf16[2048,256]{1,0:T(8,128)(2,1)}, u32[]{:S(2)}) copy-start(bf16[2048,256]{1,0:T(8,128)(2,1)} %param.9) | copy-start | bytes 3145732
  7.2 89.6 %all-gather.2.cloned.1.call-start = ((), (), s32[]{:S(2)}) async-start(), calls=%async_computation | async-start | bytes 5242880 | tf_op jit(solution)/shard_map/all_gather | solution.py:223
  10.9 5.2 %collective-permute-start = (f32[16,128]{1,0:T(8,128)S(1)}, f32[16,128]{1,0:T(8,128)S(1)}, u32[]{:S(2)}, u32[]{:S(2)}) collective-permute-start(f32[16,128]{1,0:T(8,128)S(1)} %subtract_bitcast_fusion), channel_id=1, source_target_pairs={{0,2},{1,3},{64,66},{65,67},{2,0},{3,1},{66,64},{67,65},{16,18},{1... | collective-permute-start | bytes 24584 | tf_op jit(solution)/shard_map/ppermute | solution.py:38
  16.7 6.8 %collective-permute-start.3 = (f32[16,128]{1,0:T(8,128)S(1)}, f32[16,128]{1,0:T(8,128)S(1)}, u32[]{:S(2)}, u32[]{:S(2)}) collective-permute-start(f32[16,128]{1,0:T(8,128)S(1)} %fusion.8), channel_id=1, source_target_pairs={{0,4},{1,5},{64,68},{65,69},{2,6},{3,7},{66,70},{67,71},{16,20},{1... | collective-permute-start | bytes 24584 | tf_op jit(solution)/shard_map/ppermute | solution.py:38
  17.3 25.4 %collective-permute-start.5 = (bf16[2048,256]{1,0:T(8,128)(2,1)}, bf16[2048,256]{1,0:T(8,128)(2,1)}, u32[]{:S(2)}, u32[]{:S(2)}) collective-permute-start(bf16[2048,256]{1,0:T(8,128)(2,1)} %param.9), channel_id=1, source_target_pairs={{0,12},{1,13},{64,76},{65,77},{2,14},{3,15},{66,78},{67,79},{16,28... | collective-permute-start | bytes 3145736 | tf_op jit(solution)/shard_map/ppermute | solution.py:38
  19.4 23.7 %collective-permute-start.1 = (bf16[2048,256]{1,0:T(8,128)(2,1)}, bf16[2048,256]{1,0:T(8,128)(2,1)S(1)}, u32[]{:S(2)}, u32[]{:S(2)}) collective-permute-start(bf16[2048,256]{1,0:T(8,128)(2,1)} %param.9), channel_id=1, source_target_pairs={{0,64},{1,65},{64,0},{65,1},{2,66},{3,67},{66,2},{67,3},{16,80},{1... | collective-permute-start | bytes 3145736 | tf_op jit(solution)/shard_map/ppermute | solution.py:38
  21.0 24.4 %collective-permute-start.2 = (bf16[2048,256]{1,0:T(8,128)(2,1)}, bf16[2048,256]{1,0:T(8,128)(2,1)}, u32[]{:S(2)}, u32[]{:S(2)}) collective-permute-start(bf16[2048,256]{1,0:T(8,128)(2,1)} %param.9), channel_id=1, source_target_pairs={{0,66},{1,67},{64,2},{65,3},{2,64},{3,65},{66,0},{67,1},{16,82},{1... | collective-permute-start | bytes 3145736 | tf_op jit(solution)/shard_map/ppermute | solution.py:38
  23.5 22.8 %collective-permute-start.4 = (bf16[2048,256]{1,0:T(8,128)(2,1)}, bf16[2048,256]{1,0:T(8,128)(2,1)S(1)}, u32[]{:S(2)}, u32[]{:S(2)}) collective-permute-start(bf16[2048,256]{1,0:T(8,128)(2,1)} %param.9), channel_id=1, source_target_pairs={{0,4},{1,5},{64,68},{65,69},{2,6},{3,7},{66,70},{67,71},{16,20},{1... | collective-permute-start | bytes 3145736 | tf_op jit(solution)/shard_map/ppermute | solution.py:38
  24.1 1.2 collective-permute-start.6
  25.3 3.8 %collective-permute-start.7 = (f32[16,128]{1,0:T(8,128)S(1)}, f32[16,128]{1,0:T(8,128)S(1)}, u32[]{:S(2)}, u32[]{:S(2)}) collective-permute-start(f32[16,128]{1,0:T(8,128)S(1)} %add.95), channel_id=1, source_target_pairs={{0,16},{1,17},{64,80},{65,81},{2,18},{3,19},{66,82},{67,83},{16,0}... | collective-permute-start | bytes 24584 | tf_op jit(solution)/shard_map/ppermute | solution.py:38
  29.1 5.3 %collective-permute-start.8 = (f32[16,128]{1,0:T(8,128)S(1)}, f32[16,128]{1,0:T(8,128)S(1)}, u32[]{:S(2)}, u32[]{:S(2)}) collective-permute-start(f32[16,128]{1,0:T(8,128)S(1)} %add.96), channel_id=1, source_target_pairs={{0,32},{1,33},{64,96},{65,97},{2,34},{3,35},{66,98},{67,99},{16,48... | collective-permute-start | bytes 24584 | tf_op jit(solution)/shard_map/ppermute | solution.py:38
  34.4 8.3 %collective-permute-start.9 = (f32[16,128]{1,0:T(8,128)S(1)}, f32[16,128]{1,0:T(8,128)S(1)}, u32[]{:S(2)}, u32[]{:S(2)}) collective-permute-start(f32[16,128]{1,0:T(8,128)S(1)} %add.97), channel_id=1, source_target_pairs={{0,12},{1,13},{64,76},{65,77},{2,14},{3,15},{66,78},{67,79},{16,28... | collective-permute-start | bytes 24584 | tf_op jit(solution)/shard_map/ppermute | solution.py:38
  43.1 46.2 %copy-start.1 = (bf16[2048,256]{1,0:T(8,128)(2,1)}, bf16[2048,256]{1,0:T(8,128)(2,1)S(1)}, u32[]{:S(2)}) copy-start(bf16[2048,256]{1,0:T(8,128)(2,1)S(1)} %collective-permute-done.1.refs_0_) | copy-start | bytes 3145732
  46.4 38.3 %collective-permute-start.15 = (bf16[2048,256]{1,0:T(8,128)(2,1)S(1)}, bf16[2048,256]{1,0:T(8,128)(2,1)S(1)}, u32[]{:S(2)}, u32[]{:S(2)}) collective-permute-start(bf16[2048,256]{1,0:T(8,128)(2,1)S(1)} %collective-permute-done.1.refs_0_), channel_id=1, source_target_pairs={{0,16},{1,17},{64,80},{65,81},{2,18},{3,19},{66,82},{67,83},{16,0}... | collective-permute-start | bytes 3145736 | tf_op jit(solution)/shard_map/ppermute | solution.py:38
  48.0 36.8 %collective-permute-start.16 = (bf16[2048,256]{1,0:T(8,128)(2,1)S(1)}, bf16[2048,256]{1,0:T(8,128)(2,1)S(1)}, u32[]{:S(2)}, u32[]{:S(2)}) collective-permute-start(bf16[2048,256]{1,0:T(8,128)(2,1)S(1)} %collective-permute-done.1.refs_0_), channel_id=1, source_target_pairs={{0,48},{1,49},{64,112},{65,113},{2,50},{3,51},{66,114},{67,115},{1... | collective-permute-start | bytes 3145736 | tf_op jit(solution)/shard_map/ppermute | solution.py:38
  50.1 21.6 %collective-permute-start.10 = (bf16[2048,256]{1,0:T(8,128)(2,1)}, bf16[2048,256]{1,0:T(8,128)(2,1)}, u32[]{:S(2)}, u32[]{:S(2)}) collective-permute-start(bf16[2048,256]{1,0:T(8,128)(2,1)} %collective-permute-done.5), channel_id=1, source_target_pairs={{0,4},{1,5},{64,68},{65,69},{2,6},{3,7},{66,70},{67,71},{16,20},{1... | collective-permute-start | bytes 3145736 | tf_op jit(solution)/shard_map/ppermute | solution.py:38
  50.7 3.7 %collective-permute-start.11 = (f32[16,128]{1,0:T(8,128)S(1)}, f32[16,128]{1,0:T(8,128)S(1)}, u32[]{:S(2)}, u32[]{:S(2)}) collective-permute-start(f32[16,128]{1,0:T(8,128)S(1)} %add.98), channel_id=1, source_target_pairs={{0,64},{1,65},{64,0},{65,1},{2,66},{3,67},{66,2},{67,3},{16,80},{1... | collective-permute-start | bytes 24584 | tf_op jit(solution)/shard_map/ppermute | solution.py:38
  54.4 21.5 %collective-permute-start.12 = (bf16[2048,256]{1,0:T(8,128)(2,1)S(1)}, bf16[2048,256]{1,0:T(8,128)(2,1)}, u32[]{:S(2)}, u32[]{:S(2)}) collective-permute-start(bf16[2048,256]{1,0:T(8,128)(2,1)S(1)} %get-tuple-element.49), channel_id=1, source_target_pairs={{0,66},{1,67},{64,2},{65,3},{2,64},{3,65},{66,0},{67,1},{16,82},{1... | collective-permute-start | bytes 3145736 | tf_op jit(solution)/shard_map/ppermute | solution.py:38
  56.0 20.2 %collective-permute-start.13 = (bf16[2048,256]{1,0:T(8,128)(2,1)S(1)}, bf16[2048,256]{1,0:T(8,128)(2,1)S(1)}, u32[]{:S(2)}, u32[]{:S(2)}) collective-permute-start(bf16[2048,256]{1,0:T(8,128)(2,1)S(1)} %get-tuple-element.50), channel_id=1, source_target_pairs={{0,64},{1,65},{64,0},{65,1},{2,66},{3,67},{66,2},{67,3},{16,80},{1... | collective-permute-start | bytes 3145736 | tf_op jit(solution)/shard_map/ppermute | solution.py:38
  76.2 19.5 %collective-permute-start.17 = (bf16[2048,256]{1,0:T(8,128)(2,1)}, bf16[2048,256]{1,0:T(8,128)(2,1)S(1)}, u32[]{:S(2)}, u32[]{:S(2)}) collective-permute-start(bf16[2048,256]{1,0:T(8,128)(2,1)} %collective-permute-done.12), channel_id=1, source_target_pairs={{0,4},{1,5},{64,68},{65,69},{2,6},{3,7},{66,70},{67,71},{16,20},{1... | collective-permute-start | bytes 3145736 | tf_op jit(solution)/shard_map/ppermute | solution.py:38
  77.6 33.6 %collective-permute-start.18 = (bf16[2048,256]{1,0:T(8,128)(2,1)}, bf16[2048,256]{1,0:T(8,128)(2,1)}, u32[]{:S(2)}, u32[]{:S(2)}) collective-permute-start(bf16[2048,256]{1,0:T(8,128)(2,1)} %collective-permute-done.12), channel_id=1, source_target_pairs={{0,12},{1,13},{2,14},{3,15},{16,28},{17,29},{18,30},{19,31},{32,44... | collective-permute-start | bytes 3145736 | tf_op jit(solution)/shard_map/ppermute | solution.py:42
  81.7 27.2 %collective-permute-start.14 = (bf16[2048,256]{1,0:T(8,128)(2,1)}, bf16[2048,256]{1,0:T(8,128)(2,1)}, u32[]{:S(2)}, u32[]{:S(2)}) collective-permute-start(bf16[2048,256]{1,0:T(8,128)(2,1)} %broadcast_select_fusion), channel_id=1, source_target_pairs={{0,64},{1,65},{64,2},{65,3},{2,66},{3,67},{66,0},{67,1},{16,80},{1... | collective-permute-start | bytes 3145736 | tf_op jit(solution)/shard_map/ppermute | solution.py:42
  84.8 11.0 %copy-start.3 = (bf16[2048,256]{1,0:T(8,128)(2,1)}, bf16[2048,256]{1,0:T(8,128)(2,1)S(1)}, u32[]{:S(2)}) copy-start(bf16[2048,256]{1,0:T(8,128)(2,1)S(1)} %collective-permute-done.16.refs_2_) | copy-start | bytes 3145732
  84.8 28.9 %collective-permute-start.19 = (bf16[2048,256]{1,0:T(8,128)(2,1)}, bf16[2048,256]{1,0:T(8,128)(2,1)S(1)}, u32[]{:S(2)}, u32[]{:S(2)}) collective-permute-start(bf16[2048,256]{1,0:T(8,128)(2,1)} %collective-permute-done.10), channel_id=1, source_target_pairs={{64,66},{65,67},{66,64},{67,65},{80,82},{81,83},{82,80},{83,81},{9... | collective-permute-start | bytes 3145736 | tf_op jit(solution)/shard_map/ppermute | solution.py:42
  85.5 29.4 %collective-permute-start.20 = (bf16[2048,256]{1,0:T(8,128)(2,1)S(1)}, bf16[2048,256]{1,0:T(8,128)(2,1)}, u32[]{:S(2)}, u32[]{:S(2)}) collective-permute-start(bf16[2048,256]{1,0:T(8,128)(2,1)S(1)} %collective-permute-done.1.refs_0_), channel_id=1, source_target_pairs={{0,32},{1,33},{64,96},{65,97},{2,34},{3,35},{66,98},{67,99},{16,48... | collective-permute-start | bytes 3145736 | tf_op jit(solution)/shard_map/ppermute | solution.py:38
  103.0 11.9 %copy-start.4 = (s32[4]{0:T(128)S(1)}, s32[4]{0:T(128)}, u32[]{:S(2)}) copy-start(s32[4]{0:T(128)} %iota_xor_fusion.blocks_ref) | copy-start | bytes 52
  103.0 13.2 %copy-start.5 = (s32[4]{0:T(128)S(1)}, s32[4]{0:T(128)}, u32[]{:S(2)}) copy-start(s32[4]{0:T(128)} %constant.79.clone) | copy-start | bytes 52
  103.0 13.2 %copy-start.6 = (s32[4]{0:T(128)S(1)}, s32[4]{0:T(128)}, u32[]{:S(2)}) copy-start(s32[4]{0:T(128)} %constant.80.clone) | copy-start | bytes 52
  103.0 13.2 %copy-start.7 = (s32[4]{0:T(128)S(1)}, s32[4]{0:T(128)}, u32[]{:S(2)}) copy-start(s32[4]{0:T(128)} %constant.81.clone) | copy-start | bytes 52
  103.0 13.2 %copy-start.8 = (s32[4]{0:T(128)S(1)}, s32[4]{0:T(128)}, u32[]{:S(2)}) copy-start(s32[4]{0:T(128)} %constant.82.clone) | copy-start | bytes 52
  114.9 23.9 %collective-permute-start.21 = (bf16[8,2048,256]{2,1,0:T(8,128)(2,1)}, bf16[8,2048,256]{2,1,0:T(8,128)(2,1)}, u32[]{:S(2)}, u32[]{:S(2)}) collective-permute-start(bf16[8,2048,256]{2,1,0:T(8,128)(2,1)} %bitcast_dynamic-update-slice_fusion.shards_hbm), channel_id=1, source_target_pairs={{0,1},{1,0},{64,65},{65,64},{2,3},{3,2},{66,67},{67,66},{16,17},{1... | collective-permute-start | bytes 25165832 | tf_op jit(solution)/shard_map/ppermute | solution.py:38
  134.5 3.6 %collective-permute-start.22 = (f32[256]{0:T(256)S(1)}, f32[256]{0:T(256)S(1)}, u32[]{:S(2)}, u32[]{:S(2)}) collective-permute-start(f32[256]{0:T(256)S(1)} %bitcast.57), channel_id=1, source_target_pairs={{0,64},{1,65},{64,0},{65,1},{2,66},{3,67},{66,2},{67,3},{16,80},{1... | collective-permute-start | bytes 3080 | tf_op jit(solution)/shard_map/ppermute | solution.py:38
  (1 other events, 5.8 us)
Sparse Core Ops, SparseCore 0:
  9.7 70.4 all-gather.1

commit v3 on v2

--- a/solution.py
+++ b/solution.py
@@ -78,9 +78,13 @@
 N_TILES = 4
 TILE_AT, DIAGONAL_AT, OWN_AT, OTHER_AT, ROW_AT, BLOCK_AT = 0, 4, 8, 12, 16, 17
 FIRST_NEEDS, LATER_NEEDS = (1, 3), ((2, 6), (7, 5), (4,))
-
-
-def gram_kernel(meta_ref, damping_ref, own_hbm, shards_hbm, *refs, samples, fresh):
+N_CHUNKS = 4
+AHEAD = 8
+
+
+def gram_kernel(meta_ref, damping_ref, own_hbm, stack_hbm, *refs, samples, fresh):
+    shards_hbm = [stack_hbm.at[n] for n in range(4)] + list(refs[:4])
+    refs = refs[4:]
     if fresh:
         before_hbm, spread_hbm, column_hbm = refs[:3]
         out_ref, other_hbm, weighted, slots, weighted_sems, slot_sems, column, spread, column_sems = refs[3:]
@@ -90,61 +94,81 @@
     step = pl.program_id(0)
     contract = (((0,), (0,)), ((), ()))
     scale = 1.0 / samples
+    chunk = weighted.shape[1] // N_CHUNKS
 
     def slot_copy(n):
-        return pltpu.make_async_copy(shards_hbm.at[n], slots.at[n], slot_sems.at[n])
+        return pltpu.make_async_copy(shards_hbm[n], slots.at[n], slot_sems.at[n])
 
     def product(n, at):
         return lax.dot_general(
             slots[meta_ref[at + step]], weighted[n], contract, preferred_element_type=jnp.float32)
 
-    own_copy = pltpu.make_async_copy(own_hbm, weighted.at[0], weighted_sems.at[0])
-    other_copy = pltpu.make_async_copy(before_hbm, weighted.at[1], weighted_sems.at[1])
+    def rows_at(j):
+        return pl.ds(j * chunk, chunk)
+
+    def weighted_copy(n, j):
+        source = (own_hbm, before_hbm)[n]
+        return pltpu.make_async_copy(source.at[rows_at(j)], weighted.at[n, rows_at(j)], weighted_sems.at[n, j])
+
+    def part(n, at, j):
+        return lax.dot_general(
+            slots[meta_ref[at], rows_at(j)], weighted[n, rows_at(j)], contract, preferred_element_type=jnp.float32)
+
     if fresh:
         column_copies = (
             pltpu.make_async_copy(column_hbm, column, column_sems.at[0]),
             pltpu.make_async_copy(spread_hbm, spread, column_sems.at[1]))
-        hand_on = pltpu.make_async_copy(weighted.at[1], other_hbm, weighted_sems.at[1])
-
-    def scale_column():
-        rows, width = column.shape
-        lanes = spread.shape[1]
-        chunk = 512
-
-        @pl.loop(0, rows // chunk)
-        def _(i):
-            at_rows = pl.ds(pl.multiple_of(i * chunk, chunk), chunk)
-            weight = spread[at_rows, :]
-            for part in range(0, width, lanes):
-                scaled = column[at_rows, part:part + lanes].astype(jnp.float32) * weight
-                at = pl.multiple_of(meta_ref[BLOCK_AT] * width + part, lanes)
-                weighted[1, at_rows, pl.ds(at, lanes)] = scaled.astype(jnp.bfloat16)
+        hand_on = pltpu.make_async_copy(weighted.at[1], other_hbm, column_sems.at[2])
+
+    def scale_column(j):
+        width, lanes = column.shape[1], spread.shape[1]
+        weight = spread[rows_at(j), :]
+        for first in range(0, width, lanes):
+            scaled = column[rows_at(j), first:first + lanes].astype(jnp.float32) * weight
+            at = pl.multiple_of(meta_ref[BLOCK_AT] * width + first, lanes)
+            weighted[1, rows_at(j), pl.ds(at, lanes)] = scaled.astype(jnp.bfloat16)
 
     @pl.when(step == 0)
     def _():
-        own_copy.start()
-        slot_copy(0).start()
+        queue = [slot_copy(0)] + [weighted_copy(0, j) for j in range(N_CHUNKS)]
+        queue += [slot_copy(n) for n in FIRST_NEEDS]
         if fresh:
-            for copy in column_copies:
-                copy.start()
-        other_copy.start()
-        for n in FIRST_NEEDS:
-            slot_copy(n).start()
-        own_copy.wait()
-        slot_copy(0).wait()
-        out_ref[0] = product(0, OWN_AT)
-        other_copy.wait()
+            queue += column_copies
+        queue += [weighted_copy(1, j) for j in range(N_CHUNKS)]
+        later = [slot_copy(n) for needed in LATER_NEEDS for n in needed]
+        todo = queue + later
+        for copy in todo[:AHEAD]:
+            copy.start()
+        waited = 0
+
+        def wait(count):
+            nonlocal waited
+            for n in range(waited, waited + count):
+                todo[n].wait()
+                if n + AHEAD < len(todo):
+                    todo[n + AHEAD].start()
+            waited += count
+
+        wait(1)
+        for j in range(N_CHUNKS):
+            wait(1)
+            if j == 0:
+                out_ref[0] = part(0, OWN_AT, j)
+            else:
+                out_ref[0] += part(0, OWN_AT, j)
+        wait(len(FIRST_NEEDS) + (len(column_copies) if fresh else 0))
+        for j in range(N_CHUNKS):
+            wait(1)
+            if fresh:
+                scale_column(j)
+            if j < N_CHUNKS - 1:
+                out_ref[0] += part(1, OTHER_AT, j)
+            else:
+                out_ref[0] = (out_ref[0] + part(1, OTHER_AT, j)) * scale
+        for copy in todo[waited + AHEAD:]:
+            copy.start()
         if fresh:
-            for copy in column_copies:
-                copy.wait()
-            scale_column()
             hand_on.start()
-        for n in FIRST_NEEDS:
-            slot_copy(n).wait()
-        for needed in LATER_NEEDS:
-            for n in needed:
-                slot_copy(n).start()
-        out_ref[0] = (out_ref[0] + product(1, OTHER_AT)) * scale
 
     for at, needed in enumerate(LATER_NEEDS):
         @pl.when(step == at + 1)
@@ -171,24 +195,24 @@
 
 
 def gram_blocks(meta, damping, own, other, shards, samples, spread=None, column=None, into=None):
-    _, rows, height = shards.shape
+    rows, height = shards[1].shape
     width = own.shape[1]
     fresh = into is None
     hbm = pl.BlockSpec(memory_space=pl.ANY)
-    arrays = [meta, damping, own, shards] + ([other, spread, column] if fresh else [other, into])
+    arrays = [meta, damping, own, *shards] + ([other, spread, column] if fresh else [other, into])
     result = jax.ShapeDtypeStruct((2 * N_TILES, height, width), jnp.float32)
     block = pl.BlockSpec((1, height, width), lambda i, meta: (meta[i], 0, 0))
     scratch = [
         pltpu.VMEM((2, rows, width), jnp.bfloat16),
         pltpu.VMEM((8, rows, height), jnp.bfloat16),
-        pltpu.SemaphoreType.DMA((2,)),
+        pltpu.SemaphoreType.DMA((2, N_CHUNKS)),
         pltpu.SemaphoreType.DMA((8,)),
     ]
     if fresh:
         scratch += [
             pltpu.VMEM((rows, height), jnp.bfloat16),
             pltpu.VMEM(spread.shape, jnp.float32),
-            pltpu.SemaphoreType.DMA((2,)),
+            pltpu.SemaphoreType.DMA((3,)),
         ]
     flops = N_TILES * 2 * 2 * rows * height * width
     moved = 8 * rows * height * 2 + N_TILES * height * width * 4 + 4 * rows * width
@@ -220,9 +244,6 @@
     def pick(if_native, if_far):
         return jnp.where(native, if_native, if_far)
 
-    columns = lax.all_gather(design, "trow", axis=1, tiled=True)
-
-    from_xo = move(design, x=3)
     first = (row == 0) & (col == 0)
     share = jnp.where(first, targets, 0.0) - jnp.dot(design, coeffs, preferred_element_type=jnp.float32)
     share = share.reshape(rows // 128, 128)
@@ -230,50 +251,51 @@
     design_z, share = tie((design, share))
     from_zp = move(design_z, z=1)
     from_zo = move(design_z, z=3)
-    share = share + move(share, x=1)
+    share = (share + move(share, x=1)) + (move(share, x=3) + move(share, x=2))
     design_x, share = tie((design, share))
+    from_xo = move(design_x, x=3)
     from_xp = move(design_x, x=1)
-    for where in ({"core": 1}, {"y": 1}, {"y": 2}, {"x": 3}):
+    for where in ({"core": 1}, {"y": 1}, {"y": 2}):
         share = share + move(share, **where)
+    design_y, share = tie((design, share))
+    own_y1 = move(design_y, y=1)
+    own_y3 = move(design_y, y=3)
     from_zp, from_zo, from_xp, from_xo, share = tie((from_zp, from_zo, from_xp, from_xo, share))
 
     second_xp = move(from_xo, x=1)
-    by_zo, by_zp, share_other = tie((pick(from_xo, from_zp), pick(from_xo, from_xp), move(share, z=1)))
+    by_zo, by_zp, shares = tie(
+        (pick(from_xo, from_zp), pick(from_xo, from_xp), jnp.stack([share, move(share, z=1)])))
     second_zo = move(by_zo, z=3)
     second_zp = move(by_zp, z=1)
-    other_y1 = move(from_zp, y=1)
-    other_y3 = move(from_zp, y=3)
+    by_y1, own_y1 = tie((from_zp, own_y1))
+    other_y1 = move(by_y1, y=1)
+    by_y3, own_y3 = tie((from_zp, own_y3))
+    other_y3 = move(by_y3, y=3)
     second_xp, from_xp = tie((second_xp, from_xp))
     by_z = pick(second_xp, from_xp)
-    second_xp, second_zo, second_zp, by_z, share, from_zp_y = tie((second_xp, second_zo, second_zp, by_z, share, from_zp))
+    second_xp, second_zo, second_zp, by_z, shares = tie((second_xp, second_zo, second_zp, by_z, shares))
 
     third_xp = move(second_zo, x=1)
     third_xo = move_by_role(second_zo, native=(3, 0, 0, 0))
     third_z = move_by_role(by_z, native=(0, 0, 1, 0), far=(0, 0, 3, 0))
-    by_z2, from_zp_y, other_y1, other_y3 = tie((second_xp, from_zp_y, other_y1, other_y3))
-    third_z2 = move_by_role(by_z2, far=(0, 0, 2, 0))
-    other_y2 = move(from_zp_y, y=2)
+    third_z2 = move_by_role(second_xp, far=(0, 0, 2, 0))
+    by_y1, other_y1 = tie((own_y3, other_y1))
+    own_y2 = move(by_y1, y=1)
+    by_y3, other_y3 = tie((other_y1, other_y3))
+    other_y2 = move(by_y3, y=3)
 
     cutoff = threshold[0]
-    residual, residual_other = share.reshape(rows), share_other.reshape(rows)
+    residual, residual_other = shares[0].reshape(rows), shares[1].reshape(rows)
     weight = cutoff / jnp.maximum(jnp.abs(residual), cutoff)
     weight_other = cutoff / jnp.maximum(jnp.abs(residual_other), cutoff)
     influence = weight * residual
     local_grad = jnp.dot(influence, design.astype(jnp.float32), precision=lax.Precision.HIGHEST)
+    spread_own = jnp.broadcast_to(weight[:, None], (rows, 128))
     spread = jnp.broadcast_to(weight_other[:, None], (rows, 128))
     blocks = row ^ jnp.arange(N_Y, dtype=jnp.int32)
-    columns, other_y1, other_y3 = tie((columns, other_y1, other_y3))
-    own_weighted = (columns.astype(jnp.float32) * weight[:, None]).astype(jnp.bfloat16)
+    third_z, other_y1, other_y3 = tie((third_z, other_y1, other_y3))
     other_weighted = weigh(blocks, spread, [from_zp, other_y1, other_y3], (0, 1, 3))
-    third_z, own_weighted, other_weighted, spread, local_grad = tie(
-        (third_z, own_weighted, other_weighted, spread, local_grad))
-    here = jnp.stack([
-        pick(design, from_xo), pick(from_zp, second_xp), second_zo, second_zp,
-        third_xp, third_z, pick(from_zo, third_xo), pick(from_xp, third_z2)])
-    here, other_y2 = tie((here, other_y2))
-
-    sibling = move(here, core=1)
-
+    own_weighted = weigh(blocks, spread_own, [design, own_y1, own_y2, own_y3], (0, 1, 2, 3))
     column_a = pick(x, x ^ 3)
     column_b = column_a ^ 1
     own_slots = pick(jnp.array([0, 2, 7, 4]), jnp.array([0, 6, 1, 7]))
@@ -285,13 +307,19 @@
         diagonal = tiles + 8 * slab == col
         return jnp.concatenate([tiles, diagonal, own_slots, other_slots, row[None], blocks[2:3]]).astype(jnp.int32)
 
+    stack = jnp.stack([pick(design, from_xo), pick(from_zp, second_xp), second_zo, second_zp])
+    third_z, own_weighted, other_weighted, spread, local_grad, stack, meta, meta_sibling = tie(
+        (third_z, own_weighted, other_weighted, spread, local_grad, stack, describe(core), describe(1 - core)))
+    gradient = -(local_grad + move(local_grad, z=1)) / samples
+    here = [stack, third_xp, third_z, pick(from_zo, third_xo), pick(from_xp, third_z2)]
+    *here, other_y2, gradient = tie((*here, other_y2, gradient))
+
+    sibling = [move(shard, core=1) for shard in here]
     result, other_weighted = gram_blocks(
-        describe(core), damping, own_weighted, other_weighted, here, samples, spread=spread, column=other_y2)
-    result, local_grad = tie((result, local_grad))
-    gradient = -(local_grad + move(local_grad, z=1)) / samples
+        meta, damping, own_weighted, other_weighted, here, samples, spread=spread, column=other_y2)
     result = gram_blocks(
-        describe(1 - core), damping, own_weighted, other_weighted, sibling, samples, into=result)
-    hessian = result.reshape(2 * N_TILES, 1, width, columns.shape[1])
+        meta_sibling, damping, own_weighted, other_weighted, sibling, samples, into=result)
+    hessian = result.reshape(2 * N_TILES, 1, width, N_Y * width)
     return (hessian, gradient)
 
 

time: 161 us -> 152 us (0.944)
  starting transfers between devices: 31.8 us -> 51.4 us
  waiting for transfers between devices: 42.8 us -> 28.5 us
  between operations: 15.5 us -> 2.4 us
  other arithmetic: 18.7 us -> 13.8 us
  Pallas kernels: 37.7 us -> 41.1 us
    ppermute x20 -> x28, waiting for transfers between devices: 42.1 us -> 25.5 us  [move(): return lax.ppermute(value, AXES, pairs(lambda cx, cz: (x, y, z, core)))]
    ppermute x20 -> x28, starting transfers between devices: 26.9 us -> 42.4 us  [move(): return lax.ppermute(value, AXES, pairs(lambda cx, cz: (x, y, z, core)))]
    unnamed x3 -> x0, other arithmetic: 6.18 us -> none
    pallas_call x1 -> x2, Pallas kernels: 5.88 us -> 11.8 us  [weigh(): pl.pallas_call(functools.partial(weigh_kernel, places=places), out_shape=...]
    another operation x1 -> x3, other arithmetic: 1.21 us -> 6.91 us  [local(): jnp.stack([pick(design, from_xo), pick(from_zp, second_xp), second_zo, se...]
    convert_element_type x1 -> x0, other arithmetic: 4.9 us -> none  [local(): (columns.astype(jnp.float32) * weight[:, None]).astype(jnp.bfloat16)]
    ppermute x3, starting transfers between devices: 4.83 us -> 9.01 us  [move_by_role(): lax.ppermute(value, AXES, pairs(lambda cx, cz: native if is_native(cx, cz...]
    ppermute x3, waiting for transfers between devices: 0.01 us -> 2.91 us  [move_by_role(): lax.ppermute(value, AXES, pairs(lambda cx, cz: native if is_native(cx, cz...]
  transfers between devices with their start and end apart: 24 -> 31, of which waited for: 16 -> 13; matrix products, arithmetic and copies ran while one was open for 20% -> 12% of each run, Pallas kernels for 14% -> 18%
where the time goes in v3:
time: 152 us; the launch traced here: 150 us
  starting transfers between devices  51.4 us (34%)
  Pallas kernels  41.1 us (27%)
  waiting for transfers between devices  28.5 us (19%)
  other arithmetic  13.8 us (9%)
  local copies, waits for them, and re-layouts  11 us (7%)
  between operations  2.4 us (2%)
  matrix products  2.16 us (1%)
    ppermute x28, starting transfers between devices, move(): return lax.ppermute(value, AXES, pairs(lambda cx, cz: (x, y, z, core)))  42.4 us
    pallas_call x2, Pallas kernels, gram_blocks(): pl.pallas_call(functools.partial(gram_kernel, samples=samples, fresh=fres...  29.3 us
    ppermute x28, waiting for transfers between devices, move(): return lax.ppermute(value, AXES, pairs(lambda cx, cz: (x, y, z, core)))  25.5 us
    pallas_call x2, Pallas kernels, weigh(): pl.pallas_call(functools.partial(weigh_kernel, places=places), out_shape=...  11.8 us
    ppermute x3, starting transfers between devices, move_by_role(): lax.ppermute(value, AXES, pairs(lambda cx, cz: native if is_native(cx, cz...  9.01 us
    another operation x3, other arithmetic, local(): jnp.stack([pick(design, from_xo), pick(from_zp, second_xp), second_zo, se...  6.91 us
    unnamed x31, local copies, waits for them, and re-layouts  5.22 us
    select_n x4, other arithmetic, pick(): return jnp.where(native, if_native, if_far)  4.74 us
  transfers between devices with their start and end apart: 31, of which 13 were waited for; matrix products, arithmetic and copies ran while one was open for 12% of the time, Pallas kernels for 18%

profile of v3, /device:TPU:0, one launch (start us, length us, event | category | flops | bytes accessed | tf_op | source)
XLA Modules:
  0.0 150.3 jit_solution(3449875166440622737)
XLA Ops:
  1.3 1.6 %fusion.3 = f32[1,2048]{1,0:T(1,128)S(1)} fusion(bf16[2048,256]{1,0:T(8,128)(2,1)} %refs_0_.1, bf16[256,1]{0,1:T(2,128)(2,1)S(1)} %reshape.31), kind=kOutput, calls=%fused_computation.24 | convolution fusion | flops 1048576 | bytes 1057280 | tf_op jit(solution)/shard_map/dot_general | solution.py:248
  3.7 3.3 %collective-permute-start = (f32[16,128]{1,0:T(8,128)S(1)}, f32[16,128]{1,0:T(8,128)S(1)}, u32[]{:S(2)}, u32[]{:S(2)}) collective-permute-start(f32[16,128]{1,0:T(8,128)S(1)} %subtract_bitcast_fusion), channel_id=1, source_target_pairs={{0,2},{1,3},{64,66},{65,67},{2,0},{3,1},{66,64},{67,65},{16,18},{1... | collective-permute-start | bytes 24584 | tf_op jit(solution)/shard_map/ppermute | solution.py:38
  7.0 1.8 %collective-permute-done = f32[16,128]{1,0:T(8,128)S(1)} collective-permute-done((f32[16,128]{1,0:T(8,128)S(1)}, f32[16,128]{1,0:T(8,128)S(1)}, u32[]{:S(2)}, u32[]{:S(2)}) %collective-permute-start) | collective-permute-done | bytes 8224 | tf_op jit(solution)/shard_map/ppermute | solution.py:38
  10.1 2.1 %collective-permute-start.4 = (f32[16,128]{1,0:T(8,128)S(1)}, f32[16,128]{1,0:T(8,128)S(1)}, u32[]{:S(2)}, u32[]{:S(2)}) collective-permute-start(f32[16,128]{1,0:T(8,128)S(1)} %fusion.9), channel_id=1, source_target_pairs={{0,12},{1,13},{64,76},{65,77},{2,14},{3,15},{66,78},{67,79},{16,28... | collective-permute-start | bytes 24584 | tf_op jit(solution)/shard_map/ppermute | solution.py:38
  13.6 2.0 %collective-permute-start.1 = (bf16[2048,256]{1,0:T(8,128)(2,1)}, bf16[2048,256]{1,0:T(8,128)(2,1)S(1)}, u32[]{:S(2)}, u32[]{:S(2)}) collective-permute-start(bf16[2048,256]{1,0:T(8,128)(2,1)} %refs_0_.1), channel_id=1, source_target_pairs={{0,64},{1,65},{64,0},{65,1},{2,66},{3,67},{66,2},{67,3},{16,80},{1... | collective-permute-start | bytes 3145736 | tf_op jit(solution)/shard_map/ppermute | solution.py:38
  18.4 2.1 %collective-permute-start.7 = (bf16[2048,256]{1,0:T(8,128)(2,1)}, bf16[2048,256]{1,0:T(8,128)(2,1)}, u32[]{:S(2)}, u32[]{:S(2)}) collective-permute-start(bf16[2048,256]{1,0:T(8,128)(2,1)} %refs_0_.1), channel_id=1, source_target_pairs={{0,12},{1,13},{64,76},{65,77},{2,14},{3,15},{66,78},{67,79},{16,28... | collective-permute-start | bytes 3145736 | tf_op jit(solution)/shard_map/ppermute | solution.py:38
  21.7 1.6 %collective-permute-start.9 = (f32[16,128]{1,0:T(8,128)S(1)}, f32[16,128]{1,0:T(8,128)S(1)}, u32[]{:S(2)}, u32[]{:S(2)}) collective-permute-start(f32[16,128]{1,0:T(8,128)S(1)} %add.88), channel_id=1, source_target_pairs={{0,16},{1,17},{64,80},{65,81},{2,18},{3,19},{66,82},{67,83},{16,0}... | collective-permute-start | bytes 24584 | tf_op jit(solution)/shard_map/ppermute | solution.py:38
  23.3 2.1 %collective-permute-done.9 = f32[16,128]{1,0:T(8,128)S(1)} collective-permute-done((f32[16,128]{1,0:T(8,128)S(1)}, f32[16,128]{1,0:T(8,128)S(1)}, u32[]{:S(2)}, u32[]{:S(2)}) %collective-permute-start.9) | collective-permute-done | bytes 8224 | tf_op jit(solution)/shard_map/ppermute | solution.py:38
  25.3 3.2 %collective-permute-start.10 = (f32[16,128]{1,0:T(8,128)S(1)}, f32[16,128]{1,0:T(8,128)S(1)}, u32[]{:S(2)}, u32[]{:S(2)}) collective-permute-start(f32[16,128]{1,0:T(8,128)S(1)} %add.89), channel_id=1, source_target_pairs={{0,32},{1,33},{64,96},{65,97},{2,34},{3,35},{66,98},{67,99},{16,48... | collective-permute-start | bytes 24584 | tf_op jit(solution)/shard_map/ppermute | solution.py:38
  28.5 2.0 %collective-permute-done.10 = f32[16,128]{1,0:T(8,128)S(1)} collective-permute-done((f32[16,128]{1,0:T(8,128)S(1)}, f32[16,128]{1,0:T(8,128)S(1)}, u32[]{:S(2)}, u32[]{:S(2)}) %collective-permute-start.10) | collective-permute-done | bytes 8224 | tf_op jit(solution)/shard_map/ppermute | solution.py:38
  30.5 1.6 %collective-permute-start.17 = (bf16[2048,256]{1,0:T(8,128)(2,1)}, bf16[2048,256]{1,0:T(8,128)(2,1)}, u32[]{:S(2)}, u32[]{:S(2)}) collective-permute-start(bf16[2048,256]{1,0:T(8,128)(2,1)} %refs_0_.1), channel_id=1, source_target_pairs={{0,16},{1,17},{64,80},{65,81},{2,18},{3,19},{66,82},{67,83},{16,0}... | collective-permute-start | bytes 3145736 | tf_op jit(solution)/shard_map/ppermute | solution.py:38
  32.1 4.5 %collective-permute-done.1.refs_0_ = bf16[2048,256]{1,0:T(8,128)(2,1)S(1)} collective-permute-done((bf16[2048,256]{1,0:T(8,128)(2,1)}, bf16[2048,256]{1,0:T(8,128)(2,1)S(1)}, u32[]{:S(2)}, u32[]{:S(2)}) %collective-permute-start.1) | collective-permute-done | bytes 1048608 | tf_op jit(solution)/shard_map/ppermute | solution.py:38
  36.5 3.0 %collective-permute-start.16 = (bf16[2048,256]{1,0:T(8,128)(2,1)}, bf16[2048,256]{1,0:T(8,128)(2,1)}, u32[]{:S(2)}, u32[]{:S(2)}) collective-permute-start(bf16[2048,256]{1,0:T(8,128)(2,1)} %refs_0_.1), channel_id=1, source_target_pairs={{0,48},{1,49},{64,112},{65,113},{2,50},{3,51},{66,114},{67,115},{1... | collective-permute-start | bytes 3145736 | tf_op jit(solution)/shard_map/ppermute | solution.py:38
  39.9 2.1 %collective-permute-done.7 = bf16[2048,256]{1,0:T(8,128)(2,1)} collective-permute-done((bf16[2048,256]{1,0:T(8,128)(2,1)}, bf16[2048,256]{1,0:T(8,128)(2,1)}, u32[]{:S(2)}, u32[]{:S(2)}) %collective-permute-start.7) | collective-permute-done | bytes 1048608 | tf_op jit(solution)/shard_map/ppermute | solution.py:38
  43.1 3.3 %select_bitcast_fusion.1 = (bf16[1,2048,256]{2,1,0:T(8,128)(2,1)}, bf16[2048,256]{1,0:T(8,128)(2,1)}, bf16[2048,256]{1,0:T(8,128)(2,1)}) fusion(bf16[2048,256]{1,0:T(8,128)(2,1)} %refs_0_.1, bf16[2048,256]{1,0:T(8,128)(2,1)} %collective-permute-done.7, pred[]{:T(512)S(6)} %eq.24, bf16[2048,256]{1,0:T(8,128)(2,1)S(1)} %collective-permute-done.6, ...), kind=kLoop, calls=%fused_computation.2 | loop fusion | flops 1572864 | bytes 7340033 | tf_op jit(solution)/shard_map/stack | solution.py:310
  46.4 2.5 %collective-permute-start.13 = (bf16[2048,256]{1,0:T(8,128)(2,1)}, bf16[2048,256]{1,0:T(8,128)(2,1)}, u32[]{:S(2)}, u32[]{:S(2)}) collective-permute-start(bf16[2048,256]{1,0:T(8,128)(2,1)} %get-tuple-element.61), channel_id=1, source_target_pairs={{0,66},{1,67},{64,2},{65,3},{2,64},{3,65},{66,0},{67,1},{16,82},{1... | collective-permute-start | bytes 3145736 | tf_op jit(solution)/shard_map/ppermute | solution.py:38
  54.5 1.7 %collective-permute-start.18 = (bf16[2048,256]{1,0:T(8,128)(2,1)S(1)}, bf16[2048,256]{1,0:T(8,128)(2,1)}, u32[]{:S(2)}, u32[]{:S(2)}) collective-permute-start(bf16[2048,256]{1,0:T(8,128)(2,1)S(1)} %collective-permute-done.1.refs_0_), channel_id=1, source_target_pairs={{0,16},{1,17},{64,80},{65,81},{2,18},{3,19},{66,82},{67,83},{16,0}... | collective-permute-start | bytes 3145736 | tf_op jit(solution)/shard_map/ppermute | solution.py:38
  56.1 4.7 %collective-permute-done.16.refs_3_ = bf16[2048,256]{1,0:T(8,128)(2,1)} collective-permute-done((bf16[2048,256]{1,0:T(8,128)(2,1)}, bf16[2048,256]{1,0:T(8,128)(2,1)}, u32[]{:S(2)}, u32[]{:S(2)}) %collective-permute-start.16) | collective-permute-done | bytes 1048608 | tf_op jit(solution)/shard_map/ppermute | solution.py:38
  60.8 3.0 %collective-permute-start.19 = (bf16[2048,256]{1,0:T(8,128)(2,1)S(1)}, bf16[2048,256]{1,0:T(8,128)(2,1)S(1)}, u32[]{:S(2)}, u32[]{:S(2)}) collective-permute-start(bf16[2048,256]{1,0:T(8,128)(2,1)S(1)} %collective-permute-done.1.refs_0_), channel_id=1, source_target_pairs={{0,48},{1,49},{64,112},{65,113},{2,50},{3,51},{66,114},{67,115},{1... | collective-permute-start | bytes 3145736 | tf_op jit(solution)/shard_map/ppermute | solution.py:38
  65.1 4.9 %collective-permute-done.13 = bf16[2048,256]{1,0:T(8,128)(2,1)} collective-permute-done((bf16[2048,256]{1,0:T(8,128)(2,1)}, bf16[2048,256]{1,0:T(8,128)(2,1)}, u32[]{:S(2)}, u32[]{:S(2)}) %collective-permute-start.13) | collective-permute-done | bytes 1048608 | tf_op jit(solution)/shard_map/ppermute | solution.py:38
  71.0 2.5 %collective-permute-start.15 = (bf16[2048,256]{1,0:T(8,128)(2,1)S(1)}, bf16[2048,256]{1,0:T(8,128)(2,1)S(1)}, u32[]{:S(2)}, u32[]{:S(2)}) collective-permute-start(bf16[2048,256]{1,0:T(8,128)(2,1)S(1)} %broadcast_select_fusion.2), channel_id=1, source_target_pairs={{0,64},{1,65},{64,2},{65,3},{2,66},{3,67},{66,0},{67,1},{16,80},{1... | collective-permute-start | bytes 3145736 | tf_op jit(solution)/shard_map/ppermute | solution.py:42
  73.5 1.7 %collective-permute-start.23 = (bf16[2048,256]{1,0:T(8,128)(2,1)}, bf16[2048,256]{1,0:T(8,128)(2,1)}, u32[]{:S(2)}, u32[]{:S(2)}) collective-permute-start(bf16[2048,256]{1,0:T(8,128)(2,1)} %collective-permute-done.11), channel_id=1, source_target_pairs={{64,66},{65,67},{66,64},{67,65},{80,82},{81,83},{82,80},{83,81},{9... | collective-permute-start | bytes 3145736 | tf_op jit(solution)/shard_map/ppermute | solution.py:42
  75.2 4.8 %collective-permute-start.22 = (bf16[2048,256]{1,0:T(8,128)(2,1)}, bf16[2048,256]{1,0:T(8,128)(2,1)}, u32[]{:S(2)}, u32[]{:S(2)}) collective-permute-start(bf16[2048,256]{1,0:T(8,128)(2,1)} %collective-permute-done.13), channel_id=1, source_target_pairs={{0,12},{1,13},{2,14},{3,15},{16,28},{17,29},{18,30},{19,31},{32,44... | collective-permute-start | bytes 3145736 | tf_op jit(solution)/shard_map/ppermute | solution.py:42
  82.2 3.5 %pad_maximum_fusion.stack_hbm = bf16[4,2048,256]{2,1,0:T(8,128)(2,1)} fusion(bf16[1,2048,256]{2,1,0:T(8,128)(2,1)} %bitcast.12, bf16[1,2048,256]{2,1,0:T(8,128)(2,1)} %bitcast.11, bf16[1,2048,256]{2,1,0:T(8,128)(2,1)S(1)} %select_bitcast_fusion, bf16[1,2048,256]{2,1,0:T(8,128)(2,1)S(1)} %copy-done.2), kind=kLoop, calls=%fused_computation | loop fusion | flops 6291456 | bytes 8388608 | tf_op jit(solution)/shard_map/stack | solution.py:310
  88.1 2.9 %collective-permute-done.15.refs_1_ = bf16[2048,256]{1,0:T(8,128)(2,1)S(1)} collective-permute-done((bf16[2048,256]{1,0:T(8,128)(2,1)S(1)}, bf16[2048,256]{1,0:T(8,128)(2,1)S(1)}, u32[]{:S(2)}, u32[]{:S(2)}) %collective-permute-start.15) | collective-permute-done | bytes 1048608 | tf_op jit(solution)/shard_map/ppermute | solution.py:42
  92.0 3.0 %collective-permute-start.24 = (bf16[2048,256]{1,0:T(8,128)(2,1)}, bf16[2048,256]{1,0:T(8,128)(2,1)S(1)}, u32[]{:S(2)}, u32[]{:S(2)}) collective-permute-start(bf16[2048,256]{1,0:T(8,128)(2,1)} %collective-permute-done.18.refs_1_), channel_id=1, source_target_pairs={{0,48},{1,49},{64,112},{65,113},{2,50},{3,51},{66,114},{67,115},{1... | collective-permute-start | bytes 3145736 | tf_op jit(solution)/shard_map/ppermute | solution.py:38
  96.4 5.7 %weigh.3.refs_4_ = bf16[2048,1024]{1,0:T(8,128)(2,1)} custom-call(s32[4]{0:T(128)} %copy-done.8, f32[2048,128]{1,0:T(8,128)} %broadcast_in_dim.22.spread_ref.refs_5_, bf16[2048,256]{1,0:T(8,128)(2,1)} %copy-done.1, bf16[2048,256]{1,0:T(8,128)(2,1)} %collective-permute-done.18.refs_1_, bf16[2048,256]{1,0:T(8,128)(2,1)} %copy-done.3), custom_call_target="tpu_custom_call" | custom-call | tf_op jit(solution)/shard_map/weigh/pallas_call | solution.py:63
  104.5 6.1 %weigh.2.own_hbm = bf16[2048,1024]{1,0:T(8,128)(2,1)} custom-call(s32[4]{0:T(128)} %copy-done.8, f32[2048,128]{1,0:T(8,128)} %broadcast_in_dim.11.spread_ref, bf16[2048,256]{1,0:T(8,128)(2,1)} %refs_0_.1, bf16[2048,256]{1,0:T(8,128)(2,1)} %collective-permute-done.17.refs_1_, bf16[2048,256]{1,0:T(8,128)(2,1)} %copy-done.4, ...), custom_call_target="tpu_custom_call" | custom-call | tf_op jit(solution)/shard_map/weigh/pallas_call | solution.py:63
  110.6 2.9 %collective-permute-start.25 = (f32[256]{0:T(256)S(1)}, f32[256]{0:T(256)S(1)}, u32[]{:S(2)}, u32[]{:S(2)}) collective-permute-start(f32[256]{0:T(256)S(1)} %bitcast.50), channel_id=1, source_target_pairs={{0,64},{1,65},{64,0},{65,1},{2,66},{3,67},{66,2},{67,3},{16,80},{1... | collective-permute-start | bytes 3080 | tf_op jit(solution)/shard_map/ppermute | solution.py:38
  113.5 2.3 %broadcast_select_fusion.1.refs_2_ = bf16[2048,256]{1,0:T(8,128)(2,1)} fusion(bf16[2048,256]{1,0:T(8,128)(2,1)} %collective-permute-done.2, bf16[2048,256]{1,0:T(8,128)(2,1)} %collective-permute-done.22, pred[]{:T(512)S(6)} %eq.24), kind=kLoop, calls=%fused_computation.4 | loop fusion | flops 524288 | bytes 3145729 | tf_op jit(solution)/shard_map/jit(_where)/select_n | solution.py:245
  119.0 15.2 %gram_first.1 = (f32[8,256,1024]{2,1,0:T(8,128)}, bf16[2048,1024]{1,0:T(8,128)(2,1)}) custom-call(s32[18]{0:T(128)} %concatenate.8.meta_ref, f32[1]{0:T(128)S(6)} %copy.15.damping_ref, bf16[2048,1024]{1,0:T(8,128)(2,1)} %weigh.2.own_hbm, bf16[4,2048,256]{2,1,0:T(8,128)(2,1)} %pad_maximum_fusion.stack_hbm, bf16[2048,256]{1,0:T(8,128)(2,1)} %collective-permute-done.21.refs_0_, ...), custom_call_target="tpu_custom_call" | custom-call | flops 8589934592 | bytes 20971520 | tf_op jit(solution)/shard_map/gram_first/pallas_call | solution.py:219
  136.0 14.1 %gram.1 = f32[8,256,1024]{2,1,0:T(8,128)} custom-call(s32[18]{0:T(128)} %concatenate.9.meta_ref, f32[1]{0:T(128)S(6)} %copy.15.damping_ref, bf16[2048,1024]{1,0:T(8,128)(2,1)} %weigh.2.own_hbm, bf16[4,2048,256]{2,1,0:T(8,128)(2,1)} %collective-permute-done.26.stack_hbm, bf16[2048,256]{1,0:T(8,128)(2,1)} %copy-done.5, ...), custom_call_target="tpu_custom_call", output_to_operand_aliasing={{}: (9, {})} | custom-call | flops 8589934592 | bytes 20971520 | tf_op jit(solution)/shard_map/gram/pallas_call | solution.py:219
  (91 shorter events, 30.2 us)
Async XLA Ops:
  3.7 5.2 %collective-permute-start = (f32[16,128]{1,0:T(8,128)S(1)}, f32[16,128]{1,0:T(8,128)S(1)}, u32[]{:S(2)}, u32[]{:S(2)}) collective-permute-start(f32[16,128]{1,0:T(8,128)S(1)} %subtract_bitcast_fusion), channel_id=1, source_target_pairs={{0,2},{1,3},{64,66},{65,67},{2,0},{3,1},{66,64},{67,65},{16,18},{1... | collective-permute-start | bytes 24584 | tf_op jit(solution)/shard_map/ppermute | solution.py:38
  9.5 7.4 %collective-permute-start.3 = (f32[16,128]{1,0:T(8,128)S(1)}, f32[16,128]{1,0:T(8,128)S(1)}, u32[]{:S(2)}, u32[]{:S(2)}) collective-permute-start(f32[16,128]{1,0:T(8,128)S(1)} %fusion.9), channel_id=1, source_target_pairs={{0,4},{1,5},{64,68},{65,69},{2,6},{3,7},{66,70},{67,71},{16,20},{1... | collective-permute-start | bytes 24584 | tf_op jit(solution)/shard_map/ppermute | solution.py:38
  10.1 6.8 %collective-permute-start.4 = (f32[16,128]{1,0:T(8,128)S(1)}, f32[16,128]{1,0:T(8,128)S(1)}, u32[]{:S(2)}, u32[]{:S(2)}) collective-permute-start(f32[16,128]{1,0:T(8,128)S(1)} %fusion.9), channel_id=1, source_target_pairs={{0,12},{1,13},{64,76},{65,77},{2,14},{3,15},{66,78},{67,79},{16,28... | collective-permute-start | bytes 24584 | tf_op jit(solution)/shard_map/ppermute | solution.py:38
  12.2 5.2 %collective-permute-start.5 = (f32[16,128]{1,0:T(8,128)S(1)}, f32[16,128]{1,0:T(8,128)S(1)}, u32[]{:S(2)}, u32[]{:S(2)}) collective-permute-start(f32[16,128]{1,0:T(8,128)S(1)} %fusion.9), channel_id=1, source_target_pairs={{0,8},{1,9},{64,72},{65,73},{2,10},{3,11},{66,74},{67,75},{16,24},... | collective-permute-start | bytes 24584 | tf_op jit(solution)/shard_map/ppermute | solution.py:38
  13.6 22.9 %collective-permute-start.1 = (bf16[2048,256]{1,0:T(8,128)(2,1)}, bf16[2048,256]{1,0:T(8,128)(2,1)S(1)}, u32[]{:S(2)}, u32[]{:S(2)}) collective-permute-start(bf16[2048,256]{1,0:T(8,128)(2,1)} %refs_0_.1), channel_id=1, source_target_pairs={{0,64},{1,65},{64,0},{65,1},{2,66},{3,67},{66,2},{67,3},{16,80},{1... | collective-permute-start | bytes 3145736 | tf_op jit(solution)/shard_map/ppermute | solution.py:38
  15.6 23.9 %collective-permute-start.2 = (bf16[2048,256]{1,0:T(8,128)(2,1)}, bf16[2048,256]{1,0:T(8,128)(2,1)}, u32[]{:S(2)}, u32[]{:S(2)}) collective-permute-start(bf16[2048,256]{1,0:T(8,128)(2,1)} %refs_0_.1), channel_id=1, source_target_pairs={{0,66},{1,67},{64,2},{65,3},{2,64},{3,65},{66,0},{67,1},{16,82},{1... | collective-permute-start | bytes 3145736 | tf_op jit(solution)/shard_map/ppermute | solution.py:38
  17.4 22.5 %collective-permute-start.6 = (bf16[2048,256]{1,0:T(8,128)(2,1)}, bf16[2048,256]{1,0:T(8,128)(2,1)S(1)}, u32[]{:S(2)}, u32[]{:S(2)}) collective-permute-start(bf16[2048,256]{1,0:T(8,128)(2,1)} %refs_0_.1), channel_id=1, source_target_pairs={{0,4},{1,5},{64,68},{65,69},{2,6},{3,7},{66,70},{67,71},{16,20},{1... | collective-permute-start | bytes 3145736 | tf_op jit(solution)/shard_map/ppermute | solution.py:38
  18.4 23.6 %collective-permute-start.7 = (bf16[2048,256]{1,0:T(8,128)(2,1)}, bf16[2048,256]{1,0:T(8,128)(2,1)}, u32[]{:S(2)}, u32[]{:S(2)}) collective-permute-start(bf16[2048,256]{1,0:T(8,128)(2,1)} %refs_0_.1), channel_id=1, source_target_pairs={{0,12},{1,13},{64,76},{65,77},{2,14},{3,15},{66,78},{67,79},{16,28... | collective-permute-start | bytes 3145736 | tf_op jit(solution)/shard_map/ppermute | solution.py:38
  20.5 1.2 collective-permute-start.8
  21.7 3.7 %collective-permute-start.9 = (f32[16,128]{1,0:T(8,128)S(1)}, f32[16,128]{1,0:T(8,128)S(1)}, u32[]{:S(2)}, u32[]{:S(2)}) collective-permute-start(f32[16,128]{1,0:T(8,128)S(1)} %add.88), channel_id=1, source_target_pairs={{0,16},{1,17},{64,80},{65,81},{2,18},{3,19},{66,82},{67,83},{16,0}... | collective-permute-start | bytes 24584 | tf_op jit(solution)/shard_map/ppermute | solution.py:38
  25.3 5.2 %collective-permute-start.10 = (f32[16,128]{1,0:T(8,128)S(1)}, f32[16,128]{1,0:T(8,128)S(1)}, u32[]{:S(2)}, u32[]{:S(2)}) collective-permute-start(f32[16,128]{1,0:T(8,128)S(1)} %add.89), channel_id=1, source_target_pairs={{0,32},{1,33},{64,96},{65,97},{2,34},{3,35},{66,98},{67,99},{16,48... | collective-permute-start | bytes 24584 | tf_op jit(solution)/shard_map/ppermute | solution.py:38
  30.5 49.5 %copy-start = (bf16[2048,256]{1,0:T(8,128)(2,1)S(1)}, bf16[2048,256]{1,0:T(8,128)(2,1)}, u32[]{:S(2)}) copy-start(bf16[2048,256]{1,0:T(8,128)(2,1)} %refs_0_.1) | copy-start | bytes 3145732
  30.5 24.0 %collective-permute-start.17 = (bf16[2048,256]{1,0:T(8,128)(2,1)}, bf16[2048,256]{1,0:T(8,128)(2,1)}, u32[]{:S(2)}, u32[]{:S(2)}) collective-permute-start(bf16[2048,256]{1,0:T(8,128)(2,1)} %refs_0_.1), channel_id=1, source_target_pairs={{0,16},{1,17},{64,80},{65,81},{2,18},{3,19},{66,82},{67,83},{16,0}... | collective-permute-start | bytes 3145736 | tf_op jit(solution)/shard_map/ppermute | solution.py:38
  36.5 24.2 %collective-permute-start.16 = (bf16[2048,256]{1,0:T(8,128)(2,1)}, bf16[2048,256]{1,0:T(8,128)(2,1)}, u32[]{:S(2)}, u32[]{:S(2)}) collective-permute-start(bf16[2048,256]{1,0:T(8,128)(2,1)} %refs_0_.1), channel_id=1, source_target_pairs={{0,48},{1,49},{64,112},{65,113},{2,50},{3,51},{66,114},{67,115},{1... | collective-permute-start | bytes 3145736 | tf_op jit(solution)/shard_map/ppermute | solution.py:38
  42.0 21.7 %collective-permute-start.11 = (bf16[2048,256]{1,0:T(8,128)(2,1)}, bf16[2048,256]{1,0:T(8,128)(2,1)}, u32[]{:S(2)}, u32[]{:S(2)}) collective-permute-start(bf16[2048,256]{1,0:T(8,128)(2,1)} %collective-permute-done.7), channel_id=1, source_target_pairs={{0,4},{1,5},{64,68},{65,69},{2,6},{3,7},{66,70},{67,71},{16,20},{1... | collective-permute-start | bytes 3145736 | tf_op jit(solution)/shard_map/ppermute | solution.py:38
  42.0 4.4 %collective-permute-start.12 = (f32[16,128]{1,0:T(8,128)S(1)}, f32[16,128]{1,0:T(8,128)S(1)}, u32[]{:S(2)}, u32[]{:S(2)}) collective-permute-start(f32[16,128]{1,0:T(8,128)S(1)} %add.90), channel_id=1, source_target_pairs={{0,64},{1,65},{64,0},{65,1},{2,66},{3,67},{66,2},{67,3},{16,80},{1... | collective-permute-start | bytes 24584 | tf_op jit(solution)/shard_map/ppermute | solution.py:38
  46.4 23.5 %collective-permute-start.13 = (bf16[2048,256]{1,0:T(8,128)(2,1)}, bf16[2048,256]{1,0:T(8,128)(2,1)}, u32[]{:S(2)}, u32[]{:S(2)}) collective-permute-start(bf16[2048,256]{1,0:T(8,128)(2,1)} %get-tuple-element.61), channel_id=1, source_target_pairs={{0,66},{1,67},{64,2},{65,3},{2,64},{3,65},{66,0},{67,1},{16,82},{1... | collective-permute-start | bytes 3145736 | tf_op jit(solution)/shard_map/ppermute | solution.py:38
  48.9 22.0 %collective-permute-start.14 = (bf16[2048,256]{1,0:T(8,128)(2,1)}, bf16[2048,256]{1,0:T(8,128)(2,1)}, u32[]{:S(2)}, u32[]{:S(2)}) collective-permute-start(bf16[2048,256]{1,0:T(8,128)(2,1)} %get-tuple-element.62), channel_id=1, source_target_pairs={{0,64},{1,65},{64,0},{65,1},{2,66},{3,67},{66,2},{67,3},{16,80},{1... | collective-permute-start | bytes 3145736 | tf_op jit(solution)/shard_map/ppermute | solution.py:38
  54.5 26.2 %collective-permute-start.18 = (bf16[2048,256]{1,0:T(8,128)(2,1)S(1)}, bf16[2048,256]{1,0:T(8,128)(2,1)}, u32[]{:S(2)}, u32[]{:S(2)}) collective-permute-start(bf16[2048,256]{1,0:T(8,128)(2,1)S(1)} %collective-permute-done.1.refs_0_), channel_id=1, source_target_pairs={{0,16},{1,17},{64,80},{65,81},{2,18},{3,19},{66,82},{67,83},{16,0}... | collective-permute-start | bytes 3145736 | tf_op jit(solution)/shard_map/ppermute | solution.py:38
  60.8 24.9 %collective-permute-start.19 = (bf16[2048,256]{1,0:T(8,128)(2,1)S(1)}, bf16[2048,256]{1,0:T(8,128)(2,1)S(1)}, u32[]{:S(2)}, u32[]{:S(2)}) collective-permute-start(bf16[2048,256]{1,0:T(8,128)(2,1)S(1)} %collective-permute-done.1.refs_0_), channel_id=1, source_target_pairs={{0,48},{1,49},{64,112},{65,113},{2,50},{3,51},{66,114},{67,115},{1... | collective-permute-start | bytes 3145736 | tf_op jit(solution)/shard_map/ppermute | solution.py:38
  71.0 20.0 %collective-permute-start.15 = (bf16[2048,256]{1,0:T(8,128)(2,1)S(1)}, bf16[2048,256]{1,0:T(8,128)(2,1)S(1)}, u32[]{:S(2)}, u32[]{:S(2)}) collective-permute-start(bf16[2048,256]{1,0:T(8,128)(2,1)S(1)} %broadcast_select_fusion.2), channel_id=1, source_target_pairs={{0,64},{1,65},{64,2},{65,3},{2,66},{3,67},{66,0},{67,1},{16,80},{1... | collective-permute-start | bytes 3145736 | tf_op jit(solution)/shard_map/ppermute | solution.py:42
  73.5 28.6 %collective-permute-start.23 = (bf16[2048,256]{1,0:T(8,128)(2,1)}, bf16[2048,256]{1,0:T(8,128)(2,1)}, u32[]{:S(2)}, u32[]{:S(2)}) collective-permute-start(bf16[2048,256]{1,0:T(8,128)(2,1)} %collective-permute-done.11), channel_id=1, source_target_pairs={{64,66},{65,67},{66,64},{67,65},{80,82},{81,83},{82,80},{83,81},{9... | collective-permute-start | bytes 3145736 | tf_op jit(solution)/shard_map/ppermute | solution.py:42
  75.2 38.3 %collective-permute-start.22 = (bf16[2048,256]{1,0:T(8,128)(2,1)}, bf16[2048,256]{1,0:T(8,128)(2,1)}, u32[]{:S(2)}, u32[]{:S(2)}) collective-permute-start(bf16[2048,256]{1,0:T(8,128)(2,1)} %collective-permute-done.13), channel_id=1, source_target_pairs={{0,12},{1,13},{2,14},{3,15},{16,28},{17,29},{18,30},{19,31},{32,44... | collective-permute-start | bytes 3145736 | tf_op jit(solution)/shard_map/ppermute | solution.py:42
  80.7 22.5 %collective-permute-start.20 = (bf16[2048,256]{1,0:T(8,128)(2,1)}, bf16[2048,256]{1,0:T(8,128)(2,1)S(1)}, u32[]{:S(2)}, u32[]{:S(2)}) collective-permute-start(bf16[2048,256]{1,0:T(8,128)(2,1)} %collective-permute-done.16.refs_3_), channel_id=1, source_target_pairs={{0,16},{1,17},{64,80},{65,81},{2,18},{3,19},{66,82},{67,83},{16,0}... | collective-permute-start | bytes 3145736 | tf_op jit(solution)/shard_map/ppermute | solution.py:38
  86.7 29.7 %collective-permute-start.21 = (bf16[2048,256]{1,0:T(8,128)(2,1)}, bf16[2048,256]{1,0:T(8,128)(2,1)}, u32[]{:S(2)}, u32[]{:S(2)}) collective-permute-start(bf16[2048,256]{1,0:T(8,128)(2,1)} %collective-permute-done.13), channel_id=1, source_target_pairs={{0,4},{1,5},{64,68},{65,69},{2,6},{3,7},{66,70},{67,71},{16,20},{1... | collective-permute-start | bytes 3145736 | tf_op jit(solution)/shard_map/ppermute | solution.py:38
  92.0 24.4 %collective-permute-start.24 = (bf16[2048,256]{1,0:T(8,128)(2,1)}, bf16[2048,256]{1,0:T(8,128)(2,1)S(1)}, u32[]{:S(2)}, u32[]{:S(2)}) collective-permute-start(bf16[2048,256]{1,0:T(8,128)(2,1)} %collective-permute-done.18.refs_1_), channel_id=1, source_target_pairs={{0,48},{1,49},{64,112},{65,113},{2,50},{3,51},{66,114},{67,115},{1... | collective-permute-start | bytes 3145736 | tf_op jit(solution)/shard_map/ppermute | solution.py:38
  110.6 5.2 %collective-permute-start.25 = (f32[256]{0:T(256)S(1)}, f32[256]{0:T(256)S(1)}, u32[]{:S(2)}, u32[]{:S(2)}) collective-permute-start(f32[256]{0:T(256)S(1)} %bitcast.50), channel_id=1, source_target_pairs={{0,64},{1,65},{64,0},{65,1},{2,66},{3,67},{66,2},{67,3},{16,80},{1... | collective-permute-start | bytes 3080 | tf_op jit(solution)/shard_map/ppermute | solution.py:38
  116.4 17.9 %collective-permute-start.26 = (bf16[4,2048,256]{2,1,0:T(8,128)(2,1)}, bf16[4,2048,256]{2,1,0:T(8,128)(2,1)}, u32[]{:S(2)}, u32[]{:S(2)}) collective-permute-start(bf16[4,2048,256]{2,1,0:T(8,128)(2,1)} %pad_maximum_fusion.stack_hbm), channel_id=1, source_target_pairs={{0,1},{1,0},{64,65},{65,64},{2,3},{3,2},{66,67},{67,66},{16,17},{1... | collective-permute-start | bytes 12582920 | tf_op jit(solution)/shard_map/ppermute | solution.py:38
  117.4 16.9 %collective-permute-start.27 = (bf16[2048,256]{1,0:T(8,128)(2,1)}, bf16[2048,256]{1,0:T(8,128)(2,1)S(1)}, u32[]{:S(2)}, u32[]{:S(2)}) collective-permute-start(bf16[2048,256]{1,0:T(8,128)(2,1)} %collective-permute-done.21.refs_0_), channel_id=1, source_target_pairs={{0,1},{1,0},{64,65},{65,64},{2,3},{3,2},{66,67},{67,66},{16,17},{1... | collective-permute-start | bytes 3145736 | tf_op jit(solution)/shard_map/ppermute | solution.py:38
  117.4 16.9 %collective-permute-start.28 = (bf16[2048,256]{1,0:T(8,128)(2,1)}, bf16[2048,256]{1,0:T(8,128)(2,1)S(1)}, u32[]{:S(2)}, u32[]{:S(2)}) collective-permute-start(bf16[2048,256]{1,0:T(8,128)(2,1)} %copy-done.13), channel_id=1, source_target_pairs={{0,1},{1,0},{64,65},{65,64},{2,3},{3,2},{66,67},{67,66},{16,17},{1... | collective-permute-start | bytes 3145736 | tf_op jit(solution)/shard_map/ppermute | solution.py:38
  117.9 16.4 %collective-permute-start.29 = (bf16[2048,256]{1,0:T(8,128)(2,1)}, bf16[2048,256]{1,0:T(8,128)(2,1)S(1)}, u32[]{:S(2)}, u32[]{:S(2)}) collective-permute-start(bf16[2048,256]{1,0:T(8,128)(2,1)} %broadcast_select_fusion.1.refs_2_), channel_id=1, source_target_pairs={{0,1},{1,0},{64,65},{65,64},{2,3},{3,2},{66,67},{67,66},{16,17},{1... | collective-permute-start | bytes 3145736 | tf_op jit(solution)/shard_map/ppermute | solution.py:38
  117.9 16.4 %collective-permute-start.30 = (bf16[2048,256]{1,0:T(8,128)(2,1)}, bf16[2048,256]{1,0:T(8,128)(2,1)}, u32[]{:S(2)}, u32[]{:S(2)}) collective-permute-start(bf16[2048,256]{1,0:T(8,128)(2,1)} %broadcast_select_fusion.refs_3_), channel_id=1, source_target_pairs={{0,1},{1,0},{64,65},{65,64},{2,3},{3,2},{66,67},{67,66},{16,17},{1... | collective-permute-start | bytes 3145736 | tf_op jit(solution)/shard_map/ppermute | solution.py:38
  (14 other events, 314.6 us)

commit v4 on v3

--- a/solution.py
+++ b/solution.py
@@ -75,22 +75,18 @@
     )(blocks, spread, *shards)
 
 
-N_TILES = 4
-TILE_AT, DIAGONAL_AT, OWN_AT, OTHER_AT, ROW_AT, BLOCK_AT = 0, 4, 8, 12, 16, 17
-FIRST_NEEDS, LATER_NEEDS = (1, 3), ((2, 6), (7, 5), (4,))
+N_TILES = 8
+TILE_AT, DIAGONAL_AT, OWN_AT, OTHER_AT, ROW_AT, BLOCK_AT = 0, 8, 16, 24, 32, 33
+FIRST_NEEDS = (1, 3)
+LATER_NEEDS = ((2, 6), (7, 5), (4,), (8, 9, 11), (10, 14), (15, 13), (12,))
+N_SLOTS = 16
 N_CHUNKS = 4
 AHEAD = 8
 
 
-def gram_kernel(meta_ref, damping_ref, own_hbm, stack_hbm, *refs, samples, fresh):
-    shards_hbm = [stack_hbm.at[n] for n in range(4)] + list(refs[:4])
-    refs = refs[4:]
-    if fresh:
-        before_hbm, spread_hbm, column_hbm = refs[:3]
-        out_ref, other_hbm, weighted, slots, weighted_sems, slot_sems, column, spread, column_sems = refs[3:]
-    else:
-        before_hbm = refs[0]
-        out_ref, weighted, slots, weighted_sems, slot_sems = refs[2:]
+def gram_kernel(meta_ref, damping_ref, own_hbm, other_hbm, *refs, samples):
+    spreads_hbm, columns_hbm, shards_hbm = refs[:2], refs[2:4], refs[4:4 + N_SLOTS]
+    out_ref, weighted, slots, weighted_sems, slot_sems, columns, spreads, column_sems = refs[4 + N_SLOTS:]
     step = pl.program_id(0)
     contract = (((0,), (0,)), ((), ()))
     scale = 1.0 / samples
@@ -107,33 +103,31 @@
         return pl.ds(j * chunk, chunk)
 
     def weighted_copy(n, j):
-        source = (own_hbm, before_hbm)[n]
+        source = (own_hbm, other_hbm)[n]
         return pltpu.make_async_copy(source.at[rows_at(j)], weighted.at[n, rows_at(j)], weighted_sems.at[n, j])
 
     def part(n, at, j):
         return lax.dot_general(
             slots[meta_ref[at], rows_at(j)], weighted[n, rows_at(j)], contract, preferred_element_type=jnp.float32)
 
-    if fresh:
-        column_copies = (
-            pltpu.make_async_copy(column_hbm, column, column_sems.at[0]),
-            pltpu.make_async_copy(spread_hbm, spread, column_sems.at[1]))
-        hand_on = pltpu.make_async_copy(weighted.at[1], other_hbm, column_sems.at[2])
-
-    def scale_column(j):
-        width, lanes = column.shape[1], spread.shape[1]
-        weight = spread[rows_at(j), :]
+    def column_copies(n):
+        return [
+            pltpu.make_async_copy(columns_hbm[n], columns.at[n], column_sems.at[n, 0]),
+            pltpu.make_async_copy(spreads_hbm[n], spreads.at[n], column_sems.at[n, 1])]
+
+    def scale_column(n, j):
+        width, lanes = columns.shape[2], spreads.shape[2]
+        weight = spreads[n, rows_at(j), :]
         for first in range(0, width, lanes):
-            scaled = column[rows_at(j), first:first + lanes].astype(jnp.float32) * weight
+            scaled = columns[n, rows_at(j), first:first + lanes].astype(jnp.float32) * weight
             at = pl.multiple_of(meta_ref[BLOCK_AT] * width + first, lanes)
-            weighted[1, rows_at(j), pl.ds(at, lanes)] = scaled.astype(jnp.bfloat16)
+            weighted[n, rows_at(j), pl.ds(at, lanes)] = scaled.astype(jnp.bfloat16)
 
     @pl.when(step == 0)
     def _():
-        queue = [slot_copy(0)] + [weighted_copy(0, j) for j in range(N_CHUNKS)]
+        queue = [slot_copy(0)] + column_copies(0) + [weighted_copy(0, j) for j in range(N_CHUNKS)]
         queue += [slot_copy(n) for n in FIRST_NEEDS]
-        if fresh:
-            queue += column_copies
+        queue += column_copies(1)
         queue += [weighted_copy(1, j) for j in range(N_CHUNKS)]
         later = [slot_copy(n) for needed in LATER_NEEDS for n in needed]
         todo = queue + later
@@ -149,26 +143,24 @@
                     todo[n + AHEAD].start()
             waited += count
 
-        wait(1)
+        wait(3)
         for j in range(N_CHUNKS):
             wait(1)
+            scale_column(0, j)
             if j == 0:
                 out_ref[0] = part(0, OWN_AT, j)
             else:
                 out_ref[0] += part(0, OWN_AT, j)
-        wait(len(FIRST_NEEDS) + (len(column_copies) if fresh else 0))
+        wait(len(FIRST_NEEDS) + 2)
         for j in range(N_CHUNKS):
             wait(1)
-            if fresh:
-                scale_column(j)
+            scale_column(1, j)
             if j < N_CHUNKS - 1:
                 out_ref[0] += part(1, OTHER_AT, j)
             else:
                 out_ref[0] = (out_ref[0] + part(1, OTHER_AT, j)) * scale
         for copy in todo[waited + AHEAD:]:
             copy.start()
-        if fresh:
-            hand_on.start()
 
     for at, needed in enumerate(LATER_NEEDS):
         @pl.when(step == at + 1)
@@ -188,48 +180,33 @@
                == lax.broadcasted_iota(jnp.int32, (height, height), 1))
         out_ref[0, :, pl.ds(at, height)] += jnp.where(eye, damping_ref[0], 0.0)
 
-    if fresh:
-        @pl.when(step == N_TILES - 1)
-        def _():
-            hand_on.wait()
-
-
-def gram_blocks(meta, damping, own, other, shards, samples, spread=None, column=None, into=None):
-    rows, height = shards[1].shape
+
+def gram_blocks(meta, damping, own, other, spreads, columns, shards, samples):
+    rows, height = shards[0].shape
     width = own.shape[1]
-    fresh = into is None
-    hbm = pl.BlockSpec(memory_space=pl.ANY)
-    arrays = [meta, damping, own, *shards] + ([other, spread, column] if fresh else [other, into])
-    result = jax.ShapeDtypeStruct((2 * N_TILES, height, width), jnp.float32)
-    block = pl.BlockSpec((1, height, width), lambda i, meta: (meta[i], 0, 0))
-    scratch = [
-        pltpu.VMEM((2, rows, width), jnp.bfloat16),
-        pltpu.VMEM((8, rows, height), jnp.bfloat16),
-        pltpu.SemaphoreType.DMA((2, N_CHUNKS)),
-        pltpu.SemaphoreType.DMA((8,)),
-    ]
-    if fresh:
-        scratch += [
-            pltpu.VMEM((rows, height), jnp.bfloat16),
-            pltpu.VMEM(spread.shape, jnp.float32),
-            pltpu.SemaphoreType.DMA((3,)),
-        ]
-    flops = N_TILES * 2 * 2 * rows * height * width
-    moved = 8 * rows * height * 2 + N_TILES * height * width * 4 + 4 * rows * width
+    arrays = [meta, damping, own, other, *spreads, *columns, *shards]
     return pl.pallas_call(
-        functools.partial(gram_kernel, samples=samples, fresh=fresh),
-        out_shape=(result, jax.ShapeDtypeStruct(own.shape, own.dtype)) if fresh else result,
+        functools.partial(gram_kernel, samples=samples),
+        out_shape=jax.ShapeDtypeStruct((N_TILES, height, width), jnp.float32),
         grid_spec=pltpu.PrefetchScalarGridSpec(
             num_scalar_prefetch=1,
             grid=(N_TILES,),
-            in_specs=[pl.BlockSpec(memory_space=pltpu.SMEM)] + [hbm] * (len(arrays) - 2),
-            out_specs=(block, hbm) if fresh else block,
-            scratch_shapes=scratch,
+            in_specs=[pl.BlockSpec(memory_space=pltpu.SMEM)] + [pl.BlockSpec(memory_space=pl.ANY)] * (len(arrays) - 2),
+            out_specs=pl.BlockSpec((1, height, width), lambda i, meta: (meta[i], 0, 0)),
+            scratch_shapes=[
+                pltpu.VMEM((2, rows, width), jnp.bfloat16),
+                pltpu.VMEM((N_SLOTS, rows, height), jnp.bfloat16),
+                pltpu.SemaphoreType.DMA((2, N_CHUNKS)),
+                pltpu.SemaphoreType.DMA((N_SLOTS,)),
+                pltpu.VMEM((2, rows, height), jnp.bfloat16),
+                pltpu.VMEM((2,) + spreads[0].shape, jnp.float32),
+                pltpu.SemaphoreType.DMA((2, 2)),
+            ],
         ),
-        input_output_aliases={} if fresh else {len(arrays) - 1: 0},
         compiler_params=pltpu.CompilerParams(vmem_limit_bytes=60 * 2**20),
-        cost_estimate=pl.CostEstimate(flops=flops, bytes_accessed=moved, transcendentals=0),
-        name="gram_first" if fresh else "gram",
+        cost_estimate=pl.CostEstimate(
+            flops=N_TILES * 4 * rows * height * width, bytes_accessed=N_SLOTS * rows * height * 2, transcendentals=0),
+        name="gram",
     )(*arrays)
 
 
@@ -293,33 +270,27 @@
     spread_own = jnp.broadcast_to(weight[:, None], (rows, 128))
     spread = jnp.broadcast_to(weight_other[:, None], (rows, 128))
     blocks = row ^ jnp.arange(N_Y, dtype=jnp.int32)
-    third_z, other_y1, other_y3 = tie((third_z, other_y1, other_y3))
+    third_xp, third_xo, other_y1, other_y3 = tie((third_xp, third_xo, other_y1, other_y3))
     other_weighted = weigh(blocks, spread, [from_zp, other_y1, other_y3], (0, 1, 3))
-    own_weighted = weigh(blocks, spread_own, [design, own_y1, own_y2, own_y3], (0, 1, 2, 3))
+    own_weighted = weigh(blocks, spread_own, [design, own_y1, own_y3], (0, 1, 3))
     column_a = pick(x, x ^ 3)
     column_b = column_a ^ 1
-    own_slots = pick(jnp.array([0, 2, 7, 4]), jnp.array([0, 6, 1, 7]))
-    other_slots = pick(jnp.array([1, 6, 3, 5]), jnp.array([3, 2, 5, 4]))
-
-    def describe(core_at):
-        places = ((column_a, zh), (column_a, 1 - zh), (column_b, zh), (column_b, 1 - zh))
-        tiles = jnp.stack([column * 4 + at * 2 + core_at - 8 * slab for column, at in places])
-        diagonal = tiles + 8 * slab == col
-        return jnp.concatenate([tiles, diagonal, own_slots, other_slots, row[None], blocks[2:3]]).astype(jnp.int32)
-
-    stack = jnp.stack([pick(design, from_xo), pick(from_zp, second_xp), second_zo, second_zp])
-    third_z, own_weighted, other_weighted, spread, local_grad, stack, meta, meta_sibling = tie(
-        (third_z, own_weighted, other_weighted, spread, local_grad, stack, describe(core), describe(1 - core)))
+    own_slots = pick(jnp.array([0, 2, 7, 4, 8, 10, 15, 12]), jnp.array([0, 6, 1, 7, 8, 14, 9, 15]))
+    other_slots = pick(jnp.array([1, 6, 3, 5, 9, 14, 11, 13]), jnp.array([3, 2, 5, 4, 11, 10, 13, 12]))
+    places = ((column_a, zh), (column_a, 1 - zh), (column_b, zh), (column_b, 1 - zh))
+    tiles = jnp.stack([column * 4 + at * 2 + core_at - 8 * slab for core_at in (core, 1 - core) for column, at in places])
+    diagonal = tiles + 8 * slab == col
+    meta = jnp.concatenate([tiles, diagonal, own_slots, other_slots, row[None], blocks[2:3]]).astype(jnp.int32)
+
+    early = [pick(design, from_xo), pick(from_zp, second_xp), second_zo, second_zp]
+    third_xp, third_z, third_xo, own_weighted, other_weighted, spread_own, spread, local_grad, meta, *early = tie(
+        (third_xp, third_z, third_xo, own_weighted, other_weighted, spread_own, spread, local_grad, meta, *early))
     gradient = -(local_grad + move(local_grad, z=1)) / samples
-    here = [stack, third_xp, third_z, pick(from_zo, third_xo), pick(from_xp, third_z2)]
-    *here, other_y2, gradient = tie((*here, other_y2, gradient))
-
+    here = [*early, third_xp, third_z, pick(from_zo, third_xo), pick(from_xp, third_z2)]
     sibling = [move(shard, core=1) for shard in here]
-    result, other_weighted = gram_blocks(
-        meta, damping, own_weighted, other_weighted, here, samples, spread=spread, column=other_y2)
     result = gram_blocks(
-        meta_sibling, damping, own_weighted, other_weighted, sibling, samples, into=result)
-    hessian = result.reshape(2 * N_TILES, 1, width, N_Y * width)
+        meta, damping, own_weighted, other_weighted, (spread_own, spread), (own_y2, other_y2), here + sibling, samples)
+    hessian = result.reshape(N_TILES, 1, width, N_Y * width)
     return (hessian, gradient)
 
 

time: 152 us -> 151 us (level)
  waiting for transfers between devices: 28.5 us -> 47.7 us
  starting transfers between devices: 51.4 us -> 41.7 us
  other arithmetic: 13.8 us -> 9.24 us
  Pallas kernels: 41.1 us -> 37.2 us
  local copies, waits for them, and re-layouts: 11 us -> 9.24 us
    ppermute x28 -> x31, waiting for transfers between devices: 25.5 us -> 37.8 us  [move(): return lax.ppermute(value, AXES, pairs(lambda cx, cz: (x, y, z, core)))]
    ppermute x28 -> x31, starting transfers between devices: 42.4 us -> 34.8 us  [move(): return lax.ppermute(value, AXES, pairs(lambda cx, cz: (x, y, z, core)))]
    ppermute x3, waiting for transfers between devices: 2.91 us -> 9.94 us  [move_by_role(): lax.ppermute(value, AXES, pairs(lambda cx, cz: native if is_native(cx, cz...]
    another operation x3 -> x0, other arithmetic: 6.91 us -> none  [local(): jnp.stack([pick(design, from_xo), pick(from_zp, second_xp), second_zo, se...]
    pallas_call x2 -> x1, Pallas kernels: 29.3 us -> 25.7 us  [gram_blocks(): pl.pallas_call(functools.partial(gram_kernel, samples=samples), out_shape...]
    select_n x4 -> x6, other arithmetic: 4.74 us -> 7.21 us  [pick(): return jnp.where(native, if_native, if_far)]
    ppermute x3, starting transfers between devices: 9.01 us -> 6.9 us  [move_by_role(): lax.ppermute(value, AXES, pairs(lambda cx, cz: native if is_native(cx, cz...]
    unnamed x31 -> x29, local copies, waits for them, and re-layouts: 5.22 us -> 4.54 us
  transfers between devices with their start and end apart: 31 -> 34, of which waited for: 13 -> 20; matrix products, arithmetic and copies ran while one was open for 12% -> 9% of each run, Pallas kernels for 18% -> 8%
where the time goes in v4:
time: 151 us; the launch traced here: 150 us
  waiting for transfers between devices  47.7 us (32%)
  starting transfers between devices  41.7 us (28%)
  Pallas kernels  37.2 us (25%)
  local copies, waits for them, and re-layouts  9.24 us (6%)
  other arithmetic  9.24 us (6%)
  between operations  2.28 us (2%)
  matrix products  2.16 us (1%)
    ppermute x31, waiting for transfers between devices, move(): return lax.ppermute(value, AXES, pairs(lambda cx, cz: (x, y, z, core)))  37.8 us
    ppermute x31, starting transfers between devices, move(): return lax.ppermute(value, AXES, pairs(lambda cx, cz: (x, y, z, core)))  34.8 us
    pallas_call x1, Pallas kernels, gram_blocks(): pl.pallas_call(functools.partial(gram_kernel, samples=samples), out_shape...  25.7 us
    pallas_call x2, Pallas kernels, weigh(): pl.pallas_call(functools.partial(weigh_kernel, places=places), out_shape=...  11.5 us
    ppermute x3, waiting for transfers between devices, move_by_role(): lax.ppermute(value, AXES, pairs(lambda cx, cz: native if is_native(cx, cz...  9.94 us
    select_n x6, other arithmetic, pick(): return jnp.where(native, if_native, if_far)  7.21 us
    ppermute x3, starting transfers between devices, move_by_role(): lax.ppermute(value, AXES, pairs(lambda cx, cz: native if is_native(cx, cz...  6.9 us
    unnamed x29, local copies, waits for them, and re-layouts  4.54 us
  transfers between devices with their start and end apart: 34, of which 20 were waited for; matrix products, arithmetic and copies ran while one was open for 9% of the time, Pallas kernels for 8%

profile of v4, /device:TPU:0, one launch (start us, length us, event | category | flops | bytes accessed | tf_op | source)
XLA Modules:
  0.0 149.5 jit_solution(14711522360050120762)
XLA Ops:
  1.3 1.6 %fusion.3 = f32[1,2048]{1,0:T(1,128)S(1)} fusion(bf16[2048,256]{1,0:T(8,128)(2,1)} %refs_0_.1, bf16[256,1]{0,1:T(2,128)(2,1)S(1)} %reshape.31), kind=kOutput, calls=%fused_computation.20 | convolution fusion | flops 1048576 | bytes 1057280 | tf_op jit(solution)/shard_map/dot_general | solution.py:225
  3.7 3.3 %collective-permute-start = (f32[16,128]{1,0:T(8,128)S(1)}, f32[16,128]{1,0:T(8,128)S(1)}, u32[]{:S(2)}, u32[]{:S(2)}) collective-permute-start(f32[16,128]{1,0:T(8,128)S(1)} %subtract_bitcast_fusion), channel_id=1, source_target_pairs={{0,2},{1,3},{64,66},{65,67},{2,0},{3,1},{66,64},{67,65},{16,18},{1... | collective-permute-start | bytes 24584 | tf_op jit(solution)/shard_map/ppermute | solution.py:38
  7.0 1.8 %collective-permute-done = f32[16,128]{1,0:T(8,128)S(1)} collective-permute-done((f32[16,128]{1,0:T(8,128)S(1)}, f32[16,128]{1,0:T(8,128)S(1)}, u32[]{:S(2)}, u32[]{:S(2)}) %collective-permute-start) | collective-permute-done | bytes 8224 | tf_op jit(solution)/shard_map/ppermute | solution.py:38
  9.5 2.1 %collective-permute-start.5 = (f32[16,128]{1,0:T(8,128)S(1)}, f32[16,128]{1,0:T(8,128)S(1)}, u32[]{:S(2)}, u32[]{:S(2)}) collective-permute-start(f32[16,128]{1,0:T(8,128)S(1)} %fusion.9), channel_id=1, source_target_pairs={{0,8},{1,9},{64,72},{65,73},{2,10},{3,11},{66,74},{67,75},{16,24},... | collective-permute-start | bytes 24584 | tf_op jit(solution)/shard_map/ppermute | solution.py:38
  13.0 3.5 %collective-permute-start.2 = (bf16[2048,256]{1,0:T(8,128)(2,1)}, bf16[2048,256]{1,0:T(8,128)(2,1)}, u32[]{:S(2)}, u32[]{:S(2)}) collective-permute-start(bf16[2048,256]{1,0:T(8,128)(2,1)} %refs_0_.1), channel_id=1, source_target_pairs={{0,66},{1,67},{64,2},{65,3},{2,64},{3,65},{66,0},{67,1},{16,82},{1... | collective-permute-start | bytes 3145736 | tf_op jit(solution)/shard_map/ppermute | solution.py:38
  16.5 2.2 %collective-permute-start.7 = (bf16[2048,256]{1,0:T(8,128)(2,1)}, bf16[2048,256]{1,0:T(8,128)(2,1)}, u32[]{:S(2)}, u32[]{:S(2)}) collective-permute-start(bf16[2048,256]{1,0:T(8,128)(2,1)} %refs_0_.1), channel_id=1, source_target_pairs={{0,12},{1,13},{64,76},{65,77},{2,14},{3,15},{66,78},{67,79},{16,28... | collective-permute-start | bytes 3145736 | tf_op jit(solution)/shard_map/ppermute | solution.py:38
  18.7 1.4 collective-permute-start.6
  21.3 1.6 %collective-permute-start.9 = (f32[16,128]{1,0:T(8,128)S(1)}, f32[16,128]{1,0:T(8,128)S(1)}, u32[]{:S(2)}, u32[]{:S(2)}) collective-permute-start(f32[16,128]{1,0:T(8,128)S(1)} %add.84), channel_id=1, source_target_pairs={{0,16},{1,17},{64,80},{65,81},{2,18},{3,19},{66,82},{67,83},{16,0}... | collective-permute-start | bytes 24584 | tf_op jit(solution)/shard_map/ppermute | solution.py:38
  22.9 2.1 %collective-permute-done.9 = f32[16,128]{1,0:T(8,128)S(1)} collective-permute-done((f32[16,128]{1,0:T(8,128)S(1)}, f32[16,128]{1,0:T(8,128)S(1)}, u32[]{:S(2)}, u32[]{:S(2)}) %collective-permute-start.9) | collective-permute-done | bytes 8224 | tf_op jit(solution)/shard_map/ppermute | solution.py:38
  25.0 3.2 %collective-permute-start.10 = (f32[16,128]{1,0:T(8,128)S(1)}, f32[16,128]{1,0:T(8,128)S(1)}, u32[]{:S(2)}, u32[]{:S(2)}) collective-permute-start(f32[16,128]{1,0:T(8,128)S(1)} %add.85), channel_id=1, source_target_pairs={{0,32},{1,33},{64,96},{65,97},{2,34},{3,35},{66,98},{67,99},{16,48... | collective-permute-start | bytes 24584 | tf_op jit(solution)/shard_map/ppermute | solution.py:38
  30.1 1.6 %collective-permute-start.18 = (bf16[2048,256]{1,0:T(8,128)(2,1)}, bf16[2048,256]{1,0:T(8,128)(2,1)}, u32[]{:S(2)}, u32[]{:S(2)}) collective-permute-start(bf16[2048,256]{1,0:T(8,128)(2,1)} %refs_0_.1), channel_id=1, source_target_pairs={{0,16},{1,17},{64,80},{65,81},{2,18},{3,19},{66,82},{67,83},{16,0}... | collective-permute-start | bytes 3145736 | tf_op jit(solution)/shard_map/ppermute | solution.py:38
  31.7 6.6 %collective-permute-done.2 = bf16[2048,256]{1,0:T(8,128)(2,1)} collective-permute-done((bf16[2048,256]{1,0:T(8,128)(2,1)}, bf16[2048,256]{1,0:T(8,128)(2,1)}, u32[]{:S(2)}, u32[]{:S(2)}) %collective-permute-start.2) | collective-permute-done | bytes 1048608 | tf_op jit(solution)/shard_map/ppermute | solution.py:38
  38.3 3.0 %collective-permute-start.17 = (bf16[2048,256]{1,0:T(8,128)(2,1)}, bf16[2048,256]{1,0:T(8,128)(2,1)}, u32[]{:S(2)}, u32[]{:S(2)}) collective-permute-start(bf16[2048,256]{1,0:T(8,128)(2,1)} %refs_0_.1), channel_id=1, source_target_pairs={{0,48},{1,49},{64,112},{65,113},{2,50},{3,51},{66,114},{67,115},{1... | collective-permute-start | bytes 3145736 | tf_op jit(solution)/shard_map/ppermute | solution.py:38
  41.5 1.8 %collective-permute-start.12 = (f32[16,128]{1,0:T(8,128)S(1)}, f32[16,128]{1,0:T(8,128)S(1)}, u32[]{:S(2)}, u32[]{:S(2)}) collective-permute-start(f32[16,128]{1,0:T(8,128)S(1)} %add.86), channel_id=1, source_target_pairs={{0,64},{1,65},{64,0},{65,1},{2,66},{3,67},{66,2},{67,3},{16,80},{1... | collective-permute-start | bytes 24584 | tf_op jit(solution)/shard_map/ppermute | solution.py:38
  44.4 3.3 %broadcast_select_fusion.3 = (bf16[2048,256]{1,0:T(8,128)(2,1)}, bf16[2048,256]{1,0:T(8,128)(2,1)}, bf16[2048,256]{1,0:T(8,128)(2,1)}) fusion(bf16[2048,256]{1,0:T(8,128)(2,1)} %refs_0_.1, bf16[2048,256]{1,0:T(8,128)(2,1)} %collective-permute-done.7, pred[]{:T(512)S(6)} %eq.20, bf16[2048,256]{1,0:T(8,128)(2,1)S(1)} %collective-permute-done.6, ...), kind=kLoop, calls=%fused_computation.3 | loop fusion | flops 1572864 | bytes 7340033 | tf_op jit(solution)/shard_map/jit(_where)/select_n | solution.py:222
  47.8 1.5 collective-permute-start.13
  49.2 1.6 %collective-permute-start.14 = (bf16[2048,256]{1,0:T(8,128)(2,1)}, bf16[2048,256]{1,0:T(8,128)(2,1)}, u32[]{:S(2)}, u32[]{:S(2)}) collective-permute-start(bf16[2048,256]{1,0:T(8,128)(2,1)} %get-tuple-element.59), channel_id=1, source_target_pairs={{0,64},{1,65},{64,0},{65,1},{2,66},{3,67},{66,2},{67,3},{16,80},{1... | collective-permute-start | bytes 3145736 | tf_op jit(solution)/shard_map/ppermute | solution.py:38
  54.0 8.4 %collective-permute-done.17.refs_2_ = bf16[2048,256]{1,0:T(8,128)(2,1)} collective-permute-done((bf16[2048,256]{1,0:T(8,128)(2,1)}, bf16[2048,256]{1,0:T(8,128)(2,1)}, u32[]{:S(2)}, u32[]{:S(2)}) %collective-permute-start.17) | collective-permute-done | bytes 1048608 | tf_op jit(solution)/shard_map/ppermute | solution.py:38
  62.4 3.0 %collective-permute-start.20 = (bf16[2048,256]{1,0:T(8,128)(2,1)S(1)}, bf16[2048,256]{1,0:T(8,128)(2,1)}, u32[]{:S(2)}, u32[]{:S(2)}) collective-permute-start(bf16[2048,256]{1,0:T(8,128)(2,1)S(1)} %collective-permute-done.1.refs_0_), channel_id=1, source_target_pairs={{0,48},{1,49},{64,112},{65,113},{2,50},{3,51},{66,114},{67,115},{1... | collective-permute-start | bytes 3145736 | tf_op jit(solution)/shard_map/ppermute | solution.py:38
  65.3 2.3 %broadcast_select_fusion.4 = bf16[2048,256]{1,0:T(8,128)(2,1)} fusion(bf16[2048,256]{1,0:T(8,128)(2,1)} %collective-permute-done.11, bf16[2048,256]{1,0:T(8,128)(2,1)S(1)} %collective-permute-done.6, pred[]{:T(512)S(6)} %eq.20), kind=kLoop, calls=%fused_computation.4 | loop fusion | flops 524288 | bytes 3145729 | tf_op jit(solution)/shard_map/jit(_where)/select_n | solution.py:222
  67.6 2.3 %collective-permute-done.13.refs_6_ = bf16[2048,256]{1,0:T(8,128)(2,1)} collective-permute-done((bf16[2048,256]{1,0:T(8,128)(2,1)}, bf16[2048,256]{1,0:T(8,128)(2,1)}, u32[]{:S(2)}, u32[]{:S(2)}) %collective-permute-start.13) | collective-permute-done | bytes 1048608 | tf_op jit(solution)/shard_map/ppermute | solution.py:38
  70.7 5.2 %collective-permute-start.16 = (bf16[2048,256]{1,0:T(8,128)(2,1)}, bf16[2048,256]{1,0:T(8,128)(2,1)}, u32[]{:S(2)}, u32[]{:S(2)}) collective-permute-start(bf16[2048,256]{1,0:T(8,128)(2,1)} %collective-permute-done.13.refs_6_), channel_id=1, source_target_pairs={{0,12},{1,13},{2,14},{3,15},{16,28},{17,29},{18,30},{19,31},{32,44... | collective-permute-start | bytes 3145736 | tf_op jit(solution)/shard_map/ppermute | solution.py:42
  75.9 1.6 %collective-permute-start.24 = (bf16[2048,256]{1,0:T(8,128)(2,1)}, bf16[2048,256]{1,0:T(8,128)(2,1)}, u32[]{:S(2)}, u32[]{:S(2)}) collective-permute-start(bf16[2048,256]{1,0:T(8,128)(2,1)} %collective-permute-done.11), channel_id=1, source_target_pairs={{64,66},{65,67},{66,64},{67,65},{80,82},{81,83},{82,80},{83,81},{9... | collective-permute-start | bytes 3145736 | tf_op jit(solution)/shard_map/ppermute | solution.py:42
  78.9 5.8 %weigh.2.own_hbm = bf16[2048,1024]{1,0:T(8,128)(2,1)} custom-call(s32[4]{0:T(128)} %copy-done.5, f32[2048,128]{1,0:T(8,128)} %broadcast_in_dim.20.spread_ref.refs_0_, bf16[2048,256]{1,0:T(8,128)(2,1)} %refs_0_.1, bf16[2048,256]{1,0:T(8,128)(2,1)} %collective-permute-done.18.refs_1_, bf16[2048,256]{1,0:T(8,128)(2,1)} %collective-permute-done.17.refs_2_), custom_call_target="tpu_custom_call" | custom-call | tf_op jit(solution)/shard_map/weigh/pallas_call | solution.py:63
  85.3 1.7 %collective-permute-done.19.refs_1_ = bf16[2048,256]{1,0:T(8,128)(2,1)} collective-permute-done((bf16[2048,256]{1,0:T(8,128)(2,1)S(1)}, bf16[2048,256]{1,0:T(8,128)(2,1)}, u32[]{:S(2)}, u32[]{:S(2)}) %collective-permute-start.19) | collective-permute-done | bytes 1048608 | tf_op jit(solution)/shard_map/ppermute | solution.py:38
  88.6 4.4 %collective-permute-done.16 = bf16[2048,256]{1,0:T(8,128)(2,1)} collective-permute-done((bf16[2048,256]{1,0:T(8,128)(2,1)}, bf16[2048,256]{1,0:T(8,128)(2,1)}, u32[]{:S(2)}, u32[]{:S(2)}) %collective-permute-start.16) | collective-permute-done | bytes 1048608 | tf_op jit(solution)/shard_map/ppermute | solution.py:42
  93.0 3.2 %collective-permute-done.15.refs_8_ = bf16[2048,256]{1,0:T(8,128)(2,1)} collective-permute-done((bf16[2048,256]{1,0:T(8,128)(2,1)}, bf16[2048,256]{1,0:T(8,128)(2,1)}, u32[]{:S(2)}, u32[]{:S(2)}) %collective-permute-start.15) | collective-permute-done | bytes 1048608 | tf_op jit(solution)/shard_map/ppermute | solution.py:38
  97.5 5.7 %weigh.3.other_hbm = bf16[2048,1024]{1,0:T(8,128)(2,1)} custom-call(s32[4]{0:T(128)} %copy-done.5, f32[2048,128]{1,0:T(8,128)} %broadcast_in_dim.21.spread_ref.refs_1_, bf16[2048,256]{1,0:T(8,128)(2,1)} %copy-done.1, bf16[2048,256]{1,0:T(8,128)(2,1)} %collective-permute-done.19.refs_1_, bf16[2048,256]{1,0:T(8,128)(2,1)} %collective-permute-done.20.refs_2_), custom_call_target="tpu_custom_call" | custom-call | tf_op jit(solution)/shard_map/weigh/pallas_call | solution.py:63
  103.2 5.5 %collective-permute-done.21.refs_9_ = bf16[2048,256]{1,0:T(8,128)(2,1)} collective-permute-done((bf16[2048,256]{1,0:T(8,128)(2,1)}, bf16[2048,256]{1,0:T(8,128)(2,1)}, u32[]{:S(2)}, u32[]{:S(2)}) %collective-permute-start.21) | collective-permute-done | bytes 1048608 | tf_op jit(solution)/shard_map/ppermute | solution.py:42
  110.2 2.1 %collective-permute-done.33 = f32[256]{0:T(256)S(1)} collective-permute-done((f32[256]{0:T(256)S(1)}, f32[256]{0:T(256)S(1)}, u32[]{:S(2)}, u32[]{:S(2)}) %collective-permute-start.33) | collective-permute-done | bytes 1056 | tf_op jit(solution)/shard_map/ppermute | solution.py:38
  120.7 2.0 %collective-permute-done.28.refs_15_ = bf16[2048,256]{1,0:T(8,128)(2,1)S(1)} collective-permute-done((bf16[2048,256]{1,0:T(8,128)(2,1)}, bf16[2048,256]{1,0:T(8,128)(2,1)S(1)}, u32[]{:S(2)}, u32[]{:S(2)}) %collective-permute-start.28) | collective-permute-done | bytes 1048608 | tf_op jit(solution)/shard_map/ppermute | solution.py:38
  123.6 25.7 %gram.1 = f32[8,256,1024]{2,1,0:T(8,128)} custom-call(s32[34]{0:T(128)} %concatenate.4.meta_ref, f32[1]{0:T(128)S(6)} %copy.13.damping_ref, bf16[2048,1024]{1,0:T(8,128)(2,1)} %weigh.2.own_hbm, bf16[2048,1024]{1,0:T(8,128)(2,1)} %weigh.3.other_hbm, f32[2048,128]{1,0:T(8,128)} %broadcast_in_dim.20.spread_ref.refs_0_, ...), custom_call_target="tpu_custom_call" | custom-call | flops 17179869184 | bytes 16777216 | tf_op jit(solution)/shard_map/gram/pallas_call | solution.py:188
  (93 shorter events, 26.0 us)
Async XLA Ops:
  3.7 5.2 %collective-permute-start = (f32[16,128]{1,0:T(8,128)S(1)}, f32[16,128]{1,0:T(8,128)S(1)}, u32[]{:S(2)}, u32[]{:S(2)}) collective-permute-start(f32[16,128]{1,0:T(8,128)S(1)} %subtract_bitcast_fusion), channel_id=1, source_target_pairs={{0,2},{1,3},{64,66},{65,67},{2,0},{3,1},{66,64},{67,65},{16,18},{1... | collective-permute-start | bytes 24584 | tf_op jit(solution)/shard_map/ppermute | solution.py:38
  9.5 7.0 %collective-permute-start.5 = (f32[16,128]{1,0:T(8,128)S(1)}, f32[16,128]{1,0:T(8,128)S(1)}, u32[]{:S(2)}, u32[]{:S(2)}) collective-permute-start(f32[16,128]{1,0:T(8,128)S(1)} %fusion.9), channel_id=1, source_target_pairs={{0,8},{1,9},{64,72},{65,73},{2,10},{3,11},{66,74},{67,75},{16,24},... | collective-permute-start | bytes 24584 | tf_op jit(solution)/shard_map/ppermute | solution.py:38
  11.7 4.9 %collective-permute-start.4 = (f32[16,128]{1,0:T(8,128)S(1)}, f32[16,128]{1,0:T(8,128)S(1)}, u32[]{:S(2)}, u32[]{:S(2)}) collective-permute-start(f32[16,128]{1,0:T(8,128)S(1)} %fusion.9), channel_id=1, source_target_pairs={{0,12},{1,13},{64,76},{65,77},{2,14},{3,15},{66,78},{67,79},{16,28... | collective-permute-start | bytes 24584 | tf_op jit(solution)/shard_map/ppermute | solution.py:38
  12.8 3.7 %collective-permute-start.3 = (f32[16,128]{1,0:T(8,128)S(1)}, f32[16,128]{1,0:T(8,128)S(1)}, u32[]{:S(2)}, u32[]{:S(2)}) collective-permute-start(f32[16,128]{1,0:T(8,128)S(1)} %fusion.9), channel_id=1, source_target_pairs={{0,4},{1,5},{64,68},{65,69},{2,6},{3,7},{66,70},{67,71},{16,20},{1... | collective-permute-start | bytes 24584 | tf_op jit(solution)/shard_map/ppermute | solution.py:38
  13.0 25.2 %collective-permute-start.2 = (bf16[2048,256]{1,0:T(8,128)(2,1)}, bf16[2048,256]{1,0:T(8,128)(2,1)}, u32[]{:S(2)}, u32[]{:S(2)}) collective-permute-start(bf16[2048,256]{1,0:T(8,128)(2,1)} %refs_0_.1), channel_id=1, source_target_pairs={{0,66},{1,67},{64,2},{65,3},{2,64},{3,65},{66,0},{67,1},{16,82},{1... | collective-permute-start | bytes 3145736 | tf_op jit(solution)/shard_map/ppermute | solution.py:38
  16.5 24.8 %collective-permute-start.1 = (bf16[2048,256]{1,0:T(8,128)(2,1)}, bf16[2048,256]{1,0:T(8,128)(2,1)S(1)}, u32[]{:S(2)}, u32[]{:S(2)}) collective-permute-start(bf16[2048,256]{1,0:T(8,128)(2,1)} %refs_0_.1), channel_id=1, source_target_pairs={{0,64},{1,65},{64,0},{65,1},{2,66},{3,67},{66,2},{67,3},{16,80},{1... | collective-permute-start | bytes 3145736 | tf_op jit(solution)/shard_map/ppermute | solution.py:38
  16.5 24.7 %collective-permute-start.7 = (bf16[2048,256]{1,0:T(8,128)(2,1)}, bf16[2048,256]{1,0:T(8,128)(2,1)}, u32[]{:S(2)}, u32[]{:S(2)}) collective-permute-start(bf16[2048,256]{1,0:T(8,128)(2,1)} %refs_0_.1), channel_id=1, source_target_pairs={{0,12},{1,13},{64,76},{65,77},{2,14},{3,15},{66,78},{67,79},{16,28... | collective-permute-start | bytes 3145736 | tf_op jit(solution)/shard_map/ppermute | solution.py:38
  18.7 22.8 %collective-permute-start.6 = (bf16[2048,256]{1,0:T(8,128)(2,1)}, bf16[2048,256]{1,0:T(8,128)(2,1)S(1)}, u32[]{:S(2)}, u32[]{:S(2)}) collective-permute-start(bf16[2048,256]{1,0:T(8,128)(2,1)} %refs_0_.1), channel_id=1, source_target_pairs={{0,4},{1,5},{64,68},{65,69},{2,6},{3,7},{66,70},{67,71},{16,20},{1... | collective-permute-start | bytes 3145736 | tf_op jit(solution)/shard_map/ppermute | solution.py:38
  21.3 3.7 %collective-permute-start.9 = (f32[16,128]{1,0:T(8,128)S(1)}, f32[16,128]{1,0:T(8,128)S(1)}, u32[]{:S(2)}, u32[]{:S(2)}) collective-permute-start(f32[16,128]{1,0:T(8,128)S(1)} %add.84), channel_id=1, source_target_pairs={{0,16},{1,17},{64,80},{65,81},{2,18},{3,19},{66,82},{67,83},{16,0}... | collective-permute-start | bytes 24584 | tf_op jit(solution)/shard_map/ppermute | solution.py:38
  25.0 5.2 %collective-permute-start.10 = (f32[16,128]{1,0:T(8,128)S(1)}, f32[16,128]{1,0:T(8,128)S(1)}, u32[]{:S(2)}, u32[]{:S(2)}) collective-permute-start(f32[16,128]{1,0:T(8,128)S(1)} %add.85), channel_id=1, source_target_pairs={{0,32},{1,33},{64,96},{65,97},{2,34},{3,35},{66,98},{67,99},{16,48... | collective-permute-start | bytes 24584 | tf_op jit(solution)/shard_map/ppermute | solution.py:38
  30.1 23.9 %collective-permute-start.18 = (bf16[2048,256]{1,0:T(8,128)(2,1)}, bf16[2048,256]{1,0:T(8,128)(2,1)}, u32[]{:S(2)}, u32[]{:S(2)}) collective-permute-start(bf16[2048,256]{1,0:T(8,128)(2,1)} %refs_0_.1), channel_id=1, source_target_pairs={{0,16},{1,17},{64,80},{65,81},{2,18},{3,19},{66,82},{67,83},{16,0}... | collective-permute-start | bytes 3145736 | tf_op jit(solution)/shard_map/ppermute | solution.py:38
  38.3 24.1 %collective-permute-start.17 = (bf16[2048,256]{1,0:T(8,128)(2,1)}, bf16[2048,256]{1,0:T(8,128)(2,1)}, u32[]{:S(2)}, u32[]{:S(2)}) collective-permute-start(bf16[2048,256]{1,0:T(8,128)(2,1)} %refs_0_.1), channel_id=1, source_target_pairs={{0,48},{1,49},{64,112},{65,113},{2,50},{3,51},{66,114},{67,115},{1... | collective-permute-start | bytes 3145736 | tf_op jit(solution)/shard_map/ppermute | solution.py:38
  41.5 6.2 %collective-permute-start.12 = (f32[16,128]{1,0:T(8,128)S(1)}, f32[16,128]{1,0:T(8,128)S(1)}, u32[]{:S(2)}, u32[]{:S(2)}) collective-permute-start(f32[16,128]{1,0:T(8,128)S(1)} %add.86), channel_id=1, source_target_pairs={{0,64},{1,65},{64,0},{65,1},{2,66},{3,67},{66,2},{67,3},{16,80},{1... | collective-permute-start | bytes 24584 | tf_op jit(solution)/shard_map/ppermute | solution.py:38
  43.4 22.0 %collective-permute-start.11 = (bf16[2048,256]{1,0:T(8,128)(2,1)}, bf16[2048,256]{1,0:T(8,128)(2,1)}, u32[]{:S(2)}, u32[]{:S(2)}) collective-permute-start(bf16[2048,256]{1,0:T(8,128)(2,1)} %collective-permute-done.7), channel_id=1, source_target_pairs={{0,4},{1,5},{64,68},{65,69},{2,6},{3,7},{66,70},{67,71},{16,20},{1... | collective-permute-start | bytes 3145736 | tf_op jit(solution)/shard_map/ppermute | solution.py:38
  47.8 22.2 %collective-permute-start.13 = (bf16[2048,256]{1,0:T(8,128)(2,1)}, bf16[2048,256]{1,0:T(8,128)(2,1)}, u32[]{:S(2)}, u32[]{:S(2)}) collective-permute-start(bf16[2048,256]{1,0:T(8,128)(2,1)} %get-tuple-element.58), channel_id=1, source_target_pairs={{0,66},{1,67},{64,2},{65,3},{2,64},{3,65},{66,0},{67,1},{16,82},{1... | collective-permute-start | bytes 3145736 | tf_op jit(solution)/shard_map/ppermute | solution.py:38
  49.2 21.5 %collective-permute-start.14 = (bf16[2048,256]{1,0:T(8,128)(2,1)}, bf16[2048,256]{1,0:T(8,128)(2,1)}, u32[]{:S(2)}, u32[]{:S(2)}) collective-permute-start(bf16[2048,256]{1,0:T(8,128)(2,1)} %get-tuple-element.59), channel_id=1, source_target_pairs={{0,64},{1,65},{64,0},{65,1},{2,66},{3,67},{66,2},{67,3},{16,80},{1... | collective-permute-start | bytes 3145736 | tf_op jit(solution)/shard_map/ppermute | solution.py:38
  62.4 24.7 %collective-permute-start.20 = (bf16[2048,256]{1,0:T(8,128)(2,1)S(1)}, bf16[2048,256]{1,0:T(8,128)(2,1)}, u32[]{:S(2)}, u32[]{:S(2)}) collective-permute-start(bf16[2048,256]{1,0:T(8,128)(2,1)S(1)} %collective-permute-done.1.refs_0_), channel_id=1, source_target_pairs={{0,48},{1,49},{64,112},{65,113},{2,50},{3,51},{66,114},{67,115},{1... | collective-permute-start | bytes 3145736 | tf_op jit(solution)/shard_map/ppermute | solution.py:38
  65.3 21.6 %collective-permute-start.19 = (bf16[2048,256]{1,0:T(8,128)(2,1)S(1)}, bf16[2048,256]{1,0:T(8,128)(2,1)}, u32[]{:S(2)}, u32[]{:S(2)}) collective-permute-start(bf16[2048,256]{1,0:T(8,128)(2,1)S(1)} %collective-permute-done.1.refs_0_), channel_id=1, source_target_pairs={{0,16},{1,17},{64,80},{65,81},{2,18},{3,19},{66,82},{67,83},{16,0}... | collective-permute-start | bytes 3145736 | tf_op jit(solution)/shard_map/ppermute | solution.py:38
  70.7 22.3 %collective-permute-start.16 = (bf16[2048,256]{1,0:T(8,128)(2,1)}, bf16[2048,256]{1,0:T(8,128)(2,1)}, u32[]{:S(2)}, u32[]{:S(2)}) collective-permute-start(bf16[2048,256]{1,0:T(8,128)(2,1)} %collective-permute-done.13.refs_6_), channel_id=1, source_target_pairs={{0,12},{1,13},{2,14},{3,15},{16,28},{17,29},{18,30},{19,31},{32,44... | collective-permute-start | bytes 3145736 | tf_op jit(solution)/shard_map/ppermute | solution.py:42
  75.9 20.3 %collective-permute-start.15 = (bf16[2048,256]{1,0:T(8,128)(2,1)}, bf16[2048,256]{1,0:T(8,128)(2,1)}, u32[]{:S(2)}, u32[]{:S(2)}) collective-permute-start(bf16[2048,256]{1,0:T(8,128)(2,1)} %collective-permute-done.13.refs_6_), channel_id=1, source_target_pairs={{0,4},{1,5},{64,68},{65,69},{2,6},{3,7},{66,70},{67,71},{16,20},{1... | collective-permute-start | bytes 3145736 | tf_op jit(solution)/shard_map/ppermute | solution.py:38
  75.9 12.5 %collective-permute-start.24 = (bf16[2048,256]{1,0:T(8,128)(2,1)}, bf16[2048,256]{1,0:T(8,128)(2,1)}, u32[]{:S(2)}, u32[]{:S(2)}) collective-permute-start(bf16[2048,256]{1,0:T(8,128)(2,1)} %collective-permute-done.11), channel_id=1, source_target_pairs={{64,66},{65,67},{66,64},{67,65},{80,82},{81,83},{82,80},{83,81},{9... | collective-permute-start | bytes 3145736 | tf_op jit(solution)/shard_map/ppermute | solution.py:42
  87.0 21.8 %collective-permute-start.21 = (bf16[2048,256]{1,0:T(8,128)(2,1)}, bf16[2048,256]{1,0:T(8,128)(2,1)}, u32[]{:S(2)}, u32[]{:S(2)}) collective-permute-start(bf16[2048,256]{1,0:T(8,128)(2,1)} %broadcast_select_fusion.4), channel_id=1, source_target_pairs={{0,64},{1,65},{64,2},{65,3},{2,66},{3,67},{66,0},{67,1},{16,80},{1... | collective-permute-start | bytes 3145736 | tf_op jit(solution)/shard_map/ppermute | solution.py:42
  87.1 25.2 %collective-permute-start.23 = (bf16[2048,256]{1,0:T(8,128)(2,1)}, bf16[2048,256]{1,0:T(8,128)(2,1)}, u32[]{:S(2)}, u32[]{:S(2)}) collective-permute-start(bf16[2048,256]{1,0:T(8,128)(2,1)} %collective-permute-done.19.refs_1_), channel_id=1, source_target_pairs={{0,48},{1,49},{64,112},{65,113},{2,50},{3,51},{66,114},{67,115},{1... | collective-permute-start | bytes 3145736 | tf_op jit(solution)/shard_map/ppermute | solution.py:38
  88.5 24.4 %collective-permute-start.22 = (bf16[2048,256]{1,0:T(8,128)(2,1)}, bf16[2048,256]{1,0:T(8,128)(2,1)}, u32[]{:S(2)}, u32[]{:S(2)}) collective-permute-start(bf16[2048,256]{1,0:T(8,128)(2,1)} %collective-permute-done.17.refs_2_), channel_id=1, source_target_pairs={{0,16},{1,17},{64,80},{65,81},{2,18},{3,19},{66,82},{67,83},{16,0}... | collective-permute-start | bytes 3145736 | tf_op jit(solution)/shard_map/ppermute | solution.py:38
  93.0 19.9 %collective-permute-start.32 = (bf16[2048,256]{1,0:T(8,128)(2,1)S(1)}, bf16[2048,256]{1,0:T(8,128)(2,1)}, u32[]{:S(2)}, u32[]{:S(2)}) collective-permute-start(bf16[2048,256]{1,0:T(8,128)(2,1)S(1)} %broadcast_select_fusion.refs_11_), channel_id=1, source_target_pairs={{0,1},{1,0},{64,65},{65,64},{2,3},{3,2},{66,67},{67,66},{16,17},{1... | collective-permute-start | bytes 3145736 | tf_op jit(solution)/shard_map/ppermute | solution.py:38
  108.7 3.6 %collective-permute-start.33 = (f32[256]{0:T(256)S(1)}, f32[256]{0:T(256)S(1)}, u32[]{:S(2)}, u32[]{:S(2)}) collective-permute-start(f32[256]{0:T(256)S(1)} %bitcast.43), channel_id=1, source_target_pairs={{0,64},{1,65},{64,0},{65,1},{2,66},{3,67},{66,2},{67,3},{16,80},{1... | collective-permute-start | bytes 3080 | tf_op jit(solution)/shard_map/ppermute | solution.py:38
  112.3 3.6 %collective-permute-start.25 = (bf16[2048,256]{1,0:T(8,128)(2,1)}, bf16[2048,256]{1,0:T(8,128)(2,1)}, u32[]{:S(2)}, u32[]{:S(2)}) collective-permute-start(bf16[2048,256]{1,0:T(8,128)(2,1)} %get-tuple-element.85.refs_4_), channel_id=1, source_target_pairs={{0,1},{1,0},{64,65},{65,64},{2,3},{3,2},{66,67},{67,66},{16,17},{1... | collective-permute-start | bytes 3145736 | tf_op jit(solution)/shard_map/ppermute | solution.py:38
  112.3 6.0 %collective-permute-start.26 = (bf16[2048,256]{1,0:T(8,128)(2,1)S(1)}, bf16[2048,256]{1,0:T(8,128)(2,1)S(1)}, u32[]{:S(2)}, u32[]{:S(2)}) collective-permute-start(bf16[2048,256]{1,0:T(8,128)(2,1)S(1)} %broadcast_select_fusion.2.refs_5_), channel_id=1, source_target_pairs={{0,1},{1,0},{64,65},{65,64},{2,3},{3,2},{66,67},{67,66},{16,17},{1... | collective-permute-start | bytes 3145736 | tf_op jit(solution)/shard_map/ppermute | solution.py:38
  112.8 6.8 %collective-permute-start.27 = (bf16[2048,256]{1,0:T(8,128)(2,1)}, bf16[2048,256]{1,0:T(8,128)(2,1)S(1)}, u32[]{:S(2)}, u32[]{:S(2)}) collective-permute-start(bf16[2048,256]{1,0:T(8,128)(2,1)} %collective-permute-done.13.refs_6_), channel_id=1, source_target_pairs={{0,1},{1,0},{64,65},{65,64},{2,3},{3,2},{66,67},{67,66},{16,17},{1... | collective-permute-start | bytes 3145736 | tf_op jit(solution)/shard_map/ppermute | solution.py:38
  112.9 9.8 %collective-permute-start.28 = (bf16[2048,256]{1,0:T(8,128)(2,1)}, bf16[2048,256]{1,0:T(8,128)(2,1)S(1)}, u32[]{:S(2)}, u32[]{:S(2)}) collective-permute-start(bf16[2048,256]{1,0:T(8,128)(2,1)} %collective-permute-done.14.refs_7_), channel_id=1, source_target_pairs={{0,1},{1,0},{64,65},{65,64},{2,3},{3,2},{66,67},{67,66},{16,17},{1... | collective-permute-start | bytes 3145736 | tf_op jit(solution)/shard_map/ppermute | solution.py:38
  114.4 8.3 %collective-permute-start.29 = (bf16[2048,256]{1,0:T(8,128)(2,1)}, bf16[2048,256]{1,0:T(8,128)(2,1)}, u32[]{:S(2)}, u32[]{:S(2)}) collective-permute-start(bf16[2048,256]{1,0:T(8,128)(2,1)} %collective-permute-done.15.refs_8_), channel_id=1, source_target_pairs={{0,1},{1,0},{64,65},{65,64},{2,3},{3,2},{66,67},{67,66},{16,17},{1... | collective-permute-start | bytes 3145736 | tf_op jit(solution)/shard_map/ppermute | solution.py:38
  115.9 6.9 %collective-permute-start.30 = (bf16[2048,256]{1,0:T(8,128)(2,1)}, bf16[2048,256]{1,0:T(8,128)(2,1)}, u32[]{:S(2)}, u32[]{:S(2)}) collective-permute-start(bf16[2048,256]{1,0:T(8,128)(2,1)} %collective-permute-done.21.refs_9_), channel_id=1, source_target_pairs={{0,1},{1,0},{64,65},{65,64},{2,3},{3,2},{66,67},{67,66},{16,17},{1... | collective-permute-start | bytes 3145736 | tf_op jit(solution)/shard_map/ppermute | solution.py:38
  (16 other events, 341.7 us)

commit v5 on v4

--- a/solution.py
+++ b/solution.py
@@ -85,8 +85,11 @@
 
 
 def gram_kernel(meta_ref, damping_ref, own_hbm, other_hbm, *refs, samples):
-    spreads_hbm, columns_hbm, shards_hbm = refs[:2], refs[2:4], refs[4:4 + N_SLOTS]
-    out_ref, weighted, slots, weighted_sems, slot_sems, columns, spreads, column_sems = refs[4 + N_SLOTS:]
+    spreads_hbm, columns_hbm = refs[:2], refs[2:4]
+    shards_hbm = []
+    for early, *others in (refs[4:11], refs[11:18]):
+        shards_hbm += [early.at[0], early.at[1], *others]
+    out_ref, weighted, slots, weighted_sems, slot_sems, columns, spreads, column_sems = refs[18:]
     step = pl.program_id(0)
     contract = (((0,), (0,)), ((), ()))
     scale = 1.0 / samples
@@ -182,7 +185,7 @@
 
 
 def gram_blocks(meta, damping, own, other, spreads, columns, shards, samples):
-    rows, height = shards[0].shape
+    rows, height = shards[1].shape
     width = own.shape[1]
     arrays = [meta, damping, own, other, *spreads, *columns, *shards]
     return pl.pallas_call(
@@ -282,12 +285,13 @@
     diagonal = tiles + 8 * slab == col
     meta = jnp.concatenate([tiles, diagonal, own_slots, other_slots, row[None], blocks[2:3]]).astype(jnp.int32)
 
-    early = [pick(design, from_xo), pick(from_zp, second_xp), second_zo, second_zp]
+    early = [jnp.stack([pick(design, from_xo), pick(from_zp, second_xp)]), second_zo, second_zp]
     third_xp, third_z, third_xo, own_weighted, other_weighted, spread_own, spread, local_grad, meta, *early = tie(
         (third_xp, third_z, third_xo, own_weighted, other_weighted, spread_own, spread, local_grad, meta, *early))
-    gradient = -(local_grad + move(local_grad, z=1)) / samples
     here = [*early, third_xp, third_z, pick(from_zo, third_xo), pick(from_xp, third_z2)]
     sibling = [move(shard, core=1) for shard in here]
+    sibling[-1], local_grad = tie((sibling[-1], local_grad))
+    gradient = -(local_grad + move(local_grad, z=1)) / samples
     result = gram_blocks(
         meta, damping, own_weighted, other_weighted, (spread_own, spread), (own_y2, other_y2), here + sibling, samples)
     hessian = result.reshape(N_TILES, 1, width, N_Y * width)

time: 151 us -> 150 us (level)
  local copies, waits for them, and re-layouts: 9.24 us -> 5.48 us
  other arithmetic: 9.24 us -> 11.4 us
    another operation x0 -> x3, other arithmetic: none -> 4.62 us  [local(): jnp.stack([pick(design, from_xo), pick(from_zp, second_xp)])]
    unnamed x29 -> x27, local copies, waits for them, and re-layouts: 4.54 us -> 0.87 us
    ppermute x31 -> x30, waiting for transfers between devices: 37.8 us -> 41 us  [move(): return lax.ppermute(value, AXES, pairs(lambda cx, cz: (x, y, z, core)))]
    ppermute x3, waiting for transfers between devices: 9.94 us -> 6.96 us  [move_by_role(): lax.ppermute(value, AXES, pairs(lambda cx, cz: native if is_native(cx, cz...]
    select_n x6 -> x4, other arithmetic: 7.21 us -> 4.74 us  [pick(): return jnp.where(native, if_native, if_far)]
    ppermute x31 -> x30, starting transfers between devices: 34.8 us -> 35.2 us  [move(): return lax.ppermute(value, AXES, pairs(lambda cx, cz: (x, y, z, core)))]
  transfers between devices with their start and end apart: 34 -> 33, of which waited for: 20 -> 21; matrix products, arithmetic and copies ran while one was open for 9% -> 10% of each run, Pallas kernels for 8% -> 8%
where the time goes in v5:
time: 150 us; the launch traced here: 148 us
  waiting for transfers between devices  47.9 us (32%)
  starting transfers between devices  41.8 us (28%)
  Pallas kernels  37.1 us (25%)
  other arithmetic  11.4 us (8%)
  local copies, waits for them, and re-layouts  5.48 us (4%)
  between operations  2.28 us (2%)
  matrix products  2.11 us (1%)
    ppermute x30, waiting for transfers between devices, move(): return lax.ppermute(value, AXES, pairs(lambda cx, cz: (x, y, z, core)))  41 us
    ppermute x30, starting transfers between devices, move(): return lax.ppermute(value, AXES, pairs(lambda cx, cz: (x, y, z, core)))  35.2 us
    pallas_call x1, Pallas kernels, gram_blocks(): pl.pallas_call(functools.partial(gram_kernel, samples=samples), out_shape...  25.7 us
    pallas_call x2, Pallas kernels, weigh(): pl.pallas_call(functools.partial(weigh_kernel, places=places), out_shape=...  11.4 us
    ppermute x3, waiting for transfers between devices, move_by_role(): lax.ppermute(value, AXES, pairs(lambda cx, cz: native if is_native(cx, cz...  6.96 us
    ppermute x3, starting transfers between devices, move_by_role(): lax.ppermute(value, AXES, pairs(lambda cx, cz: native if is_native(cx, cz...  6.6 us
    select_n x4, other arithmetic, pick(): return jnp.where(native, if_native, if_far)  4.74 us
    another operation x3, other arithmetic, local(): jnp.stack([pick(design, from_xo), pick(from_zp, second_xp)])  4.62 us
  transfers between devices with their start and end apart: 33, of which 21 were waited for; matrix products, arithmetic and copies ran while one was open for 10% of the time, Pallas kernels for 8%

profile of v5, /device:TPU:0, one launch (start us, length us, event | category | flops | bytes accessed | tf_op | source)
XLA Modules:
  0.0 148.1 jit_solution(3468031783478947879)
XLA Ops:
  1.4 1.6 %fusion.3 = f32[1,2048]{1,0:T(1,128)S(1)} fusion(bf16[2048,256]{1,0:T(8,128)(2,1)} %refs_0_.1, bf16[256,1]{0,1:T(2,128)(2,1)S(1)} %reshape.31), kind=kOutput, calls=%fused_computation.21 | convolution fusion | flops 1048576 | bytes 1057280 | tf_op jit(solution)/shard_map/dot_general | solution.py:228
  3.7 3.3 %collective-permute-start = (f32[16,128]{1,0:T(8,128)S(1)}, f32[16,128]{1,0:T(8,128)S(1)}, u32[]{:S(2)}, u32[]{:S(2)}) collective-permute-start(f32[16,128]{1,0:T(8,128)S(1)} %subtract_bitcast_fusion), channel_id=1, source_target_pairs={{0,2},{1,3},{64,66},{65,67},{2,0},{3,1},{66,64},{67,65},{16,18},{1... | collective-permute-start | bytes 24584 | tf_op jit(solution)/shard_map/ppermute | solution.py:38
  7.0 1.8 %collective-permute-done = f32[16,128]{1,0:T(8,128)S(1)} collective-permute-done((f32[16,128]{1,0:T(8,128)S(1)}, f32[16,128]{1,0:T(8,128)S(1)}, u32[]{:S(2)}, u32[]{:S(2)}) %collective-permute-start) | collective-permute-done | bytes 8224 | tf_op jit(solution)/shard_map/ppermute | solution.py:38
  9.6 2.1 %collective-permute-start.5 = (f32[16,128]{1,0:T(8,128)S(1)}, f32[16,128]{1,0:T(8,128)S(1)}, u32[]{:S(2)}, u32[]{:S(2)}) collective-permute-start(f32[16,128]{1,0:T(8,128)S(1)} %fusion.9), channel_id=1, source_target_pairs={{0,8},{1,9},{64,72},{65,73},{2,10},{3,11},{66,74},{67,75},{16,24},... | collective-permute-start | bytes 24584 | tf_op jit(solution)/shard_map/ppermute | solution.py:38
  13.1 3.5 %collective-permute-start.2 = (bf16[2048,256]{1,0:T(8,128)(2,1)}, bf16[2048,256]{1,0:T(8,128)(2,1)}, u32[]{:S(2)}, u32[]{:S(2)}) collective-permute-start(bf16[2048,256]{1,0:T(8,128)(2,1)} %refs_0_.1), channel_id=1, source_target_pairs={{0,66},{1,67},{64,2},{65,3},{2,64},{3,65},{66,0},{67,1},{16,82},{1... | collective-permute-start | bytes 3145736 | tf_op jit(solution)/shard_map/ppermute | solution.py:38
  16.6 2.2 %collective-permute-start.7 = (bf16[2048,256]{1,0:T(8,128)(2,1)}, bf16[2048,256]{1,0:T(8,128)(2,1)}, u32[]{:S(2)}, u32[]{:S(2)}) collective-permute-start(bf16[2048,256]{1,0:T(8,128)(2,1)} %refs_0_.1), channel_id=1, source_target_pairs={{0,12},{1,13},{64,76},{65,77},{2,14},{3,15},{66,78},{67,79},{16,28... | collective-permute-start | bytes 3145736 | tf_op jit(solution)/shard_map/ppermute | solution.py:38
  21.3 1.6 %collective-permute-start.9 = (f32[16,128]{1,0:T(8,128)S(1)}, f32[16,128]{1,0:T(8,128)S(1)}, u32[]{:S(2)}, u32[]{:S(2)}) collective-permute-start(f32[16,128]{1,0:T(8,128)S(1)} %add.84), channel_id=1, source_target_pairs={{0,16},{1,17},{64,80},{65,81},{2,18},{3,19},{66,82},{67,83},{16,0}... | collective-permute-start | bytes 24584 | tf_op jit(solution)/shard_map/ppermute | solution.py:38
  22.9 2.1 %collective-permute-done.9 = f32[16,128]{1,0:T(8,128)S(1)} collective-permute-done((f32[16,128]{1,0:T(8,128)S(1)}, f32[16,128]{1,0:T(8,128)S(1)}, u32[]{:S(2)}, u32[]{:S(2)}) %collective-permute-start.9) | collective-permute-done | bytes 8224 | tf_op jit(solution)/shard_map/ppermute | solution.py:38
  25.0 3.2 %collective-permute-start.10 = (f32[16,128]{1,0:T(8,128)S(1)}, f32[16,128]{1,0:T(8,128)S(1)}, u32[]{:S(2)}, u32[]{:S(2)}) collective-permute-start(f32[16,128]{1,0:T(8,128)S(1)} %add.85), channel_id=1, source_target_pairs={{0,32},{1,33},{64,96},{65,97},{2,34},{3,35},{66,98},{67,99},{16,48... | collective-permute-start | bytes 24584 | tf_op jit(solution)/shard_map/ppermute | solution.py:38
  30.2 1.7 %collective-permute-start.18 = (bf16[2048,256]{1,0:T(8,128)(2,1)}, bf16[2048,256]{1,0:T(8,128)(2,1)}, u32[]{:S(2)}, u32[]{:S(2)}) collective-permute-start(bf16[2048,256]{1,0:T(8,128)(2,1)} %refs_0_.1), channel_id=1, source_target_pairs={{0,16},{1,17},{64,80},{65,81},{2,18},{3,19},{66,82},{67,83},{16,0}... | collective-permute-start | bytes 3145736 | tf_op jit(solution)/shard_map/ppermute | solution.py:38
  31.8 6.5 %collective-permute-done.2 = bf16[2048,256]{1,0:T(8,128)(2,1)} collective-permute-done((bf16[2048,256]{1,0:T(8,128)(2,1)}, bf16[2048,256]{1,0:T(8,128)(2,1)}, u32[]{:S(2)}, u32[]{:S(2)}) %collective-permute-start.2) | collective-permute-done | bytes 1048608 | tf_op jit(solution)/shard_map/ppermute | solution.py:38
  38.3 3.0 %collective-permute-start.17 = (bf16[2048,256]{1,0:T(8,128)(2,1)}, bf16[2048,256]{1,0:T(8,128)(2,1)}, u32[]{:S(2)}, u32[]{:S(2)}) collective-permute-start(bf16[2048,256]{1,0:T(8,128)(2,1)} %refs_0_.1), channel_id=1, source_target_pairs={{0,48},{1,49},{64,112},{65,113},{2,50},{3,51},{66,114},{67,115},{1... | collective-permute-start | bytes 3145736 | tf_op jit(solution)/shard_map/ppermute | solution.py:38
  41.6 1.8 %collective-permute-start.12 = (f32[16,128]{1,0:T(8,128)S(1)}, f32[16,128]{1,0:T(8,128)S(1)}, u32[]{:S(2)}, u32[]{:S(2)}) collective-permute-start(f32[16,128]{1,0:T(8,128)S(1)} %add.86), channel_id=1, source_target_pairs={{0,64},{1,65},{64,0},{65,1},{2,66},{3,67},{66,2},{67,3},{16,80},{1... | collective-permute-start | bytes 24584 | tf_op jit(solution)/shard_map/ppermute | solution.py:38
  44.5 3.0 %select_bitcast_fusion.1 = (bf16[1,2048,256]{2,1,0:T(8,128)(2,1)}, bf16[2048,256]{1,0:T(8,128)(2,1)}, bf16[2048,256]{1,0:T(8,128)(2,1)}) fusion(bf16[2048,256]{1,0:T(8,128)(2,1)S(1)} %copy-done, bf16[2048,256]{1,0:T(8,128)(2,1)} %collective-permute-done.7, pred[]{:T(512)S(6)} %eq.20, bf16[2048,256]{1,0:T(8,128)(2,1)S(1)} %collective-permute-done.6, ...), kind=kLoop, calls=%fused_computation.2 | loop fusion | flops 1572864 | bytes 7340033 | tf_op jit(solution)/shard_map/stack | solution.py:288
  47.5 1.7 %collective-permute-start.13 = (bf16[2048,256]{1,0:T(8,128)(2,1)}, bf16[2048,256]{1,0:T(8,128)(2,1)}, u32[]{:S(2)}, u32[]{:S(2)}) collective-permute-start(bf16[2048,256]{1,0:T(8,128)(2,1)} %get-tuple-element.59), channel_id=1, source_target_pairs={{0,66},{1,67},{64,2},{65,3},{2,64},{3,65},{66,0},{67,1},{16,82},{1... | collective-permute-start | bytes 3145736 | tf_op jit(solution)/shard_map/ppermute | solution.py:38
  52.5 1.6 %collective-permute-done.18.refs_1_ = bf16[2048,256]{1,0:T(8,128)(2,1)} collective-permute-done((bf16[2048,256]{1,0:T(8,128)(2,1)}, bf16[2048,256]{1,0:T(8,128)(2,1)}, u32[]{:S(2)}, u32[]{:S(2)}) %collective-permute-start.18) | collective-permute-done | bytes 1048608 | tf_op jit(solution)/shard_map/ppermute | solution.py:38
  54.1 8.3 %collective-permute-done.17.refs_2_ = bf16[2048,256]{1,0:T(8,128)(2,1)} collective-permute-done((bf16[2048,256]{1,0:T(8,128)(2,1)}, bf16[2048,256]{1,0:T(8,128)(2,1)}, u32[]{:S(2)}, u32[]{:S(2)}) %collective-permute-start.17) | collective-permute-done | bytes 1048608 | tf_op jit(solution)/shard_map/ppermute | solution.py:38
  62.4 3.0 %collective-permute-start.20 = (bf16[2048,256]{1,0:T(8,128)(2,1)S(1)}, bf16[2048,256]{1,0:T(8,128)(2,1)S(1)}, u32[]{:S(2)}, u32[]{:S(2)}) collective-permute-start(bf16[2048,256]{1,0:T(8,128)(2,1)S(1)} %collective-permute-done.1.refs_0_), channel_id=1, source_target_pairs={{0,48},{1,49},{64,112},{65,113},{2,50},{3,51},{66,114},{67,115},{1... | collective-permute-start | bytes 3145736 | tf_op jit(solution)/shard_map/ppermute | solution.py:38
  65.4 2.3 %broadcast_select_fusion.2 = bf16[2048,256]{1,0:T(8,128)(2,1)} fusion(bf16[2048,256]{1,0:T(8,128)(2,1)} %collective-permute-done.11, bf16[2048,256]{1,0:T(8,128)(2,1)S(1)} %collective-permute-done.6, pred[]{:T(512)S(6)} %eq.20), kind=kLoop, calls=%fused_computation.5 | loop fusion | flops 524288 | bytes 3145729 | tf_op jit(solution)/shard_map/jit(_where)/select_n | solution.py:225
  67.7 2.0 %collective-permute-done.13.refs_5_ = bf16[2048,256]{1,0:T(8,128)(2,1)} collective-permute-done((bf16[2048,256]{1,0:T(8,128)(2,1)}, bf16[2048,256]{1,0:T(8,128)(2,1)}, u32[]{:S(2)}, u32[]{:S(2)}) %collective-permute-start.13) | collective-permute-done | bytes 1048608 | tf_op jit(solution)/shard_map/ppermute | solution.py:38
  70.7 5.0 %collective-permute-start.16 = (bf16[2048,256]{1,0:T(8,128)(2,1)}, bf16[2048,256]{1,0:T(8,128)(2,1)}, u32[]{:S(2)}, u32[]{:S(2)}) collective-permute-start(bf16[2048,256]{1,0:T(8,128)(2,1)} %collective-permute-done.13.refs_5_), channel_id=1, source_target_pairs={{0,12},{1,13},{2,14},{3,15},{16,28},{17,29},{18,30},{19,31},{32,44... | collective-permute-start | bytes 3145736 | tf_op jit(solution)/shard_map/ppermute | solution.py:42
  75.6 1.6 %collective-permute-start.24 = (bf16[2048,256]{1,0:T(8,128)(2,1)}, bf16[2048,256]{1,0:T(8,128)(2,1)}, u32[]{:S(2)}, u32[]{:S(2)}) collective-permute-start(bf16[2048,256]{1,0:T(8,128)(2,1)} %collective-permute-done.11), channel_id=1, source_target_pairs={{64,66},{65,67},{66,64},{67,65},{80,82},{81,83},{82,80},{83,81},{9... | collective-permute-start | bytes 3145736 | tf_op jit(solution)/shard_map/ppermute | solution.py:42
  78.6 5.7 %weigh.2.own_hbm = bf16[2048,1024]{1,0:T(8,128)(2,1)} custom-call(s32[4]{0:T(128)} %copy-done.7, f32[2048,128]{1,0:T(8,128)} %broadcast_in_dim.20.spread_ref.refs_0_, bf16[2048,256]{1,0:T(8,128)(2,1)} %refs_0_.1, bf16[2048,256]{1,0:T(8,128)(2,1)} %collective-permute-done.18.refs_1_, bf16[2048,256]{1,0:T(8,128)(2,1)} %collective-permute-done.17.refs_2_), custom_call_target="tpu_custom_call" | custom-call | tf_op jit(solution)/shard_map/weigh/pallas_call | solution.py:63
  84.4 2.4 %collective-permute-done.19.refs_1_ = bf16[2048,256]{1,0:T(8,128)(2,1)} collective-permute-done((bf16[2048,256]{1,0:T(8,128)(2,1)S(1)}, bf16[2048,256]{1,0:T(8,128)(2,1)}, u32[]{:S(2)}, u32[]{:S(2)}) %collective-permute-start.19) | collective-permute-done | bytes 1048608 | tf_op jit(solution)/shard_map/ppermute | solution.py:38
  87.3 1.5 %pad_maximum_fusion.refs_4_ = bf16[2,2048,256]{2,1,0:T(8,128)(2,1)} fusion(bf16[1,2048,256]{2,1,0:T(8,128)(2,1)S(1)} %select_bitcast_fusion, bf16[1,2048,256]{2,1,0:T(8,128)(2,1)S(1)} %copy-done.3), kind=kLoop, calls=%fused_computation | loop fusion | flops 1048576 | bytes 4194304 | tf_op jit(solution)/shard_map/stack | solution.py:288
  88.9 1.5 %collective-permute-start.23 = (bf16[2048,256]{1,0:T(8,128)(2,1)}, bf16[2048,256]{1,0:T(8,128)(2,1)}, u32[]{:S(2)}, u32[]{:S(2)}) collective-permute-start(bf16[2048,256]{1,0:T(8,128)(2,1)} %collective-permute-done.19.refs_1_), channel_id=1, source_target_pairs={{0,48},{1,49},{64,112},{65,113},{2,50},{3,51},{66,114},{67,115},{1... | collective-permute-start | bytes 3145736 | tf_op jit(solution)/shard_map/ppermute | solution.py:38
  92.7 3.2 %collective-permute-done.15.refs_7_ = bf16[2048,256]{1,0:T(8,128)(2,1)} collective-permute-done((bf16[2048,256]{1,0:T(8,128)(2,1)}, bf16[2048,256]{1,0:T(8,128)(2,1)}, u32[]{:S(2)}, u32[]{:S(2)}) %collective-permute-start.15) | collective-permute-done | bytes 1048608 | tf_op jit(solution)/shard_map/ppermute | solution.py:38
  97.2 5.7 %weigh.3.other_hbm = bf16[2048,1024]{1,0:T(8,128)(2,1)} custom-call(s32[4]{0:T(128)} %copy-done.7, f32[2048,128]{1,0:T(8,128)} %broadcast_in_dim.21.spread_ref.refs_1_, bf16[2048,256]{1,0:T(8,128)(2,1)} %copy-done.2, bf16[2048,256]{1,0:T(8,128)(2,1)} %collective-permute-done.19.refs_1_, bf16[2048,256]{1,0:T(8,128)(2,1)} %copy-done.5), custom_call_target="tpu_custom_call" | custom-call | tf_op jit(solution)/shard_map/weigh/pallas_call | solution.py:63
  102.9 5.9 %collective-permute-done.21.refs_8_ = bf16[2048,256]{1,0:T(8,128)(2,1)} collective-permute-done((bf16[2048,256]{1,0:T(8,128)(2,1)}, bf16[2048,256]{1,0:T(8,128)(2,1)}, u32[]{:S(2)}, u32[]{:S(2)}) %collective-permute-start.21) | collective-permute-done | bytes 1048608 | tf_op jit(solution)/shard_map/ppermute | solution.py:42
  111.3 2.0 %collective-permute-done.30.refs_16_ = bf16[2048,256]{1,0:T(8,128)(2,1)S(1)} collective-permute-done((bf16[2048,256]{1,0:T(8,128)(2,1)S(1)}, bf16[2048,256]{1,0:T(8,128)(2,1)S(1)}, u32[]{:S(2)}, u32[]{:S(2)}) %collective-permute-start.30) | collective-permute-done | bytes 1048608 | tf_op jit(solution)/shard_map/ppermute | solution.py:38
  116.7 2.5 %collective-permute-done.27.refs_13_ = bf16[2048,256]{1,0:T(8,128)(2,1)} collective-permute-done((bf16[2048,256]{1,0:T(8,128)(2,1)}, bf16[2048,256]{1,0:T(8,128)(2,1)}, u32[]{:S(2)}, u32[]{:S(2)}) %collective-permute-start.27) | collective-permute-done | bytes 1048608 | tf_op jit(solution)/shard_map/ppermute | solution.py:38
  122.2 25.7 %gram.1 = f32[8,256,1024]{2,1,0:T(8,128)} custom-call(s32[34]{0:T(128)} %concatenate.4.meta_ref, f32[1]{0:T(128)S(6)} %copy.13.damping_ref, bf16[2048,1024]{1,0:T(8,128)(2,1)} %weigh.2.own_hbm, bf16[2048,1024]{1,0:T(8,128)(2,1)} %weigh.3.other_hbm, f32[2048,128]{1,0:T(8,128)} %broadcast_in_dim.20.spread_ref.refs_0_, ...), custom_call_target="tpu_custom_call" | custom-call | flops 17179869184 | bytes 16777216 | tf_op jit(solution)/shard_map/gram/pallas_call | solution.py:191
  (90 shorter events, 27.0 us)
Async XLA Ops:
  3.7 5.2 %collective-permute-start = (f32[16,128]{1,0:T(8,128)S(1)}, f32[16,128]{1,0:T(8,128)S(1)}, u32[]{:S(2)}, u32[]{:S(2)}) collective-permute-start(f32[16,128]{1,0:T(8,128)S(1)} %subtract_bitcast_fusion), channel_id=1, source_target_pairs={{0,2},{1,3},{64,66},{65,67},{2,0},{3,1},{66,64},{67,65},{16,18},{1... | collective-permute-start | bytes 24584 | tf_op jit(solution)/shard_map/ppermute | solution.py:38
  9.6 7.0 %collective-permute-start.5 = (f32[16,128]{1,0:T(8,128)S(1)}, f32[16,128]{1,0:T(8,128)S(1)}, u32[]{:S(2)}, u32[]{:S(2)}) collective-permute-start(f32[16,128]{1,0:T(8,128)S(1)} %fusion.9), channel_id=1, source_target_pairs={{0,8},{1,9},{64,72},{65,73},{2,10},{3,11},{66,74},{67,75},{16,24},... | collective-permute-start | bytes 24584 | tf_op jit(solution)/shard_map/ppermute | solution.py:38
  11.7 4.9 %collective-permute-start.4 = (f32[16,128]{1,0:T(8,128)S(1)}, f32[16,128]{1,0:T(8,128)S(1)}, u32[]{:S(2)}, u32[]{:S(2)}) collective-permute-start(f32[16,128]{1,0:T(8,128)S(1)} %fusion.9), channel_id=1, source_target_pairs={{0,12},{1,13},{64,76},{65,77},{2,14},{3,15},{66,78},{67,79},{16,28... | collective-permute-start | bytes 24584 | tf_op jit(solution)/shard_map/ppermute | solution.py:38
  12.8 3.7 %collective-permute-start.3 = (f32[16,128]{1,0:T(8,128)S(1)}, f32[16,128]{1,0:T(8,128)S(1)}, u32[]{:S(2)}, u32[]{:S(2)}) collective-permute-start(f32[16,128]{1,0:T(8,128)S(1)} %fusion.9), channel_id=1, source_target_pairs={{0,4},{1,5},{64,68},{65,69},{2,6},{3,7},{66,70},{67,71},{16,20},{1... | collective-permute-start | bytes 24584 | tf_op jit(solution)/shard_map/ppermute | solution.py:38
  13.1 25.2 %collective-permute-start.2 = (bf16[2048,256]{1,0:T(8,128)(2,1)}, bf16[2048,256]{1,0:T(8,128)(2,1)}, u32[]{:S(2)}, u32[]{:S(2)}) collective-permute-start(bf16[2048,256]{1,0:T(8,128)(2,1)} %refs_0_.1), channel_id=1, source_target_pairs={{0,66},{1,67},{64,2},{65,3},{2,64},{3,65},{66,0},{67,1},{16,82},{1... | collective-permute-start | bytes 3145736 | tf_op jit(solution)/shard_map/ppermute | solution.py:38
  16.5 24.8 %collective-permute-start.1 = (bf16[2048,256]{1,0:T(8,128)(2,1)}, bf16[2048,256]{1,0:T(8,128)(2,1)S(1)}, u32[]{:S(2)}, u32[]{:S(2)}) collective-permute-start(bf16[2048,256]{1,0:T(8,128)(2,1)} %refs_0_.1), channel_id=1, source_target_pairs={{0,64},{1,65},{64,0},{65,1},{2,66},{3,67},{66,2},{67,3},{16,80},{1... | collective-permute-start | bytes 3145736 | tf_op jit(solution)/shard_map/ppermute | solution.py:38
  16.6 24.7 %collective-permute-start.7 = (bf16[2048,256]{1,0:T(8,128)(2,1)}, bf16[2048,256]{1,0:T(8,128)(2,1)}, u32[]{:S(2)}, u32[]{:S(2)}) collective-permute-start(bf16[2048,256]{1,0:T(8,128)(2,1)} %refs_0_.1), channel_id=1, source_target_pairs={{0,12},{1,13},{64,76},{65,77},{2,14},{3,15},{66,78},{67,79},{16,28... | collective-permute-start | bytes 3145736 | tf_op jit(solution)/shard_map/ppermute | solution.py:38
  18.7 22.8 %collective-permute-start.6 = (bf16[2048,256]{1,0:T(8,128)(2,1)}, bf16[2048,256]{1,0:T(8,128)(2,1)S(1)}, u32[]{:S(2)}, u32[]{:S(2)}) collective-permute-start(bf16[2048,256]{1,0:T(8,128)(2,1)} %refs_0_.1), channel_id=1, source_target_pairs={{0,4},{1,5},{64,68},{65,69},{2,6},{3,7},{66,70},{67,71},{16,20},{1... | collective-permute-start | bytes 3145736 | tf_op jit(solution)/shard_map/ppermute | solution.py:38
  21.3 3.7 %collective-permute-start.9 = (f32[16,128]{1,0:T(8,128)S(1)}, f32[16,128]{1,0:T(8,128)S(1)}, u32[]{:S(2)}, u32[]{:S(2)}) collective-permute-start(f32[16,128]{1,0:T(8,128)S(1)} %add.84), channel_id=1, source_target_pairs={{0,16},{1,17},{64,80},{65,81},{2,18},{3,19},{66,82},{67,83},{16,0}... | collective-permute-start | bytes 24584 | tf_op jit(solution)/shard_map/ppermute | solution.py:38
  25.0 5.2 %collective-permute-start.10 = (f32[16,128]{1,0:T(8,128)S(1)}, f32[16,128]{1,0:T(8,128)S(1)}, u32[]{:S(2)}, u32[]{:S(2)}) collective-permute-start(f32[16,128]{1,0:T(8,128)S(1)} %add.85), channel_id=1, source_target_pairs={{0,32},{1,33},{64,96},{65,97},{2,34},{3,35},{66,98},{67,99},{16,48... | collective-permute-start | bytes 24584 | tf_op jit(solution)/shard_map/ppermute | solution.py:38
  30.2 24.0 %collective-permute-start.18 = (bf16[2048,256]{1,0:T(8,128)(2,1)}, bf16[2048,256]{1,0:T(8,128)(2,1)}, u32[]{:S(2)}, u32[]{:S(2)}) collective-permute-start(bf16[2048,256]{1,0:T(8,128)(2,1)} %refs_0_.1), channel_id=1, source_target_pairs={{0,16},{1,17},{64,80},{65,81},{2,18},{3,19},{66,82},{67,83},{16,0}... | collective-permute-start | bytes 3145736 | tf_op jit(solution)/shard_map/ppermute | solution.py:38
  38.3 24.1 %collective-permute-start.17 = (bf16[2048,256]{1,0:T(8,128)(2,1)}, bf16[2048,256]{1,0:T(8,128)(2,1)}, u32[]{:S(2)}, u32[]{:S(2)}) collective-permute-start(bf16[2048,256]{1,0:T(8,128)(2,1)} %refs_0_.1), channel_id=1, source_target_pairs={{0,48},{1,49},{64,112},{65,113},{2,50},{3,51},{66,114},{67,115},{1... | collective-permute-start | bytes 3145736 | tf_op jit(solution)/shard_map/ppermute | solution.py:38
  41.6 5.9 %collective-permute-start.12 = (f32[16,128]{1,0:T(8,128)S(1)}, f32[16,128]{1,0:T(8,128)S(1)}, u32[]{:S(2)}, u32[]{:S(2)}) collective-permute-start(f32[16,128]{1,0:T(8,128)S(1)} %add.86), channel_id=1, source_target_pairs={{0,64},{1,65},{64,0},{65,1},{2,66},{3,67},{66,2},{67,3},{16,80},{1... | collective-permute-start | bytes 24584 | tf_op jit(solution)/shard_map/ppermute | solution.py:38
  43.4 22.0 %collective-permute-start.11 = (bf16[2048,256]{1,0:T(8,128)(2,1)}, bf16[2048,256]{1,0:T(8,128)(2,1)}, u32[]{:S(2)}, u32[]{:S(2)}) collective-permute-start(bf16[2048,256]{1,0:T(8,128)(2,1)} %collective-permute-done.7), channel_id=1, source_target_pairs={{0,4},{1,5},{64,68},{65,69},{2,6},{3,7},{66,70},{67,71},{16,20},{1... | collective-permute-start | bytes 3145736 | tf_op jit(solution)/shard_map/ppermute | solution.py:38
  47.5 22.2 %collective-permute-start.13 = (bf16[2048,256]{1,0:T(8,128)(2,1)}, bf16[2048,256]{1,0:T(8,128)(2,1)}, u32[]{:S(2)}, u32[]{:S(2)}) collective-permute-start(bf16[2048,256]{1,0:T(8,128)(2,1)} %get-tuple-element.59), channel_id=1, source_target_pairs={{0,66},{1,67},{64,2},{65,3},{2,64},{3,65},{66,0},{67,1},{16,82},{1... | collective-permute-start | bytes 3145736 | tf_op jit(solution)/shard_map/ppermute | solution.py:38
  49.2 21.5 %collective-permute-start.14 = (bf16[2048,256]{1,0:T(8,128)(2,1)}, bf16[2048,256]{1,0:T(8,128)(2,1)}, u32[]{:S(2)}, u32[]{:S(2)}) collective-permute-start(bf16[2048,256]{1,0:T(8,128)(2,1)} %get-tuple-element.60), channel_id=1, source_target_pairs={{0,64},{1,65},{64,0},{65,1},{2,66},{3,67},{66,2},{67,3},{16,80},{1... | collective-permute-start | bytes 3145736 | tf_op jit(solution)/shard_map/ppermute | solution.py:38
  62.4 26.4 %collective-permute-start.20 = (bf16[2048,256]{1,0:T(8,128)(2,1)S(1)}, bf16[2048,256]{1,0:T(8,128)(2,1)S(1)}, u32[]{:S(2)}, u32[]{:S(2)}) collective-permute-start(bf16[2048,256]{1,0:T(8,128)(2,1)S(1)} %collective-permute-done.1.refs_0_), channel_id=1, source_target_pairs={{0,48},{1,49},{64,112},{65,113},{2,50},{3,51},{66,114},{67,115},{1... | collective-permute-start | bytes 3145736 | tf_op jit(solution)/shard_map/ppermute | solution.py:38
  65.4 21.4 %collective-permute-start.19 = (bf16[2048,256]{1,0:T(8,128)(2,1)S(1)}, bf16[2048,256]{1,0:T(8,128)(2,1)}, u32[]{:S(2)}, u32[]{:S(2)}) collective-permute-start(bf16[2048,256]{1,0:T(8,128)(2,1)S(1)} %collective-permute-done.1.refs_0_), channel_id=1, source_target_pairs={{0,16},{1,17},{64,80},{65,81},{2,18},{3,19},{66,82},{67,83},{16,0}... | collective-permute-start | bytes 3145736 | tf_op jit(solution)/shard_map/ppermute | solution.py:38
  70.7 22.0 %collective-permute-start.16 = (bf16[2048,256]{1,0:T(8,128)(2,1)}, bf16[2048,256]{1,0:T(8,128)(2,1)}, u32[]{:S(2)}, u32[]{:S(2)}) collective-permute-start(bf16[2048,256]{1,0:T(8,128)(2,1)} %collective-permute-done.13.refs_5_), channel_id=1, source_target_pairs={{0,12},{1,13},{2,14},{3,15},{16,28},{17,29},{18,30},{19,31},{32,44... | collective-permute-start | bytes 3145736 | tf_op jit(solution)/shard_map/ppermute | solution.py:42
  75.6 20.3 %collective-permute-start.15 = (bf16[2048,256]{1,0:T(8,128)(2,1)}, bf16[2048,256]{1,0:T(8,128)(2,1)}, u32[]{:S(2)}, u32[]{:S(2)}) collective-permute-start(bf16[2048,256]{1,0:T(8,128)(2,1)} %collective-permute-done.13.refs_5_), channel_id=1, source_target_pairs={{0,4},{1,5},{64,68},{65,69},{2,6},{3,7},{66,70},{67,71},{16,20},{1... | collective-permute-start | bytes 3145736 | tf_op jit(solution)/shard_map/ppermute | solution.py:38
  75.6 14.7 %collective-permute-start.24 = (bf16[2048,256]{1,0:T(8,128)(2,1)}, bf16[2048,256]{1,0:T(8,128)(2,1)}, u32[]{:S(2)}, u32[]{:S(2)}) collective-permute-start(bf16[2048,256]{1,0:T(8,128)(2,1)} %collective-permute-done.11), channel_id=1, source_target_pairs={{64,66},{65,67},{66,64},{67,65},{80,82},{81,83},{82,80},{83,81},{9... | collective-permute-start | bytes 3145736 | tf_op jit(solution)/shard_map/ppermute | solution.py:42
  86.8 21.9 %collective-permute-start.21 = (bf16[2048,256]{1,0:T(8,128)(2,1)}, bf16[2048,256]{1,0:T(8,128)(2,1)}, u32[]{:S(2)}, u32[]{:S(2)}) collective-permute-start(bf16[2048,256]{1,0:T(8,128)(2,1)} %broadcast_select_fusion.2), channel_id=1, source_target_pairs={{0,64},{1,65},{64,2},{65,3},{2,66},{3,67},{66,0},{67,1},{16,80},{1... | collective-permute-start | bytes 3145736 | tf_op jit(solution)/shard_map/ppermute | solution.py:42
  88.9 21.9 %collective-permute-start.23 = (bf16[2048,256]{1,0:T(8,128)(2,1)}, bf16[2048,256]{1,0:T(8,128)(2,1)}, u32[]{:S(2)}, u32[]{:S(2)}) collective-permute-start(bf16[2048,256]{1,0:T(8,128)(2,1)} %collective-permute-done.19.refs_1_), channel_id=1, source_target_pairs={{0,48},{1,49},{64,112},{65,113},{2,50},{3,51},{66,114},{67,115},{1... | collective-permute-start | bytes 3145736 | tf_op jit(solution)/shard_map/ppermute | solution.py:38
  90.4 20.5 %collective-permute-start.22 = (bf16[2048,256]{1,0:T(8,128)(2,1)}, bf16[2048,256]{1,0:T(8,128)(2,1)}, u32[]{:S(2)}, u32[]{:S(2)}) collective-permute-start(bf16[2048,256]{1,0:T(8,128)(2,1)} %collective-permute-done.17.refs_2_), channel_id=1, source_target_pairs={{0,16},{1,17},{64,80},{65,81},{2,18},{3,19},{66,82},{67,83},{16,0}... | collective-permute-start | bytes 3145736 | tf_op jit(solution)/shard_map/ppermute | solution.py:38
  92.7 18.0 %collective-permute-start.31 = (bf16[2048,256]{1,0:T(8,128)(2,1)}, bf16[2048,256]{1,0:T(8,128)(2,1)}, u32[]{:S(2)}, u32[]{:S(2)}) collective-permute-start(bf16[2048,256]{1,0:T(8,128)(2,1)} %broadcast_select_fusion.refs_10_), channel_id=1, source_target_pairs={{0,1},{1,0},{64,65},{65,64},{2,3},{3,2},{66,67},{67,66},{16,17},{1... | collective-permute-start | bytes 3145736 | tf_op jit(solution)/shard_map/ppermute | solution.py:38
  110.1 3.2 %collective-permute-start.30 = (bf16[2048,256]{1,0:T(8,128)(2,1)S(1)}, bf16[2048,256]{1,0:T(8,128)(2,1)S(1)}, u32[]{:S(2)}, u32[]{:S(2)}) collective-permute-start(bf16[2048,256]{1,0:T(8,128)(2,1)S(1)} %broadcast_select_fusion.1.refs_9_), channel_id=1, source_target_pairs={{0,1},{1,0},{64,65},{65,64},{2,3},{3,2},{66,67},{67,66},{16,17},{1... | collective-permute-start | bytes 3145736 | tf_op jit(solution)/shard_map/ppermute | solution.py:38
  110.2 12.0 %collective-permute-start.25 = (bf16[2,2048,256]{2,1,0:T(8,128)(2,1)S(1)}, bf16[2,2048,256]{2,1,0:T(8,128)(2,1)}, u32[]{:S(2)}, u32[]{:S(2)}) collective-permute-start(bf16[2,2048,256]{2,1,0:T(8,128)(2,1)S(1)} %copy-done.4), channel_id=1, source_target_pairs={{0,1},{1,0},{64,65},{65,64},{2,3},{3,2},{66,67},{67,66},{16,17},{1... | collective-permute-start | bytes 6291464 | tf_op jit(solution)/shard_map/ppermute | solution.py:38
  110.7 3.6 %collective-permute-start.32 = (f32[256]{0:T(256)S(1)}, f32[256]{0:T(256)S(1)}, u32[]{:S(2)}, u32[]{:S(2)}) collective-permute-start(f32[256]{0:T(256)S(1)} %bitcast.47), channel_id=1, source_target_pairs={{0,64},{1,65},{64,0},{65,1},{2,66},{3,67},{66,2},{67,3},{16,80},{1... | collective-permute-start | bytes 3080 | tf_op jit(solution)/shard_map/ppermute | solution.py:38
  110.8 5.9 %collective-permute-start.26 = (bf16[2048,256]{1,0:T(8,128)(2,1)}, bf16[2048,256]{1,0:T(8,128)(2,1)}, u32[]{:S(2)}, u32[]{:S(2)}) collective-permute-start(bf16[2048,256]{1,0:T(8,128)(2,1)} %collective-permute-done.13.refs_5_), channel_id=1, source_target_pairs={{0,1},{1,0},{64,65},{65,64},{2,3},{3,2},{66,67},{67,66},{16,17},{1... | collective-permute-start | bytes 3145736 | tf_op jit(solution)/shard_map/ppermute | solution.py:38
  110.9 8.3 %collective-permute-start.27 = (bf16[2048,256]{1,0:T(8,128)(2,1)}, bf16[2048,256]{1,0:T(8,128)(2,1)}, u32[]{:S(2)}, u32[]{:S(2)}) collective-permute-start(bf16[2048,256]{1,0:T(8,128)(2,1)} %collective-permute-done.14.refs_6_), channel_id=1, source_target_pairs={{0,1},{1,0},{64,65},{65,64},{2,3},{3,2},{66,67},{67,66},{16,17},{1... | collective-permute-start | bytes 3145736 | tf_op jit(solution)/shard_map/ppermute | solution.py:38
  113.3 7.4 %collective-permute-start.28 = (bf16[2048,256]{1,0:T(8,128)(2,1)}, bf16[2048,256]{1,0:T(8,128)(2,1)}, u32[]{:S(2)}, u32[]{:S(2)}) collective-permute-start(bf16[2048,256]{1,0:T(8,128)(2,1)} %collective-permute-done.15.refs_7_), channel_id=1, source_target_pairs={{0,1},{1,0},{64,65},{65,64},{2,3},{3,2},{66,67},{67,66},{16,17},{1... | collective-permute-start | bytes 3145736 | tf_op jit(solution)/shard_map/ppermute | solution.py:38
  114.4 7.8 %collective-permute-start.29 = (bf16[2048,256]{1,0:T(8,128)(2,1)}, bf16[2048,256]{1,0:T(8,128)(2,1)}, u32[]{:S(2)}, u32[]{:S(2)}) collective-permute-start(bf16[2048,256]{1,0:T(8,128)(2,1)} %collective-permute-done.21.refs_8_), channel_id=1, source_target_pairs={{0,1},{1,0},{64,65},{65,64},{2,3},{3,2},{66,67},{67,66},{16,17},{1... | collective-permute-start | bytes 3145736 | tf_op jit(solution)/shard_map/ppermute | solution.py:38
  (14 other events, 234.8 us)
